TPU v7x, 32 devices: a whole 2x2x4 slice. The times are simulated.
32 devices in a mesh: member: 2 (over core), space: 16 (over z, y, x).
Axes of the slice: x: 2, y: 2, z: 4, core: 2. Of those that a mesh axis runs over, the one named last changes fastest.
Arguments:
- state: float32 [64, 2, 1024, 512], P('member', None, 'space'), may hold values from -6 to 6
- courant: float32 [2, 1024, 512], P(None, 'space'), may hold values from -0.3 to 0.3
- diffusion: float32 [2, 1024, 512], P(None, 'space'), may hold values from 0.02 to 0.1
- obs_cells: int32 [8, 512], replicated, may hold values from 0 to 32767
- obs_owner: int32 [8], replicated, may hold values from 0 to 15
- batch_order: int32 [8], replicated, may hold values from 0 to 7, each once
- obs_values: float32 [8, 64, 512], replicated, may hold values from -8 to 8
- obs_error: float32 [8, 512], replicated, may hold values from 0.5 to 2
Outputs:
- analysis: float32 [64, 2, 1024, 512], P(None, None, 'space', 'member')
All inputs are finite; a program needn't handle non-finite values.
Results may differ from a plain program's by a relative error of at most 0.0003.
Values sent between devices are 32-bit elements; how exact they have to be, the bound alone decides.
No kernel may reach another device: no remote copies, remote signals or barrier semaphores. Data moves between devices by JAX's collectives and lax.ppermute only.
A program may use at most 128 MiB of HBM per device.

v0:
```python
import jax
import jax.numpy as jnp
from jax import lax
from jax.sharding import PartitionSpec as P

HIGH = lax.Precision.HIGHEST


def padded_2(array, sides, width):
    for axis, dim in sides:
        size, length = (lax.axis_size(axis), array.shape[dim])
        up = [(i, (i + 1) % size) for i in range(size - 1)]
        down = [(j, i) for i, j in up]
        last = lax.slice_in_dim(array, length - width, length, axis=dim)
        leading = lax.slice_in_dim(array, 0, width, axis=dim)
        before = lax.ppermute(last, axis, up)
        after = lax.ppermute(leading, axis, down)
        array = jnp.concatenate([before, array, after], axis=dim)
    return array


def spread(value, axis, source):
    kept = jnp.where(lax.axis_index(axis) == source, value, 0).astype(value.dtype)
    return lax.psum(kept, axis)


def advance(padded, flow_x, flow_y, diffuse):
    center = padded[..., 1:-1, 1:-1]
    western = padded[..., :-2, 1:-1]
    eastern = padded[..., 2:, 1:-1]
    southern = padded[..., 1:-1, :-2]
    northern = padded[..., 1:-1, 2:]
    upwind = jnp.maximum(flow_x, 0.0) * (center - western) + jnp.minimum(flow_x, 0.0) * (
        eastern - center
    )
    upwind = (
        upwind
        + jnp.maximum(flow_y, 0.0) * (center - southern)
        + jnp.minimum(flow_y, 0.0) * (northern - center)
    )
    return center - upwind + diffuse * (eastern + western + northern + southern - 4.0 * center)


def batch_transform(prior_ens, observed, obs_var):
    members = prior_ens.shape[0]
    anomaly = prior_ens - jnp.mean(prior_ens, axis=0, keepdims=True)
    inverse_var = 1.0 / obs_var
    scaled_misfit = (observed - prior_ens).T * inverse_var[:, None]
    scaled_anom = anomaly * inverse_var[None, :]
    inner = jnp.dot(scaled_anom, anomaly.T, precision=HIGH) + (members - 1) * jnp.eye(
        members, dtype=jnp.float32
    )
    lower_factor = jnp.linalg.cholesky(inner)
    projected = jnp.dot(anomaly, scaled_misfit, precision=HIGH)
    half_solved = lax.linalg.triangular_solve(lower_factor, projected, left_side=True, lower=True)
    inner_solved = lax.linalg.triangular_solve(
        lower_factor, half_solved, left_side=True, lower=True, transpose_a=True
    )
    solved = scaled_misfit - jnp.dot(scaled_anom.T, inner_solved, precision=HIGH)
    weights = jnp.dot(anomaly, solved, precision=HIGH) / (members - 1)
    return jnp.eye(members, dtype=jnp.float32) + weights - jnp.mean(weights, axis=0, keepdims=True)


def pad_columns(padded):
    return jnp.pad(padded, ((0, 0), (0, 0), (0, 0), (1, 1)))


def body(state, courant, diffusion, obs_cells, obs_owner, batch_order, obs_values, obs_error):
    slab_id = lax.axis_index("space")
    rows = state.shape[2]
    width_all = state.shape[3]
    nobs = obs_cells.shape[1]
    cells_flat = obs_cells.reshape(-1)
    owner_flat = jnp.repeat(obs_owner, nobs)
    in_slab = owner_flat == slab_id
    fields = state
    for turn in range(2):
        padded = padded_2(fields, (("space", 2),), 1)
        fields = advance(pad_columns(padded), courant[0], courant[1], diffusion)
    local_idx = jnp.clip(cells_flat, 0, rows * width_all - 1)
    flat = fields[:, 0].reshape(fields.shape[0], -1)
    picks = jnp.where(in_slab[None, :], jnp.take(flat, local_idx, axis=1), 0.0)
    priors = lax.all_gather(picks, "member", axis=0, tiled=True)
    fields = lax.all_to_all(fields, "member", split_axis=3, concat_axis=0, tiled=True)
    members = fields.shape[0]
    ensemble = fields.reshape(members, -1)
    for position in range(obs_cells.shape[0]):
        batch_id = batch_order[position]
        prior_ens = lax.dynamic_slice_in_dim(priors, batch_id * nobs, nobs, 1)
        prior_ens = spread(prior_ens, "space", obs_owner[batch_id])
        transform = batch_transform(prior_ens, obs_values[batch_id], obs_error[batch_id])
        priors = jnp.dot(transform.T, priors, precision=HIGH)
        ensemble = jnp.dot(transform.T, ensemble, precision=HIGH)
    return ensemble.reshape(fields.shape)


def solution(mesh):
    placed = (
        P("member", None, "space", None),
        P(None, "space", None),
        P(None, "space", None),
        P(),
        P(),
        P(),
        P(),
        P(),
    )
    return jax.shard_map(
        body,
        mesh=mesh,
        in_specs=placed,
        out_specs=P(None, None, "space", "member"),
        check_vma=False,
    )
```

profile of v0, /device:TPU:0, one launch (start us, length us, event | category | flops | bytes accessed | tf_op | source)
XLA Modules:
  0.0 1183.3 jit_solution(2879293241514404704)
XLA Ops:
  30.6 11.1 select_maximum_fusion.2
  41.7 11.8 fusion.21
  82.8 10.5 copy.112
  93.2 16.6 %gather_fusion = f32[4096,32]{1,0:T(8,128)S(1)} fusion(f32[32,32768]{0,1:T(8,128)} %bitcast.285, s32[4096]{0:T(1024)S(1)} %broadcast_clamp_fusion), kind=kCustom, calls=%fused_computation | custom fusion | bytes 1064960 | tf_op jit(solution)/shard_map/jit(_take)/gather | solution.py:82
  139.6 16.3 %copy.138 = f32[32,2,64,512]{2,0,1,3:T(8,128)} copy(f32[32,2,64,512]{3,0,2,1:T(8,128)} %fusion.7) | data formatting | bytes 16777216 | tf_op jit(solution)/shard_map/add | solution.py:41
  155.9 21.2 %reshape.283 = f32[2,1,1048576]{2,1,0:T(1,128)} reshape(f32[512,2,32,64]{3,2,1,0:T(8,128)} %bitcast.281) | data formatting | bytes 16777216
  177.1 18.5 %all_to_all.15 = f32[2,1,1048576]{2,1,0:T(1,128)} all-to-all(f32[2,1,1048576]{2,1,0:T(1,128)} %reshape.283), channel_id=1, replica_groups=mesh['member'=2,'space'=16] {'member'}, dimensions={0} | all-to-all | bytes 16777216 | tf_op jit(solution)/shard_map/all_to_all | solution.py:84
  196.1 31.3 %reduce.4 = f32[2,1048576]{1,0:T(2,128)} reduce(f32[2,1,1048576]{2,1,0:T(1,128)} %all_to_all.15, f32[]{:T(128)} %broadcast.449), dimensions={1}, to_apply=%all_to_all.11.reduce_sub_computation | reduce | bytes 16777220 | tf_op jit(solution)/shard_map/all_to_all | solution.py:84
  227.4 21.2 %reshape.284 = f32[512,2,32,64]{3,2,1,0:T(8,128)} reshape(f32[2,1048576]{1,0:T(2,128)} %reduce.4) | data formatting | bytes 16777216
  248.6 14.2 %copy.139 = f32[32,2,64,2,256]{4,2,1,0,3:T(8,128)} copy(f32[32,2,64,2,256]{2,0,1,4,3:T(8,128)} %bitcast.282) | data formatting | bytes 16777216 | tf_op jit(solution)/shard_map/all_to_all | solution.py:84
  292.8 11.6 fusion.231
  304.4 94.4 %all-reduce.13.cloned.1.call-done = f32[64,512]{1,0:T(8,128)} async-done(((f32[64,512]{1,0:T(8,128)}), f32[64,512]{1,0:T(8,128)}) %all-reduce.13.cloned.1.call-update) | async-done | bytes 131088 | tf_op jit(solution)/shard_map/psum | solution.py:24
  419.4 11.8 fusion.227
  431.2 91.5 %all-reduce.15.cloned.1.call-done = f32[64,512]{1,0:T(8,128)} async-done(((f32[64,512]{1,0:T(8,128)}), f32[64,512]{1,0:T(8,128)}) %all-reduce.15.cloned.1.call-update) | async-done | bytes 131088 | tf_op jit(solution)/shard_map/psum | solution.py:24
  543.1 11.9 %fusion.223 = f32[64,32768]{1,0:T(8,128)} fusion(f32[64,32768]{1,0:T(8,128)} %fusion.227, f32[64,64]{0,1:T(8,128)S(1)} %get-tuple-element.47, f32[64]{0:T(128)S(1)} %broadcast_multiply_fusion.13), kind=kOutput, calls=%fused_computation.299 | convolution fusion | flops 1610629120 | bytes 16793856 | tf_op jit(solution)/shard_map/dot_general | solution.py:93
  555.0 91.4 %all-reduce.17.cloned.1.call-done = f32[64,512]{1,0:T(8,128)} async-done(((f32[64,512]{1,0:T(8,128)}), f32[64,512]{1,0:T(8,128)}) %all-reduce.17.cloned.1.call-update) | async-done | bytes 131088 | tf_op jit(solution)/shard_map/psum | solution.py:24
  666.9 12.1 %fusion.219 = f32[64,32768]{1,0:T(8,128)} fusion(f32[64,32768]{1,0:T(8,128)} %fusion.223, f32[64,64]{0,1:T(8,128)S(1)} %get-tuple-element.49, f32[64]{0:T(128)S(1)} %broadcast_multiply_fusion.12), kind=kOutput, calls=%fused_computation.297 | convolution fusion | flops 1610629120 | bytes 16793856 | tf_op jit(solution)/shard_map/dot_general | solution.py:93
  679.0 91.3 %all-reduce.19.cloned.1.call-done = f32[64,512]{1,0:T(8,128)} async-done(((f32[64,512]{1,0:T(8,128)}), f32[64,512]{1,0:T(8,128)}) %all-reduce.19.cloned.1.call-update) | async-done | bytes 131088 | tf_op jit(solution)/shard_map/psum | solution.py:24
  790.7 11.8 fusion.215
  802.5 91.5 %all-reduce.21.cloned.1.call-done = f32[64,512]{1,0:T(8,128)} async-done(((f32[64,512]{1,0:T(8,128)}), f32[64,512]{1,0:T(8,128)}) %all-reduce.21.cloned.1.call-update) | async-done | bytes 131088 | tf_op jit(solution)/shard_map/psum | solution.py:24
  914.5 11.8 fusion.211
  926.3 91.5 %all-reduce.23.cloned.1.call-done = f32[64,512]{1,0:T(8,128)} async-done(((f32[64,512]{1,0:T(8,128)}), f32[64,512]{1,0:T(8,128)}) %all-reduce.23.cloned.1.call-update) | async-done | bytes 131088 | tf_op jit(solution)/shard_map/psum | solution.py:24
  1038.2 11.9 %fusion.207 = f32[64,32768]{1,0:T(8,128)} fusion(f32[64,32768]{1,0:T(8,128)} %fusion.211, f32[64,64]{0,1:T(8,128)S(1)} %get-tuple-element.55, f32[64]{0:T(128)S(1)} %broadcast_multiply_fusion.9), kind=kOutput, calls=%fused_computation.291 | convolution fusion | flops 1610629120 | bytes 16793856 | tf_op jit(solution)/shard_map/dot_general | solution.py:93
  1050.1 91.5 %all-reduce.25.cloned.1.call-done = f32[64,512]{1,0:T(8,128)} async-done(((f32[64,512]{1,0:T(8,128)}), f32[64,512]{1,0:T(8,128)}) %all-reduce.25.cloned.1.call-update) | async-done | bytes 131088 | tf_op jit(solution)/shard_map/psum | solution.py:24
  (219 shorter events, 245.0 us)
Async XLA Ops:
  6.5 17.9 %copy-start.4 = (f32[2,64,512]{2,1,0:T(8,128)S(1)}, f32[2,64,512]{2,1,0:T(8,128)}, u32[]{:S(2)}) copy-start(f32[2,64,512]{2,1,0:T(8,128)} %param.14) | copy-start | bytes 786436
  6.5 17.9 %copy-start.7 = (s32[8,512]{1,0:T(8,128)S(1)}, s32[8,512]{1,0:T(8,128)}, u32[]{:S(2)}) copy-start(s32[8,512]{1,0:T(8,128)} %param.16) | copy-start | bytes 49156
  6.5 18.0 %copy-start.5 = (s32[8]{0:T(128)S(1)}, s32[8]{0:T(128)}, u32[]{:S(2)}) copy-start(s32[8]{0:T(128)} %param.17) | copy-start | bytes 100
  6.5 122.7 %all-gather.2.cloned.1.call-start = ((), (), s32[]{:S(2)}) async-start(), calls=%async_computation.1 | async-start | bytes 1572864 | tf_op jit(solution)/shard_map/all_gather | solution.py:83
  14.8 3.4 copy-start
  18.2 7.6 collective-permute-start
  23.1 7.5 collective-permute-start.1
  24.7 17.0 %slice-start = ((s8[8388608]{0:T(1024)(128)(4,1)}), s8[4194304]{0:T(1024)(128)(4,1)S(1)}, s32[]{:S(2)}) async-start(s8[8388608]{0:T(1024)(128)(4,1)} %bitcast.279), calls=%async_computation.10 | async-start | bytes 8388608
  24.7 16.9 %slice-start.1 = ((s8[8388608]{0:T(1024)(128)(4,1)}), s8[4194304]{0:T(1024)(128)(4,1)S(1)}, s32[]{:S(2)}) async-start(s8[8388608]{0:T(1024)(128)(4,1)} %bitcast.279), calls=%async_computation.11 | async-start | bytes 8388608
  24.7 16.9 %copy-start.3 = (f32[2,64,512]{2,1,0:T(8,128)S(1)}, f32[2,64,512]{2,1,0:T(8,128)}, u32[]{:S(2)}) copy-start(f32[2,64,512]{2,1,0:T(8,128)} %param.15) | copy-start | bytes 786436
  53.5 6.2 collective-permute-start.2
  57.2 6.9 collective-permute-start.3
  93.2 18.1 %copy-start.6 = (s32[8]{0:T(128)S(1)}, s32[8]{0:T(128)}, u32[]{:S(2)}) copy-start(s32[8]{0:T(128)} %param.18) | copy-start | bytes 100
  93.2 46.3 %copy-start.8 = (f32[8,512]{1,0:T(8,128)S(1)}, f32[8,512]{1,0:T(8,128)}, u32[]{:S(2)}) copy-start(f32[8,512]{1,0:T(8,128)} %param.20) | copy-start | bytes 49156
  111.3 161.1 %all-reduce.11.cloned.1.call-start = ((), (), s32[]{:S(2)}) async-start(), calls=%async_computation.2 | async-start | bytes 262144 | tf_op jit(solution)/shard_map/psum | solution.py:24
  130.8 268.0 %all-reduce.13.cloned.1.call-start = ((), (), s32[]{:S(2)}) async-start(), calls=%async_computation.3 | async-start | bytes 262144 | tf_op jit(solution)/shard_map/psum | solution.py:24
  262.8 23.9 %copy-start.1 = (f32[8,64,512]{2,1,0:T(8,128)S(1)}, f32[8,64,512]{2,1,0:T(8,128)}, u32[]{:S(2)}) copy-start(f32[8,64,512]{2,1,0:T(8,128)} %param.19) | copy-start | bytes 3145732
  262.8 28.2 %copy-start.2 = (f32[64,4096]{1,0:T(8,128)S(1)}, f32[64,4096]{1,0:T(8,128)}, u32[]{:S(2)}) copy-start(f32[64,4096]{1,0:T(8,128)} %all-gather.2.cloned.1.call-done) | copy-start | bytes 3145732
  292.7 229.9 %all-reduce.15.cloned.1.call-start = ((), (), s32[]{:S(2)}) async-start(), calls=%async_computation.4 | async-start | bytes 262144 | tf_op jit(solution)/shard_map/psum | solution.py:24
  419.3 227.1 %all-reduce.17.cloned.1.call-start = ((), (), s32[]{:S(2)}) async-start(), calls=%async_computation.5 | async-start | bytes 262144 | tf_op jit(solution)/shard_map/psum | solution.py:24
  543.0 227.2 %all-reduce.19.cloned.1.call-start = ((), (), s32[]{:S(2)}) async-start(), calls=%async_computation.6 | async-start | bytes 262144 | tf_op jit(solution)/shard_map/psum | solution.py:24
  666.9 227.1 %all-reduce.21.cloned.1.call-start = ((), (), s32[]{:S(2)}) async-start(), calls=%async_computation.7 | async-start | bytes 262144 | tf_op jit(solution)/shard_map/psum | solution.py:24
  790.6 227.2 %all-reduce.23.cloned.1.call-start = ((), (), s32[]{:S(2)}) async-start(), calls=%async_computation.8 | async-start | bytes 262144 | tf_op jit(solution)/shard_map/psum | solution.py:24
  914.5 227.1 %all-reduce.25.cloned.1.call-start = ((), (), s32[]{:S(2)}) async-start(), calls=%async_computation.9 | async-start | bytes 262144 | tf_op jit(solution)/shard_map/psum | solution.py:24
Sparse Core Ops, SparseCore 0:
  111.4 10.7 all-gather.1
  130.9 105.9 all-reduce.10
  292.8 105.9 all-reduce.12
  419.4 103.1 all-reduce.14
  543.2 103.1 all-reduce.16
  667.0 103.2 all-reduce.18
  790.8 103.1 all-reduce.20
  914.6 103.1 all-reduce.22
  1038.3 103.1 all-reduce.24
where the time goes:
time: 1190 us; the launch traced here: 1180 us
  waiting for transfers between devices  654 us (55%)
  other arithmetic  180 us (15%)
  matrix products  144 us (12%)
  local copies, waits for them, and re-layouts  135 us (11%)
  between operations  39.7 us (3%)
  blocking collectives  18.5 us (2%)
    psum x8, waiting for transfers between devices, spread(): return lax.psum(kept, axis)  643 us
    dot_general x8, matrix products, body(): ensemble = jnp.dot(transform.T, ensemble, precision=HIGH)  92.9 us
    unnamed x30, local copies, waits for them, and re-layouts  60.1 us
    another operation x24, other arithmetic, batch_transform(): lower_factor = jnp.linalg.cholesky(inner)  52.5 us
    another operation x16, other arithmetic, batch_transform(): lax.linalg.triangular_solve(lower_factor, half_solved, left_side=True, lo...  44.6 us
    all_to_all x1, other arithmetic, body(): lax.all_to_all(fields, 'member', split_axis=3, concat_axis=0, tiled=True)  31.3 us
  transfers between devices with their start and end apart: 13, of which 11 were waited for; matrix products, arithmetic and copies ran while one was open for 17% of the time, Pallas kernels for 0%

commit v1 on v0

v1 whole, which is shorter than its diff:
```python
import functools

import jax
import jax.numpy as jnp
from jax import lax
from jax.experimental import pallas as pl
from jax.experimental.pallas import tpu as pltpu
from jax.sharding import PartitionSpec as P

HIGH = lax.Precision.HIGHEST
F32 = jnp.float32
BF16 = jnp.bfloat16
LANES = 128
SUB = 8
PACK = 8
VMEM_LIMIT = 56 * 1024 * 1024


def params(**kw):
    return pltpu.CompilerParams(vmem_limit_bytes=VMEM_LIMIT, **kw)


def tiled(array):
    *lead, rows, cols = array.shape
    n = len(lead)
    split = array.reshape(*lead, rows // SUB, SUB, cols // LANES, LANES)
    return jnp.transpose(split, (*range(n), n, n + 2, n + 1, n + 3))


def untiled(array):
    *lead, r8, ct, sub, lanes = array.shape
    n = len(lead)
    back = jnp.transpose(array, (*range(n), n, n + 2, n + 1, n + 3))
    return back.reshape(*lead, r8 * sub, ct * lanes)


def pack_kernel(first, last, flow_first, flow_last, nu_first, nu_last, *outs):
    members = first.shape[0]
    fields = first.shape[1]
    nct = first.shape[3]
    up, down = outs[:fields], outs[fields:]
    for field in range(fields):
        for msg, src, flow, nu, rows, edge in (
            (up[field], last, flow_last, nu_last, (SUB - 2, SUB - 1), SUB - 1),
            (down[field], first, flow_first, nu_first, (0, 1), 0),
        ):
            flat = src.reshape(members * fields * nct * SUB, LANES)
            for ct in range(nct):
                for at, row in enumerate(rows):
                    start = (field * nct + ct) * SUB + row
                    msg[ct, pl.ds(at * members, members), :] = flat[
                        pl.ds(start, members, stride=fields * nct * SUB), :
                    ]
                extra = jnp.concatenate(
                    [
                        flow[0, 0, ct, edge : edge + 1, :],
                        flow[1, 0, ct, edge : edge + 1, :],
                        nu[field, 0, ct, edge : edge + 1, :],
                        jnp.zeros((PACK - 3, LANES), F32),
                    ],
                    axis=0,
                )
                msg[ct, pl.ds(2 * members, PACK), :] = extra


def pack_edges(state6, flow5, nu5):
    members, fields, r8, nct = state6.shape[:4]
    msg = jax.ShapeDtypeStruct((nct, 2 * members + PACK, LANES), F32)
    last = r8 - 1

    def state_block(at):
        return pl.BlockSpec((members, fields, 1, nct, SUB, LANES), lambda i: (0, 0, at, 0, 0, 0))

    def row_block(at):
        return pl.BlockSpec((2, 1, nct, SUB, LANES), lambda i: (0, at, 0, 0, 0))

    return pl.pallas_call(
        pack_kernel,
        grid=(1,),
        out_shape=[msg] * (2 * fields),
        in_specs=[
            state_block(0), state_block(last), row_block(0), row_block(last),
            row_block(0), row_block(last),
        ],
        out_specs=[pl.BlockSpec(msg.shape, lambda i: (0, 0, 0))] * (2 * fields),
        compiler_params=params(),
        name="pack_edges",
    )(state6, state6, flow5, flow5, nu5, nu5)


def stencil_coefs(flow_x, flow_y, nu, col, width):
    east = nu - jnp.minimum(flow_x, 0.0)
    west = nu + jnp.maximum(flow_x, 0.0)
    north = nu - jnp.minimum(flow_y, 0.0)
    south = nu + jnp.maximum(flow_y, 0.0)
    centre = 1.0 - (east + west + north + south)
    south = jnp.where(col == 0, 0.0, south)
    north = jnp.where(col == width - 1, 0.0, north)
    return centre, west, east, south, north


def stencil_row(src, row, dst, coef, members):
    nct = src.shape[1]
    lane = lax.broadcasted_iota(jnp.int32, (SUB, LANES), 1)
    first, last = lane == 0, lane == LANES - 1
    weights = [
        [jnp.broadcast_to(coef[k, ct, pl.ds(row, 1), :], (SUB, LANES)) for k in range(5)]
        for ct in range(nct)
    ]
    for group in range(members // SUB):
        rows = pl.ds(group * SUB, SUB)
        mid = [src[row + 1, ct, rows, :] for ct in range(nct)]
        right = [pltpu.roll(x, 1, 1) for x in mid]
        left = [pltpu.roll(x, LANES - 1, 1) for x in mid]
        for ct in range(nct):
            south = jnp.where(first, right[(ct - 1) % nct], right[ct])
            north = jnp.where(last, left[(ct + 1) % nct], left[ct])
            centre, west, east, w_s, w_n = weights[ct]
            value = (
                centre * mid[ct]
                + west * src[row, ct, rows, :]
                + east * src[row + 2, ct, rows, :]
                + (w_s * south + w_n * north)
            )
            dst(ct, rows, value)


def forecast_kernel(
    gather, ids, cells, owner, order, state, flow, nu, before, after, *rest
):
    if gather:
        own, send, keep, away, q0, q1, coef = rest
    else:
        own, send, q0, q1, coef = rest
    members, _, r8, nct = state.shape[:4]
    rows = r8 * SUB
    half = nct // 2
    width = nct * LANES
    slab, member = ids[0], ids[1]
    flat = state.reshape(members * r8 * nct * SUB, LANES)

    def phys(ct):
        return lax.rem(ct + member * half, nct)

    for ct in range(nct):
        at = phys(ct)
        col = lax.broadcasted_iota(jnp.int32, (rows, LANES), 1) + at * LANES
        flow_x = flow[0, :, at, :, :].reshape(rows, LANES)
        flow_y = flow[1, :, at, :, :].reshape(rows, LANES)
        diffuse = nu[0, :, at, :, :].reshape(rows, LANES)
        for k, value in enumerate(stencil_coefs(flow_x, flow_y, diffuse, col, width)):
            coef[k, ct, pl.ds(SUB, rows), :] = value
        for msg, row in ((before, SUB - 1), (after, SUB + rows)):
            base = 2 * members
            edge = [msg[at, pl.ds(base + k, 1), :] for k in range(3)]
            for k, value in enumerate(stencil_coefs(*edge, col[0:1], width)):
                coef[k, ct, pl.ds(row, 1), :] = value

    for ct in range(nct):
        at = phys(ct)
        for k in range(2):
            q0[k, ct] = before[at, pl.ds(k * members, members), :]
            q0[rows + 2 + k, ct] = after[at, pl.ds(k * members, members), :]

    def load(r, carry):
        for ct in range(nct):
            start = (lax.div(r, SUB) * nct + phys(ct)) * SUB + lax.rem(r, SUB)
            q0[r + 2, ct] = flat[pl.ds(start, members, stride=r8 * nct * SUB), :]
        return carry

    lax.fori_loop(0, rows, load, 0)

    def first_step(r, carry):
        def put(ct, at, value):
            q1[r, ct, at, :] = value

        stencil_row(q0, r, put, coef.at[:, :, pl.ds(SUB - 1, rows + 2)], members)
        return carry

    lax.fori_loop(0, rows + 2, first_step, 0)

    def second_step(r, carry):
        def put(ct, at, value):
            if ct < half:
                own[r, ct, at, :] = value
            else:
                send[r, ct - half, at, :] = value
            if gather:
                q0[r, ct, at, :] = value

        stencil_row(q1, r, put, coef.at[:, :, pl.ds(SUB, rows)], members)
        return carry

    lax.fori_loop(0, rows, second_step, 0)

    if not gather:
        return
    nobs = cells.shape[1]
    lane = lax.broadcasted_iota(jnp.int32, (members, LANES), 1)
    for position in range(order.shape[0]):
        batch = order[position]
        mine = owner[batch] == slab
        kept = lax.rem(position, 2) == member

        def pick(tile, carry, batch=batch, mine=mine, kept=kept, position=position):
            def one(o, acc):
                cell = cells[batch, tile * LANES + o]
                r = lax.div(cell, width)
                c = lax.rem(cell, width)
                at = lax.rem(lax.div(c, LANES) + member * half, nct)
                shift = lax.rem(o - lax.rem(c, LANES) + LANES, LANES)
                moved = pltpu.roll(q0[r, at], shift, 1)
                return jnp.where(lane == o, moved, acc)

            count = jnp.where(mine, LANES, 0)
            acc = lax.fori_loop(0, count // 8, lambda g, a: functools.reduce(
                lambda v, u: one(g * 8 + u, v), range(8), a), jnp.zeros((members, LANES), F32))

            @pl.when(kept)
            def _():
                keep[position // 2, tile] = acc

            @pl.when(jnp.logical_not(kept))
            def _():
                away[position // 2, tile] = acc

            return carry

        lax.fori_loop(0, nobs // LANES, pick, 0)


def forecast(field, gather, ids, cells, owner, order, state6, flow5, nu5, before, after):
    members, fields, r8, nct = state6.shape[:4]
    rows = r8 * SUB
    half = nct // 2
    part = jax.ShapeDtypeStruct((rows, half, members, LANES), F32)
    out_shape = [part, part]
    if gather:
        nb, nobs = cells.shape
        picks = jax.ShapeDtypeStruct((nb // 2, nobs // LANES, members, LANES), F32)
        out_shape += [picks, picks]
    msg = pl.BlockSpec(before.shape, lambda i, *s: (0, 0, 0))
    cells_n = rows * nct * members * LANES
    return pl.pallas_call(
        functools.partial(forecast_kernel, gather),
        out_shape=out_shape,
        grid_spec=pltpu.PrefetchScalarGridSpec(
            num_scalar_prefetch=4,
            grid=(1,),
            in_specs=[
                pl.BlockSpec((members, 1, r8, nct, SUB, LANES), lambda i, *s: (0, field, 0, 0, 0, 0)),
                pl.BlockSpec((2, r8, nct, SUB, LANES), lambda i, *s: (0, 0, 0, 0, 0)),
                pl.BlockSpec((1, r8, nct, SUB, LANES), lambda i, *s: (field, 0, 0, 0, 0)),
                msg,
                msg,
            ],
            out_specs=[
                pl.BlockSpec(o.shape, lambda i, *s: (0, 0, 0, 0)) for o in out_shape
            ],
            scratch_shapes=[
                pltpu.VMEM((rows + 4, nct, members, LANES), F32),
                pltpu.VMEM((rows + 2, nct, members, LANES), F32),
                pltpu.VMEM((5, nct, rows + 2 * SUB, LANES), F32),
            ],
        ),
        compiler_params=params(),
        cost_estimate=pl.CostEstimate(
            flops=40 * cells_n, bytes_accessed=8 * cells_n, transcendentals=0
        ),
        name="forecast_gather" if gather else "forecast",
    )(ids, cells, owner, order, state6, flow5, nu5, before, after)


def gram_kernel(ids, owner, order, keep, other, observed, variance, out):
    slab, member = ids[0], ids[1]
    count, tiles, members = keep.shape[:3]
    for k in range(count):
        batch = order[2 * k + member]
        mine = owner[batch] == slab

        @pl.when(jnp.logical_not(mine))
        def _():
            out[k] = jnp.zeros(out.shape[1:], F32)

        @pl.when(mine)
        def _():
            total = jnp.zeros(out.shape[1:], F32)
            for t in range(tiles):
                a, b = keep[k, t], other[k, t]
                prior = jnp.concatenate(
                    [jnp.where(member == 0, a, b), jnp.where(member == 0, b, a)], axis=0
                )
                mean = jnp.sum(prior, axis=0, keepdims=True) / (2 * members)
                anomaly = prior - mean
                scaled = anomaly / variance[batch, :, pl.ds(t * LANES, LANES)]
                misfit = observed[batch, :, pl.ds(t * LANES, LANES)] - mean
                total += lax.dot_general(
                    scaled,
                    jnp.concatenate([anomaly, misfit], axis=0),
                    (((1,), (1,)), ((), ())),
                    precision=HIGH,
                    preferred_element_type=F32,
                )
            out[k] = total


def gram(ids, owner, order, keep, other, observed, variance):
    count, _, members, _ = keep.shape
    total = 2 * members
    smem = pl.BlockSpec(memory_space=pltpu.SMEM)
    vmem = pl.BlockSpec(memory_space=pltpu.VMEM)
    return pl.pallas_call(
        gram_kernel,
        out_shape=jax.ShapeDtypeStruct((count, total, 2 * total), F32),
        in_specs=[smem] * 3 + [vmem] * 4,
        out_specs=vmem,
        compiler_params=params(),
        name="gram",
    )(ids, owner, order, keep, other, observed, variance[:, None, :])


def solve(inner, rhs):
    size = inner.shape[0]
    groups = size // SUB
    wide = (SUB, LANES)
    sub = lax.broadcasted_iota(jnp.int32, wide, 0)
    a = [inner[g * SUB : (g + 1) * SUB] for g in range(groups)]
    b = [rhs[g * SUB : (g + 1) * SUB] for g in range(groups)]

    def column(x, k):
        return jnp.broadcast_to(x[:, k : k + 1], wide)

    def row(x, k):
        return jnp.broadcast_to(x[k : k + 1, :], wide)

    for p in range(groups):
        cols = [[column(a[g], p * SUB + k) for k in range(SUB)] for g in range(groups)]
        c, pa, pb = cols[p], a[p], b[p]
        for k in range(SUB):
            here = sub == k
            scale = 1.0 / row(c[k], k)
            for j in range(k + 1, SUB):
                t = row(c[j], k) * scale
                c[j] = jnp.where(here, t, c[j] - c[k] * t)
            ra, rb = row(pa, k) * scale, row(pb, k) * scale
            pa = jnp.where(here, ra, pa - c[k] * ra)
            pb = jnp.where(here, rb, pb - c[k] * rb)
        a[p], b[p] = pa, pb
        ra = [row(pa, k) for k in range(SUB)]
        rb = [row(pb, k) for k in range(SUB)]
        for g in range(groups):
            if g == p:
                continue
            for k in range(SUB):
                if p + 1 < groups:
                    a[g] = a[g] - cols[g][k] * ra[k]
                b[g] = b[g] - cols[g][k] * rb[k]
    return jnp.concatenate(b, axis=0)


def chain_kernel(ids, mine, other, out):
    member = ids[1]
    count, size, _ = mine.shape
    eye = (
        lax.broadcasted_iota(jnp.int32, (size, 2 * size), 0)
        == lax.broadcasted_iota(jnp.int32, (size, 2 * size), 1)
    ).astype(F32)
    unit = eye[:, :size]

    def dot(x, y, lhs=1):
        return lax.dot_general(
            x, y, (((lhs,), (0,)), ((), ())), precision=HIGH, preferred_element_type=F32
        )

    def step(position, v):
        k = lax.div(position, 2)
        gh = jnp.where(lax.rem(position, 2) == member, mine[k], other[k])
        g, h = gh[:, :size], gh[:, size:]
        centred = h - jnp.sum(h, axis=1, keepdims=True) / size
        z = v[:, :size]
        gv = dot(g, v)
        both = dot(z, jnp.concatenate([gv, centred, h], axis=1), lhs=0)
        inner = both[:, : 2 * size] + (size - 1) * eye
        rhs = both[:, 2 * size :] - both[:, : 2 * size]
        return v + dot(z, solve(inner, rhs))

    start = jnp.concatenate([unit - 1.0 / size, unit], axis=1)
    v = lax.fori_loop(0, 2 * count, step, start)
    w = v[:, size:].T
    half = size // 2
    first, second = w[:, :half], w[:, half:]
    w = jnp.concatenate(
        [jnp.where(member == 0, first, second), jnp.where(member == 0, second, first)], axis=1
    )
    high = w.astype(BF16).astype(F32)
    low = w - high
    out[...] = jnp.concatenate([high, high, low], axis=1)


def chain(ids, mine, other):
    count, size, _ = mine.shape
    smem = pl.BlockSpec(memory_space=pltpu.SMEM)
    vmem = pl.BlockSpec(memory_space=pltpu.VMEM)
    return pl.pallas_call(
        chain_kernel,
        out_shape=jax.ShapeDtypeStruct((size, 3 * size), F32),
        in_specs=[smem, vmem, vmem],
        out_specs=vmem,
        compiler_params=params(),
        name="chain",
    )(ids, mine, other)


def apply_kernel(w_ref, own0, other0, own1, other1, out):
    field = pl.program_id(0)
    size = w_ref.shape[0]
    rows, half = own0.shape[:2]
    weights = w_ref[...].astype(BF16)
    flat = out.reshape(size * half * rows, LANES)

    def run(own, other):
        for r in range(rows):
            parts = [
                jnp.concatenate([src[r, ct] for ct in range(half)], axis=1) for src in (own, other)
            ]
            high = [x.astype(BF16) for x in parts]
            low = [(x - y.astype(F32)).astype(BF16) for x, y in zip(parts, high)]
            stacked = jnp.concatenate([*high, *low, *high], axis=0)
            result = jnp.dot(weights, stacked, preferred_element_type=F32)
            for ct in range(half):
                flat[pl.ds(ct * rows + r, size, stride=half * rows), :] = result[
                    :, ct * LANES : (ct + 1) * LANES
                ]

    @pl.when(field == 0)
    def _():
        run(own0, other0)

    @pl.when(field == 1)
    def _():
        run(own1, other1)


def apply(weights, own0, other0, own1, other1):
    rows, half, members, _ = own0.shape
    size = 2 * members
    r8 = rows // SUB
    block = (SUB, half, members, LANES)
    zero = pl.BlockSpec(block, lambda f, r: (jnp.where(f == 0, r, r8 - 1), 0, 0, 0))
    one = pl.BlockSpec(block, lambda f, r: (jnp.where(f == 1, r, 0), 0, 0, 0))
    return pl.pallas_call(
        apply_kernel,
        grid=(2, r8),
        out_shape=jax.ShapeDtypeStruct((size, 2, r8, half, SUB, LANES), F32),
        in_specs=[
            pl.BlockSpec(weights.shape, lambda f, r: (0, 0)), zero, zero, one, one,
        ],
        out_specs=pl.BlockSpec((size, 1, 1, half, SUB, LANES), lambda f, r: (0, f, r, 0, 0, 0)),
        compiler_params=params(),
        name="apply",
    )(weights, own0, other0, own1, other1)


def body(state, courant, diffusion, obs_cells, obs_owner, batch_order, obs_values, obs_error):
    slab = lax.axis_index("space")
    member = lax.axis_index("member")
    space = lax.axis_size("space")
    ids = jnp.stack([slab, member]).astype(jnp.int32)
    up = [(i, i + 1) for i in range(space - 1)]
    down = [(i + 1, i) for i in range(space - 1)]
    swap = [(0, 1), (1, 0)]

    state6, flow5, nu5 = tiled(state), tiled(courant), tiled(diffusion)
    up0, up1, down0, down1 = pack_edges(state6, flow5, nu5)
    before0 = lax.ppermute(up0, "space", up)
    after0 = lax.ppermute(down0, "space", down)
    before1 = lax.ppermute(up1, "space", up)
    after1 = lax.ppermute(down1, "space", down)

    scalars = (ids, obs_cells, obs_owner, batch_order)
    own0, send0, keep, away = forecast(0, True, *scalars, state6, flow5, nu5, before0, after0)
    other = lax.ppermute(away, "member", swap)
    gh = gram(ids, obs_owner, batch_order, keep, other, obs_values, obs_error)
    own1, send1 = forecast(1, False, *scalars, state6, flow5, nu5, before1, after1)
    other0 = lax.ppermute(send0, "member", swap)
    other1 = lax.ppermute(send1, "member", swap)
    bit = 1
    while bit < space:
        gh = gh + lax.ppermute(gh, "space", [(i, i ^ bit) for i in range(space)])
        bit *= 2
    theirs = lax.ppermute(gh, "member", swap)
    weights = chain(ids, gh, theirs)
    return untiled(apply(weights, own0, other0, own1, other1))


def solution(mesh):
    placed = (
        P("member", None, "space", None),
        P(None, "space", None),
        P(None, "space", None),
        P(),
        P(),
        P(),
        P(),
        P(),
    )
    return jax.shard_map(
        body,
        mesh=mesh,
        in_specs=placed,
        out_specs=P(None, None, "space", "member"),
        check_vma=False,
    )
```

time: 1190 us -> 178 us (0.15)
  waiting for transfers between devices: 654 us -> 26.5 us
  other arithmetic: 180 us -> 1.59 us
  matrix products: 144 us -> 0 us
  local copies, waits for them, and re-layouts: 135 us -> 5.96 us
  Pallas kernels: 0 us -> 113 us
  between operations: 39.7 us -> 0.13 us
  blocking collectives: 18.5 us -> 0 us
  starting transfers between devices: 11.7 us -> 28.9 us
    psum x8 -> x0, waiting for transfers between devices: 643 us -> none  [spread(): return lax.psum(kept, axis)]
    dot_general x47 -> x0, matrix products: 141 us -> none  [the longest x8 92.9 us: body(): ensemble = jnp.dot(transform.T, ensemble, precision=HIGH)]
    pallas_call x0 -> x6, Pallas kernels: none -> 113 us  [the longest x2 69.5 us: forecast(): pl.pallas_call(functools.partial(forecast_kernel, gather), out_shape=out_...]
    another operation x40 -> x1, other arithmetic: 97 us -> 0.62 us  [body(): ids = jnp.stack([slab, member]).astype(jnp.int32)]
    unnamed x30 -> x20, local copies, waits for them, and re-layouts: 60.1 us -> 5.35 us
    all_to_all x1 -> x0, other arithmetic: 31.3 us -> none  [body(): lax.all_to_all(fields, 'member', split_axis=3, concat_axis=0, tiled=True)]
    add x2 -> x4, other arithmetic: 21.1 us -> 0.97 us  [body(): gh = gh + lax.ppermute(gh, 'space', [(i, i ^ bit) for i in range(space)])]
    all_to_all x1 -> x0, blocking collectives: 18.5 us -> none  [body(): lax.all_to_all(fields, 'member', split_axis=3, concat_axis=0, tiled=True)]
  transfers between devices with their start and end apart: 13 -> 12, of which waited for: 11 -> 7; matrix products, arithmetic and copies ran while one was open for 17% -> 1% of each run, Pallas kernels for 0% -> 55%
where the time goes in v1:
time: 178 us; the launch traced here: 176 us
  Pallas kernels  113 us (63%)
  starting transfers between devices  28.9 us (16%)
  waiting for transfers between devices  26.5 us (15%)
  local copies, waits for them, and re-layouts  5.96 us (3%)
    pallas_call x2, Pallas kernels, forecast(): pl.pallas_call(functools.partial(forecast_kernel, gather), out_shape=out_...  69.5 us
    pallas_call x1, Pallas kernels, chain(): pl.pallas_call(chain_kernel, out_shape=jax.ShapeDtypeStruct((size, 3 * si...  24.5 us
    ppermute x4, waiting for transfers between devices, body(): gh = gh + lax.ppermute(gh, 'space', [(i, i ^ bit) for i in range(space)])  20.8 us
    ppermute x4, starting transfers between devices, body(): gh = gh + lax.ppermute(gh, 'space', [(i, i ^ bit) for i in range(space)])  16.3 us
    pallas_call x1, Pallas kernels, apply(): pl.pallas_call(apply_kernel, grid=(2, r8), out_shape=jax.ShapeDtypeStruct...  14.2 us
    unnamed x20, local copies, waits for them, and re-layouts  5.35 us
    ppermute x1, starting transfers between devices, body(): before1 = lax.ppermute(up1, 'space', up)  4.84 us
    ppermute x1, starting transfers between devices, body(): before0 = lax.ppermute(up0, 'space', up)  4.55 us
  transfers between devices with their start and end apart: 12, of which 7 were waited for; matrix products, arithmetic and copies ran while one was open for 1% of the time, Pallas kernels for 55%

profile of v1, /device:TPU:0, one launch (start us, length us, event | category | flops | bytes accessed | tf_op | source)
XLA Modules:
  0.0 176.5 jit_solution(13214415660141632727)
XLA Ops:
  0.0 2.5 %pack_edges.1 = (f32[4,72,128]{2,1,0:T(8,128)}, f32[4,72,128]{2,1,0:T(8,128)}, f32[4,72,128]{2,1,0:T(8,128)}, f32[4,72,128]{2,1,0:T(8,128)}) custom-call(f32[32,2,8,4,8,128]{5,4,3,2,1,0:T(8,128)} %bitcast.14, f32[32,2,8,4,8,128]{5,4,3,2,1,0:T(8,128)} %bitcast.15, f32[2,8,4,8,128]{4,3,2,1,0:T(8,128)} %bitcast.18, f32[2,8,4,8,128]{4,3,2,1,0:T(8,128)} %bitcast.19, ...), custom_call_target="tpu_custom_call" | custom-call | tf_op jit(solution)/shard_map/pack_edges/pallas_call | solution.py:77
  2.5 4.8 %collective-permute-start.9 = (f32[4,72,128]{2,1,0:T(8,128)}, f32[4,72,128]{2,1,0:T(8,128)S(1)}, u32[]{:S(2)}, u32[]{:S(2)}) collective-permute-start(f32[4,72,128]{2,1,0:T(8,128)} %get-tuple-element.21), channel_id=1, source_target_pairs={{0,1},{1,2},{2,3},{3,4},{4,5},{5,6},{6,7},{7,8},{8,9},{9,10},{10,1... | collective-permute-start | bytes 442376 | tf_op jit(solution)/shard_map/ppermute | solution.py:477
  7.4 1.3 collective-permute-start.10
  8.7 4.6 %collective-permute-start = (f32[4,72,128]{2,1,0:T(8,128)}, f32[4,72,128]{2,1,0:T(8,128)S(1)}, u32[]{:S(2)}, u32[]{:S(2)}) collective-permute-start(f32[4,72,128]{2,1,0:T(8,128)} %get-tuple-element.15), channel_id=1, source_target_pairs={{0,1},{1,2},{2,3},{3,4},{4,5},{5,6},{6,7},{7,8},{8,9},{9,10},{10,1... | collective-permute-start | bytes 442376 | tf_op jit(solution)/shard_map/ppermute | solution.py:475
  13.2 1.3 collective-permute-start.1
  15.2 0.7 collective-permute-done.10.after
  15.8 0.7 copy-done.7
  16.5 24.5 %forecast.1 = (f32[64,2,32,128]{3,2,1,0:T(8,128)}, f32[64,2,32,128]{3,2,1,0:T(8,128)}) custom-call(s32[2]{0:T(128)} %pad_add_fusion.ids, s32[8,512]{1,0:T(8,128)} %cells.3, s32[8]{0:T(128)} %owner.5, s32[8]{0:T(128)} %order.5, f32[32,2,8,4,8,128]{5,4,3,2,1,0:T(8,128)} %bitcast.16, f32[2,8,4,8,128]{4,3,2,1,0:T(8,128)} %bitcast.20, ...), custom_call_target="tpu_custom_call" | custom-call | flops 41943040 | bytes 8388608 | tf_op jit(solution)/shard_map/forecast/pallas_call | solution.py:244
  42.4 45.0 %forecast_gather.1 = (f32[64,2,32,128]{3,2,1,0:T(8,128)}, f32[64,2,32,128]{3,2,1,0:T(8,128)}, f32[4,4,32,128]{3,2,1,0:T(8,128)}, f32[4,4,32,128]{3,2,1,0:T(8,128)}) custom-call(s32[2]{0:T(128)} %pad_add_fusion.ids, s32[8,512]{1,0:T(8,128)} %cells.3, s32[8]{0:T(128)} %owner.5, s32[8]{0:T(128)} %order.5, f32[32,2,8,4,8,128]{5,4,3,2,1,0:T(8,128)} %bitcast.17, ...), custom_call_target="tpu_custom_call" | custom-call | flops 41943040 | bytes 8388608 | tf_op jit(solution)/shard_map/forecast_gather/pallas_call | solution.py:244
  88.4 3.7 %collective-permute-done.2.other = f32[4,4,32,128]{3,2,1,0:T(8,128)S(1)} collective-permute-done((f32[4,4,32,128]{3,2,1,0:T(8,128)}, f32[4,4,32,128]{3,2,1,0:T(8,128)S(1)}, u32[]{:S(2)}, u32[]{:S(2)}) %collective-permute-start.2) | collective-permute-done | bytes 262176 | tf_op jit(solution)/shard_map/ppermute | solution.py:482
  92.2 0.7 copy-done.3
  92.9 2.8 %gram.1 = f32[4,64,128]{2,1,0:T(8,128)} custom-call(s32[2]{0:T(128)} %pad_add_fusion.ids, s32[8]{0:T(128)} %owner.5, s32[8]{0:T(128)} %order.5, f32[4,4,32,128]{3,2,1,0:T(8,128)} %get-tuple-element.17.keep, f32[4,4,32,128]{3,2,1,0:T(8,128)} %copy-done.3, f32[8,64,512]{2,1,0:T(8,128)} %observed.1, f32[8,1,512]{2,1,0:T(1,128)} %broadcast_in_dim.3.variance), custom_call_target="tpu_custom_call" | custom-call | tf_op jit(solution)/shard_map/gram/pallas_call | solution.py:312
  95.6 6.0 %collective-permute-done.3 = f32[4,64,128]{2,1,0:T(8,128)S(1)} collective-permute-done((f32[4,64,128]{2,1,0:T(8,128)}, f32[4,64,128]{2,1,0:T(8,128)S(1)}, u32[]{:S(2)}, u32[]{:S(2)}) %collective-permute-start.3) | collective-permute-done | bytes 131104 | tf_op jit(solution)/shard_map/ppermute | solution.py:489
  101.6 0.9 add.12
  102.6 5.0 %collective-permute-done.4 = f32[4,64,128]{2,1,0:T(8,128)S(1)} collective-permute-done((f32[4,64,128]{2,1,0:T(8,128)S(1)}, f32[4,64,128]{2,1,0:T(8,128)S(1)}, u32[]{:S(2)}, u32[]{:S(2)}) %collective-permute-start.4) | collective-permute-done | bytes 131104 | tf_op jit(solution)/shard_map/ppermute | solution.py:489
  107.7 5.0 %collective-permute-done.5 = f32[4,64,128]{2,1,0:T(8,128)S(1)} collective-permute-done((f32[4,64,128]{2,1,0:T(8,128)S(1)}, f32[4,64,128]{2,1,0:T(8,128)S(1)}, u32[]{:S(2)}, u32[]{:S(2)}) %collective-permute-start.5) | collective-permute-done | bytes 131104 | tf_op jit(solution)/shard_map/ppermute | solution.py:489
  112.7 16.2 %collective-permute-start.6 = (f32[4,64,128]{2,1,0:T(8,128)S(1)}, f32[4,64,128]{2,1,0:T(8,128)S(1)}, u32[]{:S(2)}, u32[]{:S(2)}) collective-permute-start(f32[4,64,128]{2,1,0:T(8,128)S(1)} %add.14), channel_id=1, source_target_pairs={{0,8},{1,9},{2,10},{3,11},{4,12},{5,13},{6,14},{7,15},{8,0},{9,1},... | collective-permute-start | bytes 393224 | tf_op jit(solution)/shard_map/ppermute | solution.py:489
  128.8 4.9 %collective-permute-done.6 = f32[4,64,128]{2,1,0:T(8,128)S(1)} collective-permute-done((f32[4,64,128]{2,1,0:T(8,128)S(1)}, f32[4,64,128]{2,1,0:T(8,128)S(1)}, u32[]{:S(2)}, u32[]{:S(2)}) %collective-permute-start.6) | collective-permute-done | bytes 131104 | tf_op jit(solution)/shard_map/ppermute | solution.py:489
  133.8 1.3 collective-permute-done.7.other
  135.1 0.7 copy-done.8
  135.8 24.5 %chain.1.w_ref = f32[64,192]{1,0:T(8,128)} custom-call(s32[2]{0:T(128)} %pad_add_fusion.ids, f32[4,64,128]{2,1,0:T(8,128)} %copy-done.2, f32[4,64,128]{2,1,0:T(8,128)} %copy-done.8), custom_call_target="tpu_custom_call" | custom-call | tf_op jit(solution)/shard_map/chain/pallas_call | solution.py:404
  160.3 1.4 copy-done
  161.6 0.7 copy-done.1
  162.3 14.2 %apply.1 = f32[64,2,8,2,8,128]{5,4,3,2,1,0:T(8,128)} custom-call(f32[64,192]{1,0:T(8,128)} %chain.1.w_ref, f32[64,2,32,128]{3,2,1,0:T(8,128)} %get-tuple-element.19.own0, f32[64,2,32,128]{3,2,1,0:T(8,128)} %copy-done.1, f32[64,2,32,128]{3,2,1,0:T(8,128)} %get-tuple-element.23.own1, f32[64,2,32,128]{3,2,1,0:T(8,128)} %copy-done), custom_call_target="tpu_custom_call" | custom-call | tf_op jit(solution)/shard_map/apply/pallas_call | solution.py:451
  (32 shorter events, 3.3 us)
Async XLA Ops:
  2.5 12.6 %collective-permute-start.9 = (f32[4,72,128]{2,1,0:T(8,128)}, f32[4,72,128]{2,1,0:T(8,128)S(1)}, u32[]{:S(2)}, u32[]{:S(2)}) collective-permute-start(f32[4,72,128]{2,1,0:T(8,128)} %get-tuple-element.21), channel_id=1, source_target_pairs={{0,1},{1,2},{2,3},{3,4},{4,5},{5,6},{6,7},{7,8},{8,9},{9,10},{10,1... | collective-permute-start | bytes 442376 | tf_op jit(solution)/shard_map/ppermute | solution.py:477
  7.4 8.5 %collective-permute-start.10 = (f32[4,72,128]{2,1,0:T(8,128)}, f32[4,72,128]{2,1,0:T(8,128)S(1)}, u32[]{:S(2)}, u32[]{:S(2)}) collective-permute-start(f32[4,72,128]{2,1,0:T(8,128)} %get-tuple-element.22), channel_id=1, source_target_pairs={{1,0},{2,1},{3,2},{4,3},{5,4},{6,5},{7,6},{8,7},{9,8},{10,9},{11,1... | collective-permute-start | bytes 442376 | tf_op jit(solution)/shard_map/ppermute | solution.py:478
  8.7 32.4 %collective-permute-start = (f32[4,72,128]{2,1,0:T(8,128)}, f32[4,72,128]{2,1,0:T(8,128)S(1)}, u32[]{:S(2)}, u32[]{:S(2)}) collective-permute-start(f32[4,72,128]{2,1,0:T(8,128)} %get-tuple-element.15), channel_id=1, source_target_pairs={{0,1},{1,2},{2,3},{3,4},{4,5},{5,6},{6,7},{7,8},{8,9},{9,10},{10,1... | collective-permute-start | bytes 442376 | tf_op jit(solution)/shard_map/ppermute | solution.py:475
  13.2 27.8 %collective-permute-start.1 = (f32[4,72,128]{2,1,0:T(8,128)}, f32[4,72,128]{2,1,0:T(8,128)S(1)}, u32[]{:S(2)}, u32[]{:S(2)}) collective-permute-start(f32[4,72,128]{2,1,0:T(8,128)} %get-tuple-element.16), channel_id=1, source_target_pairs={{1,0},{2,1},{3,2},{4,3},{5,4},{6,5},{7,6},{8,7},{9,8},{10,9},{11,1... | collective-permute-start | bytes 442376 | tf_op jit(solution)/shard_map/ppermute | solution.py:476
  15.2 0.7 copy-start.6
  15.8 0.7 copy-start.7
  41.0 46.8 %copy-start.9 = (f32[8,512]{1,0:T(8,128)S(1)}, f32[8,512]{1,0:T(8,128)}, u32[]{:S(2)}) copy-start(f32[8,512]{1,0:T(8,128)} %param.15) | copy-start | bytes 49156
  41.0 119.2 %collective-permute-start.11 = (f32[64,2,32,128]{3,2,1,0:T(8,128)}, f32[64,2,32,128]{3,2,1,0:T(8,128)S(1)}, u32[]{:S(2)}, u32[]{:S(2)}) collective-permute-start(f32[64,2,32,128]{3,2,1,0:T(8,128)} %get-tuple-element.24), channel_id=1, source_target_pairs={{0,16},{16,0},{1,17},{17,1},{2,18},{18,2},{3,19},{19,3},{4,20},{20... | collective-permute-start | bytes 6291464 | tf_op jit(solution)/shard_map/ppermute | solution.py:486
  41.0 0.7 copy-start.4
  41.7 0.7 copy-start.5
  87.3 72.9 %collective-permute-start.8 = (f32[64,2,32,128]{3,2,1,0:T(8,128)}, f32[64,2,32,128]{3,2,1,0:T(8,128)S(1)}, u32[]{:S(2)}, u32[]{:S(2)}) collective-permute-start(f32[64,2,32,128]{3,2,1,0:T(8,128)} %get-tuple-element.20), channel_id=1, source_target_pairs={{0,16},{16,0},{1,17},{17,1},{2,18},{18,2},{3,19},{19,3},{4,20},{20... | collective-permute-start | bytes 6291464 | tf_op jit(solution)/shard_map/ppermute | solution.py:485
  87.8 4.4 %collective-permute-start.2 = (f32[4,4,32,128]{3,2,1,0:T(8,128)}, f32[4,4,32,128]{3,2,1,0:T(8,128)S(1)}, u32[]{:S(2)}, u32[]{:S(2)}) collective-permute-start(f32[4,4,32,128]{3,2,1,0:T(8,128)} %get-tuple-element.18), channel_id=1, source_target_pairs={{0,16},{16,0},{1,17},{17,1},{2,18},{18,2},{3,19},{19,3},{4,20},{20... | collective-permute-start | bytes 786440 | tf_op jit(solution)/shard_map/ppermute | solution.py:482
  92.2 0.7 copy-start.3
  95.6 6.0 %collective-permute-start.3 = (f32[4,64,128]{2,1,0:T(8,128)}, f32[4,64,128]{2,1,0:T(8,128)S(1)}, u32[]{:S(2)}, u32[]{:S(2)}) collective-permute-start(f32[4,64,128]{2,1,0:T(8,128)} %gram.1), channel_id=1, source_target_pairs={{0,1},{1,0},{2,3},{3,2},{4,5},{5,4},{6,7},{7,6},{8,9},{9,8},{10,11... | collective-permute-start | bytes 393224 | tf_op jit(solution)/shard_map/ppermute | solution.py:489
  102.5 5.0 %collective-permute-start.4 = (f32[4,64,128]{2,1,0:T(8,128)S(1)}, f32[4,64,128]{2,1,0:T(8,128)S(1)}, u32[]{:S(2)}, u32[]{:S(2)}) collective-permute-start(f32[4,64,128]{2,1,0:T(8,128)S(1)} %add.12), channel_id=1, source_target_pairs={{0,2},{1,3},{2,0},{3,1},{4,6},{5,7},{6,4},{7,5},{8,10},{9,11},{10,... | collective-permute-start | bytes 393224 | tf_op jit(solution)/shard_map/ppermute | solution.py:489
  107.6 5.0 %collective-permute-start.5 = (f32[4,64,128]{2,1,0:T(8,128)S(1)}, f32[4,64,128]{2,1,0:T(8,128)S(1)}, u32[]{:S(2)}, u32[]{:S(2)}) collective-permute-start(f32[4,64,128]{2,1,0:T(8,128)S(1)} %add.13), channel_id=1, source_target_pairs={{0,4},{1,5},{2,6},{3,7},{4,0},{5,1},{6,2},{7,3},{8,12},{9,13},{10,... | collective-permute-start | bytes 393224 | tf_op jit(solution)/shard_map/ppermute | solution.py:489
  112.7 21.0 %collective-permute-start.6 = (f32[4,64,128]{2,1,0:T(8,128)S(1)}, f32[4,64,128]{2,1,0:T(8,128)S(1)}, u32[]{:S(2)}, u32[]{:S(2)}) collective-permute-start(f32[4,64,128]{2,1,0:T(8,128)S(1)} %add.14), channel_id=1, source_target_pairs={{0,8},{1,9},{2,10},{3,11},{4,12},{5,13},{6,14},{7,15},{8,0},{9,1},... | collective-permute-start | bytes 393224 | tf_op jit(solution)/shard_map/ppermute | solution.py:489
  133.7 1.4 copy-start.2
  133.7 1.4 collective-permute-start.7
  135.1 0.7 copy-start.8
  160.3 1.4 copy-start
  160.3 2.0 %copy-start.1 = (f32[64,2,32,128]{3,2,1,0:T(8,128)}, f32[64,2,32,128]{3,2,1,0:T(8,128)S(1)}, u32[]{:S(2)}) copy-start(f32[64,2,32,128]{3,2,1,0:T(8,128)S(1)} %collective-permute-done.8.other0) | copy-start | bytes 6291460

commit v2 on v1

--- a/solution.py
+++ b/solution.py
@@ -12,12 +12,27 @@
 BF16 = jnp.bfloat16
 LANES = 128
 SUB = 8
+GATHER = 32
 PACK = 8
-VMEM_LIMIT = 56 * 1024 * 1024
-
-
-def params(**kw):
-    return pltpu.CompilerParams(vmem_limit_bytes=VMEM_LIMIT, **kw)
+
+
+def params(mib):
+    return pltpu.CompilerParams(vmem_limit_bytes=mib * 1024 * 1024)
+
+
+def unrolled(count, most):
+    return max(d for d in range(1, most + 1) if count % d == 0)
+
+
+def rows_loop(count, most, fn):
+    step = unrolled(count, most)
+
+    def run(i, carry):
+        for u in range(step):
+            fn(i * step + u)
+        return carry
+
+    lax.fori_loop(0, count // step, run, 0)
 
 
 def tiled(array):
@@ -83,7 +98,7 @@
             row_block(0), row_block(last),
         ],
         out_specs=[pl.BlockSpec(msg.shape, lambda i: (0, 0, 0))] * (2 * fields),
-        compiler_params=params(),
+        compiler_params=params(60),
         name="pack_edges",
     )(state6, state6, flow5, flow5, nu5, nu5)
 
@@ -162,24 +177,26 @@
             q0[k, ct] = before[at, pl.ds(k * members, members), :]
             q0[rows + 2 + k, ct] = after[at, pl.ds(k * members, members), :]
 
-    def load(r, carry):
-        for ct in range(nct):
-            start = (lax.div(r, SUB) * nct + phys(ct)) * SUB + lax.rem(r, SUB)
-            q0[r + 2, ct] = flat[pl.ds(start, members, stride=r8 * nct * SUB), :]
+    def load(block, carry):
+        for sub in range(SUB):
+            for ct in range(nct):
+                start = (block * nct + phys(ct)) * SUB + sub
+                q0[block * SUB + sub + 2, ct] = flat[
+                    pl.ds(start, members, stride=r8 * nct * SUB), :
+                ]
         return carry
 
-    lax.fori_loop(0, rows, load, 0)
-
-    def first_step(r, carry):
+    lax.fori_loop(0, r8, load, 0)
+
+    def first_step(r):
         def put(ct, at, value):
             q1[r, ct, at, :] = value
 
         stencil_row(q0, r, put, coef.at[:, :, pl.ds(SUB - 1, rows + 2)], members)
-        return carry
-
-    lax.fori_loop(0, rows + 2, first_step, 0)
-
-    def second_step(r, carry):
+
+    rows_loop(rows + 2, 6, first_step)
+
+    def second_step(r):
         def put(ct, at, value):
             if ct < half:
                 own[r, ct, at, :] = value
@@ -189,13 +206,14 @@
                 q0[r, ct, at, :] = value
 
         stencil_row(q1, r, put, coef.at[:, :, pl.ds(SUB, rows)], members)
-        return carry
-
-    lax.fori_loop(0, rows, second_step, 0)
+
+    rows_loop(rows, 4, second_step)
 
     if not gather:
         return
     nobs = cells.shape[1]
+    bits = width.bit_length() - 1
+    assert width == 1 << bits
     lane = lax.broadcasted_iota(jnp.int32, (members, LANES), 1)
     for position in range(order.shape[0]):
         batch = order[position]
@@ -203,18 +221,20 @@
         kept = lax.rem(position, 2) == member
 
         def pick(tile, carry, batch=batch, mine=mine, kept=kept, position=position):
-            def one(o, acc):
-                cell = cells[batch, tile * LANES + o]
-                r = lax.div(cell, width)
-                c = lax.rem(cell, width)
-                at = lax.rem(lax.div(c, LANES) + member * half, nct)
-                shift = lax.rem(o - lax.rem(c, LANES) + LANES, LANES)
-                moved = pltpu.roll(q0[r, at], shift, 1)
-                return jnp.where(lane == o, moved, acc)
-
-            count = jnp.where(mine, LANES, 0)
-            acc = lax.fori_loop(0, count // 8, lambda g, a: functools.reduce(
-                lambda v, u: one(g * 8 + u, v), range(8), a), jnp.zeros((members, LANES), F32))
+            def some(group, acc):
+                for u in range(GATHER):
+                    o = group * GATHER + u
+                    cell = cells[batch, tile * LANES + o]
+                    r = lax.shift_right_logical(cell, bits)
+                    c = cell & (width - 1)
+                    at = (lax.shift_right_logical(c, 7) + member * half) & (nct - 1)
+                    moved = pltpu.roll(q0[r, at], (o - c) & (LANES - 1), 1)
+                    acc = jnp.where(lane == o, moved, acc)
+                return acc
+
+            acc = lax.fori_loop(
+                0, jnp.where(mine, LANES // GATHER, 0), some, jnp.zeros((members, LANES), F32)
+            )
 
             @pl.when(kept)
             def _():
@@ -263,7 +283,7 @@
                 pltpu.VMEM((5, nct, rows + 2 * SUB, LANES), F32),
             ],
         ),
-        compiler_params=params(),
+        compiler_params=params(32),
         cost_estimate=pl.CostEstimate(
             flops=40 * cells_n, bytes_accessed=8 * cells_n, transcendentals=0
         ),
@@ -314,7 +334,7 @@
         out_shape=jax.ShapeDtypeStruct((count, total, 2 * total), F32),
         in_specs=[smem] * 3 + [vmem] * 4,
         out_specs=vmem,
-        compiler_params=params(),
+        compiler_params=params(12),
         name="gram",
     )(ids, owner, order, keep, other, observed, variance[:, None, :])
 
@@ -394,7 +414,10 @@
     )
     high = w.astype(BF16).astype(F32)
     low = w - high
-    out[...] = jnp.concatenate([high, high, low], axis=1)
+    out[...] = jnp.concatenate(
+        [jnp.concatenate([high, high], axis=1), jnp.concatenate([low, jnp.zeros_like(low)], axis=1)],
+        axis=0,
+    )
 
 
 def chain(ids, mine, other):
@@ -403,17 +426,17 @@
     vmem = pl.BlockSpec(memory_space=pltpu.VMEM)
     return pl.pallas_call(
         chain_kernel,
-        out_shape=jax.ShapeDtypeStruct((size, 3 * size), F32),
+        out_shape=jax.ShapeDtypeStruct((2 * size, 2 * size), F32),
         in_specs=[smem, vmem, vmem],
         out_specs=vmem,
-        compiler_params=params(),
+        compiler_params=params(12),
         name="chain",
     )(ids, mine, other)
 
 
 def apply_kernel(w_ref, own0, other0, own1, other1, out):
     field = pl.program_id(0)
-    size = w_ref.shape[0]
+    size = w_ref.shape[0] // 2
     rows, half = own0.shape[:2]
     weights = w_ref[...].astype(BF16)
     flat = out.reshape(size * half * rows, LANES)
@@ -425,8 +448,9 @@
             ]
             high = [x.astype(BF16) for x in parts]
             low = [(x - y.astype(F32)).astype(BF16) for x, y in zip(parts, high)]
-            stacked = jnp.concatenate([*high, *low, *high], axis=0)
+            stacked = jnp.concatenate([*high, *low], axis=0)
             result = jnp.dot(weights, stacked, preferred_element_type=F32)
+            result = result[:size] + result[size:]
             for ct in range(half):
                 flat[pl.ds(ct * rows + r, size, stride=half * rows), :] = result[
                     :, ct * LANES : (ct + 1) * LANES
@@ -456,7 +480,7 @@
             pl.BlockSpec(weights.shape, lambda f, r: (0, 0)), zero, zero, one, one,
         ],
         out_specs=pl.BlockSpec((size, 1, 1, half, SUB, LANES), lambda f, r: (0, f, r, 0, 0, 0)),
-        compiler_params=params(),
+        compiler_params=params(12),
         name="apply",
     )(weights, own0, other0, own1, other1)
 
@@ -474,13 +498,14 @@
     up0, up1, down0, down1 = pack_edges(state6, flow5, nu5)
     before0 = lax.ppermute(up0, "space", up)
     after0 = lax.ppermute(down0, "space", down)
-    before1 = lax.ppermute(up1, "space", up)
-    after1 = lax.ppermute(down1, "space", down)
-
     scalars = (ids, obs_cells, obs_owner, batch_order)
     own0, send0, keep, away = forecast(0, True, *scalars, state6, flow5, nu5, before0, after0)
     other = lax.ppermute(away, "member", swap)
     gh = gram(ids, obs_owner, batch_order, keep, other, obs_values, obs_error)
+    up1, down1, _ = lax.optimization_barrier((up1, down1, keep))
+    before1 = lax.ppermute(up1, "space", up)
+    after1 = lax.ppermute(down1, "space", down)
+    before1, after1, gh = lax.optimization_barrier((before1, after1, gh))
     own1, send1 = forecast(1, False, *scalars, state6, flow5, nu5, before1, after1)
     other0 = lax.ppermute(send0, "member", swap)
     other1 = lax.ppermute(send1, "member", swap)

time: 178 us -> 119 us (0.67)
  Pallas kernels: 113 us -> 63.7 us
  starting transfers between devices: 28.9 us -> 22.8 us
  local copies, waits for them, and re-layouts: 5.96 us -> 3.42 us
  waiting for transfers between devices: 26.5 us -> 28.9 us
    pallas_call x2, Pallas kernels: 69.5 us -> 27 us  [forecast(): pl.pallas_call(functools.partial(forecast_kernel, gather), out_shape=out_...]
    ppermute x4, waiting for transfers between devices: 20.8 us -> 15.6 us  [body(): gh = gh + lax.ppermute(gh, 'space', [(i, i ^ bit) for i in range(space)])]
    ppermute x1, waiting for transfers between devices: 0.01 us -> 5 us  [body(): after0 = lax.ppermute(down0, 'space', down)]
    pallas_call x1, Pallas kernels: 14.2 us -> 9.49 us  [apply(): pl.pallas_call(apply_kernel, grid=(2, r8), out_shape=jax.ShapeDtypeStruct...]
    ppermute x1, waiting for transfers between devices: 3.75 us -> 0.01 us  [body(): other = lax.ppermute(away, 'member', swap)]
    ppermute x1, starting transfers between devices: 4.84 us -> 1.3 us  [body(): before1 = lax.ppermute(up1, 'space', up)]
    ppermute x1, waiting for transfers between devices: 0.66 us -> 4.13 us  [body(): after1 = lax.ppermute(down1, 'space', down)]
    ppermute x4, starting transfers between devices: 16.3 us -> 13.3 us  [body(): gh = gh + lax.ppermute(gh, 'space', [(i, i ^ bit) for i in range(space)])]
  transfers between devices with their start and end apart: 12 -> 12, of which waited for: 7 -> 9; matrix products, arithmetic and copies ran while one was open for 1% -> 0% of each run, Pallas kernels for 55% -> 30%
where the time goes in v2:
time: 119 us
  Pallas kernels  63.7 us (54%)
  waiting for transfers between devices  28.9 us (24%)
  starting transfers between devices  22.8 us (19%)
  local copies, waits for them, and re-layouts  3.42 us (3%)
    pallas_call x2, Pallas kernels, forecast(): pl.pallas_call(functools.partial(forecast_kernel, gather), out_shape=out_...  27 us
    pallas_call x1, Pallas kernels, chain(): pl.pallas_call(chain_kernel, out_shape=jax.ShapeDtypeStruct((2 * size, 2...  23.4 us
    ppermute x4, waiting for transfers between devices, body(): gh = gh + lax.ppermute(gh, 'space', [(i, i ^ bit) for i in range(space)])  15.6 us
    ppermute x4, starting transfers between devices, body(): gh = gh + lax.ppermute(gh, 'space', [(i, i ^ bit) for i in range(space)])  13.3 us
    pallas_call x1, Pallas kernels, apply(): pl.pallas_call(apply_kernel, grid=(2, r8), out_shape=jax.ShapeDtypeStruct...  9.49 us
    ppermute x1, waiting for transfers between devices, body(): after0 = lax.ppermute(down0, 'space', down)  5 us
    ppermute x1, starting transfers between devices, body(): before0 = lax.ppermute(up0, 'space', up)  4.85 us
    ppermute x1, waiting for transfers between devices, body(): after1 = lax.ppermute(down1, 'space', down)  4.13 us
  transfers between devices with their start and end apart: 12, of which 9 were waited for; matrix products, arithmetic and copies ran while one was open for 0% of the time, Pallas kernels for 30%

profile of v2, /device:TPU:0, one launch (start us, length us, event | category | flops | bytes accessed | tf_op | source)
XLA Modules:
  0.0 119.1 jit_solution(15459285824597873873)
XLA Ops:
  0.0 2.6 %pack_edges.1 = (f32[4,72,128]{2,1,0:T(8,128)}, f32[4,72,128]{2,1,0:T(8,128)}, f32[4,72,128]{2,1,0:T(8,128)}, f32[4,72,128]{2,1,0:T(8,128)}) custom-call(f32[32,2,8,4,8,128]{5,4,3,2,1,0:T(8,128)} %bitcast.14, f32[32,2,8,4,8,128]{5,4,3,2,1,0:T(8,128)} %bitcast.15, f32[2,8,4,8,128]{4,3,2,1,0:T(8,128)} %bitcast.18, f32[2,8,4,8,128]{4,3,2,1,0:T(8,128)} %bitcast.19, ...), custom_call_target="tpu_custom_call" | custom-call | tf_op jit(solution)/shard_map/pack_edges/pallas_call | solution.py:92
  2.6 4.9 %collective-permute-start = (f32[4,72,128]{2,1,0:T(8,128)}, f32[4,72,128]{2,1,0:T(8,128)S(1)}, u32[]{:S(2)}, u32[]{:S(2)}) collective-permute-start(f32[4,72,128]{2,1,0:T(8,128)} %get-tuple-element.22), channel_id=1, source_target_pairs={{0,1},{1,2},{2,3},{3,4},{4,5},{5,6},{6,7},{7,8},{8,9},{9,10},{10,1... | collective-permute-start | bytes 442376 | tf_op jit(solution)/shard_map/ppermute | solution.py:499
  7.5 1.3 %collective-permute-start.1 = (f32[4,72,128]{2,1,0:T(8,128)}, f32[4,72,128]{2,1,0:T(8,128)S(1)}, u32[]{:S(2)}, u32[]{:S(2)}) collective-permute-start(f32[4,72,128]{2,1,0:T(8,128)} %get-tuple-element.23), channel_id=1, source_target_pairs={{1,0},{2,1},{3,2},{4,3},{5,4},{6,5},{7,6},{8,7},{9,8},{10,9},{11,1... | collective-permute-start | bytes 442376 | tf_op jit(solution)/shard_map/ppermute | solution.py:500
  8.8 2.0 %collective-permute-done.before = f32[4,72,128]{2,1,0:T(8,128)S(1)} collective-permute-done((f32[4,72,128]{2,1,0:T(8,128)}, f32[4,72,128]{2,1,0:T(8,128)S(1)}, u32[]{:S(2)}, u32[]{:S(2)}) %collective-permute-start) | collective-permute-done | bytes 147488 | tf_op jit(solution)/shard_map/ppermute | solution.py:499
  10.9 5.0 %collective-permute-done.1.after = f32[4,72,128]{2,1,0:T(8,128)S(1)} collective-permute-done((f32[4,72,128]{2,1,0:T(8,128)}, f32[4,72,128]{2,1,0:T(8,128)S(1)}, u32[]{:S(2)}, u32[]{:S(2)}) %collective-permute-start.1) | collective-permute-done | bytes 147488 | tf_op jit(solution)/shard_map/ppermute | solution.py:500
  15.9 3.4 %copy-done = f32[32,2,64,512]{3,2,1,0:T(8,128)S(1)} copy-done((f32[32,2,64,512]{3,2,1,0:T(8,128)S(1)}, f32[32,2,64,512]{3,2,1,0:T(8,128)}, u32[]{:S(2)}) %copy-start) | copy-done | bytes 8388632
  19.3 15.8 %forecast_gather.1 = (f32[64,2,32,128]{3,2,1,0:T(8,128)S(1)}, f32[64,2,32,128]{3,2,1,0:T(8,128)S(1)}, f32[4,4,32,128]{3,2,1,0:T(8,128)S(1)}, f32[4,4,32,128]{3,2,1,0:T(8,128)S(1)}) custom-call(s32[2]{0:T(128)S(1)} %pad_add_fusion.ids, s32[8,512]{1,0:T(8,128)S(1)} %copy-done.4, s32[8]{0:T(128)S(1)} %copy-done.5, s32[8]{0:T(128)S(1)} %copy-done.6, ...), custom_call_target="tpu_custom_call" | custom-call | flops 41943040 | bytes 8388608 | tf_op jit(solution)/shard_map/forecast_gather/pallas_call | solution.py:264
  35.2 1.3 %collective-permute-start.2 = (f32[4,72,128]{2,1,0:T(8,128)S(1)}, f32[4,72,128]{2,1,0:T(8,128)S(1)}, u32[]{:S(2)}, u32[]{:S(2)}) collective-permute-start(f32[4,72,128]{2,1,0:T(8,128)S(1)} %copy-done.9), channel_id=1, source_target_pairs={{0,1},{1,2},{2,3},{3,4},{4,5},{5,6},{6,7},{7,8},{8,9},{9,10},{10,1... | collective-permute-start | bytes 442376 | tf_op jit(solution)/shard_map/ppermute | solution.py:506
  36.5 1.3 %collective-permute-start.3 = (f32[4,72,128]{2,1,0:T(8,128)S(1)}, f32[4,72,128]{2,1,0:T(8,128)S(1)}, u32[]{:S(2)}, u32[]{:S(2)}) collective-permute-start(f32[4,72,128]{2,1,0:T(8,128)S(1)} %copy-done.8), channel_id=1, source_target_pairs={{1,0},{2,1},{3,2},{4,3},{5,4},{6,5},{7,6},{8,7},{9,8},{10,9},{11,1... | collective-permute-start | bytes 442376 | tf_op jit(solution)/shard_map/ppermute | solution.py:507
  38.4 1.2 %gram.1 = f32[4,64,128]{2,1,0:T(8,128)S(1)} custom-call(s32[2]{0:T(128)S(1)} %pad_add_fusion.ids, s32[8]{0:T(128)S(1)} %copy-done.5, s32[8]{0:T(128)S(1)} %copy-done.6, f32[4,4,32,128]{3,2,1,0:T(8,128)S(1)} %get-tuple-element.24.keep, f32[4,4,32,128]{3,2,1,0:T(8,128)S(1)} %collective-permute-done.4.other, f32[8,64,512]{2,1,0:T(8,128)S(1)} %copy-done.3, ...), custom_call_target="tpu_custom_call" | custom-call | tf_op jit(solution)/shard_map/gram/pallas_call | solution.py:332
  39.6 0.9 collective-permute-done.2.before
  40.5 4.1 %collective-permute-done.3.after = f32[4,72,128]{2,1,0:T(8,128)S(1)} collective-permute-done((f32[4,72,128]{2,1,0:T(8,128)S(1)}, f32[4,72,128]{2,1,0:T(8,128)S(1)}, u32[]{:S(2)}, u32[]{:S(2)}) %collective-permute-start.3) | collective-permute-done | bytes 147488 | tf_op jit(solution)/shard_map/ppermute | solution.py:507
  44.6 11.2 %forecast.1 = (f32[64,2,32,128]{3,2,1,0:T(8,128)S(1)}, f32[64,2,32,128]{3,2,1,0:T(8,128)S(1)}) custom-call(s32[2]{0:T(128)S(1)} %pad_add_fusion.ids, s32[8,512]{1,0:T(8,128)S(1)} %copy-done.4, s32[8]{0:T(128)S(1)} %copy-done.5, s32[8]{0:T(128)S(1)} %copy-done.6, f32[32,2,8,4,8,128]{5,4,3,2,1,0:T(8,128)S(1)} %bitcast.17, f32[2,8,4,8,128]{4,3,2,1,0:T(8,128)S(1)} %bitcast.21, ...), custom_call_target="tpu_custom_call" | custom-call | flops 41943040 | bytes 8388608 | tf_op jit(solution)/shard_map/forecast/pallas_call | solution.py:264
  55.9 1.4 %collective-permute-start.5 = (f32[4,64,128]{2,1,0:T(8,128)S(1)}, f32[4,64,128]{2,1,0:T(8,128)S(1)}, u32[]{:S(2)}, u32[]{:S(2)}) collective-permute-start(f32[4,64,128]{2,1,0:T(8,128)S(1)} %gram.1), channel_id=1, source_target_pairs={{0,1},{1,0},{2,3},{3,2},{4,5},{5,4},{6,7},{7,6},{8,9},{9,8},{10,11... | collective-permute-start | bytes 393224 | tf_op jit(solution)/shard_map/ppermute | solution.py:514
  57.3 4.5 %collective-permute-done.5 = f32[4,64,128]{2,1,0:T(8,128)S(1)} collective-permute-done((f32[4,64,128]{2,1,0:T(8,128)S(1)}, f32[4,64,128]{2,1,0:T(8,128)S(1)}, u32[]{:S(2)}, u32[]{:S(2)}) %collective-permute-start.5) | collective-permute-done | bytes 131104 | tf_op jit(solution)/shard_map/ppermute | solution.py:514
  61.8 2.9 %collective-permute-start.6 = (f32[4,64,128]{2,1,0:T(8,128)S(1)}, f32[4,64,128]{2,1,0:T(8,128)S(1)}, u32[]{:S(2)}, u32[]{:S(2)}) collective-permute-start(f32[4,64,128]{2,1,0:T(8,128)S(1)} %add.12), channel_id=1, source_target_pairs={{0,2},{1,3},{2,0},{3,1},{4,6},{5,7},{6,4},{7,5},{8,10},{9,11},{10,... | collective-permute-start | bytes 393224 | tf_op jit(solution)/shard_map/ppermute | solution.py:514
  64.7 3.5 %collective-permute-done.6 = f32[4,64,128]{2,1,0:T(8,128)S(1)} collective-permute-done((f32[4,64,128]{2,1,0:T(8,128)S(1)}, f32[4,64,128]{2,1,0:T(8,128)S(1)}, u32[]{:S(2)}, u32[]{:S(2)}) %collective-permute-start.6) | collective-permute-done | bytes 131104 | tf_op jit(solution)/shard_map/ppermute | solution.py:514
  68.2 7.7 %collective-permute-start.7 = (f32[4,64,128]{2,1,0:T(8,128)S(1)}, f32[4,64,128]{2,1,0:T(8,128)S(1)}, u32[]{:S(2)}, u32[]{:S(2)}) collective-permute-start(f32[4,64,128]{2,1,0:T(8,128)S(1)} %add.13), channel_id=1, source_target_pairs={{0,4},{1,5},{2,6},{3,7},{4,0},{5,1},{6,2},{7,3},{8,12},{9,13},{10,... | collective-permute-start | bytes 393224 | tf_op jit(solution)/shard_map/ppermute | solution.py:514
  75.9 2.9 %collective-permute-done.7 = f32[4,64,128]{2,1,0:T(8,128)S(1)} collective-permute-done((f32[4,64,128]{2,1,0:T(8,128)S(1)}, f32[4,64,128]{2,1,0:T(8,128)S(1)}, u32[]{:S(2)}, u32[]{:S(2)}) %collective-permute-start.7) | collective-permute-done | bytes 131104 | tf_op jit(solution)/shard_map/ppermute | solution.py:514
  78.9 1.4 %collective-permute-start.8 = (f32[4,64,128]{2,1,0:T(8,128)S(1)}, f32[4,64,128]{2,1,0:T(8,128)S(1)}, u32[]{:S(2)}, u32[]{:S(2)}) collective-permute-start(f32[4,64,128]{2,1,0:T(8,128)S(1)} %add.14), channel_id=1, source_target_pairs={{0,8},{1,9},{2,10},{3,11},{4,12},{5,13},{6,14},{7,15},{8,0},{9,1},... | collective-permute-start | bytes 393224 | tf_op jit(solution)/shard_map/ppermute | solution.py:514
  80.2 4.6 %collective-permute-done.8 = f32[4,64,128]{2,1,0:T(8,128)S(1)} collective-permute-done((f32[4,64,128]{2,1,0:T(8,128)S(1)}, f32[4,64,128]{2,1,0:T(8,128)S(1)}, u32[]{:S(2)}, u32[]{:S(2)}) %collective-permute-start.8) | collective-permute-done | bytes 131104 | tf_op jit(solution)/shard_map/ppermute | solution.py:514
  84.9 1.3 %collective-permute-done.9.other = f32[4,64,128]{2,1,0:T(8,128)S(1)} collective-permute-done((f32[4,64,128]{2,1,0:T(8,128)S(1)}, f32[4,64,128]{2,1,0:T(8,128)S(1)}, u32[]{:S(2)}, u32[]{:S(2)}) %collective-permute-start.9) | collective-permute-done | bytes 131104 | tf_op jit(solution)/shard_map/ppermute | solution.py:516
  86.2 23.4 %chain.1.w_ref = f32[128,128]{1,0:T(8,128)S(1)} custom-call(s32[2]{0:T(128)S(1)} %pad_add_fusion.ids, f32[4,64,128]{2,1,0:T(8,128)S(1)} %add.15.mine, f32[4,64,128]{2,1,0:T(8,128)S(1)} %collective-permute-done.9.other), custom_call_target="tpu_custom_call" | custom-call | tf_op jit(solution)/shard_map/chain/pallas_call | solution.py:427
  109.6 9.5 %apply.1 = f32[64,2,8,2,8,128]{5,4,3,2,1,0:T(8,128)} custom-call(f32[128,128]{1,0:T(8,128)S(1)} %chain.1.w_ref, f32[64,2,32,128]{3,2,1,0:T(8,128)S(1)} %get-tuple-element.29.own0, f32[64,2,32,128]{3,2,1,0:T(8,128)S(1)} %collective-permute-done.10.other0, f32[64,2,32,128]{3,2,1,0:T(8,128)S(1)} %get-tuple-element.33.own1, ...), custom_call_target="tpu_custom_call" | custom-call | tf_op jit(solution)/shard_map/apply/pallas_call | solution.py:475
  (32 shorter events, 1.0 us)
Async XLA Ops:
  0.0 15.9 %copy-start.1 = (f32[2,64,512]{2,1,0:T(8,128)S(1)}, f32[2,64,512]{2,1,0:T(8,128)}, u32[]{:S(2)}) copy-start(f32[2,64,512]{2,1,0:T(8,128)} %param.9) | copy-start | bytes 786436
  0.0 15.9 %copy-start.2 = (f32[2,64,512]{2,1,0:T(8,128)S(1)}, f32[2,64,512]{2,1,0:T(8,128)}, u32[]{:S(2)}) copy-start(f32[2,64,512]{2,1,0:T(8,128)} %param.10) | copy-start | bytes 786436
  0.0 15.9 %copy-start.4 = (s32[8,512]{1,0:T(8,128)S(1)}, s32[8,512]{1,0:T(8,128)}, u32[]{:S(2)}) copy-start(s32[8,512]{1,0:T(8,128)} %cells.3) | copy-start | bytes 49156
  0.0 15.9 %copy-start.5 = (s32[8]{0:T(128)S(1)}, s32[8]{0:T(128)}, u32[]{:S(2)}) copy-start(s32[8]{0:T(128)} %owner.5) | copy-start | bytes 100
  0.0 15.9 %copy-start.6 = (s32[8]{0:T(128)S(1)}, s32[8]{0:T(128)}, u32[]{:S(2)}) copy-start(s32[8]{0:T(128)} %order.5) | copy-start | bytes 100
  2.6 8.3 %collective-permute-start = (f32[4,72,128]{2,1,0:T(8,128)}, f32[4,72,128]{2,1,0:T(8,128)S(1)}, u32[]{:S(2)}, u32[]{:S(2)}) collective-permute-start(f32[4,72,128]{2,1,0:T(8,128)} %get-tuple-element.22), channel_id=1, source_target_pairs={{0,1},{1,2},{2,3},{3,4},{4,5},{5,6},{6,7},{7,8},{8,9},{9,10},{10,1... | collective-permute-start | bytes 442376 | tf_op jit(solution)/shard_map/ppermute | solution.py:499
  7.5 8.4 %collective-permute-start.1 = (f32[4,72,128]{2,1,0:T(8,128)}, f32[4,72,128]{2,1,0:T(8,128)S(1)}, u32[]{:S(2)}, u32[]{:S(2)}) collective-permute-start(f32[4,72,128]{2,1,0:T(8,128)} %get-tuple-element.23), channel_id=1, source_target_pairs={{1,0},{2,1},{3,2},{4,3},{5,4},{6,5},{7,6},{8,7},{9,8},{10,9},{11,1... | collective-permute-start | bytes 442376 | tf_op jit(solution)/shard_map/ppermute | solution.py:500
  15.9 3.4 %copy-start = (f32[32,2,64,512]{3,2,1,0:T(8,128)S(1)}, f32[32,2,64,512]{3,2,1,0:T(8,128)}, u32[]{:S(2)}) copy-start(f32[32,2,64,512]{3,2,1,0:T(8,128)} %param.8) | copy-start | bytes 25165828
  19.3 15.9 %copy-start.9 = (f32[4,72,128]{2,1,0:T(8,128)S(1)}, f32[4,72,128]{2,1,0:T(8,128)}, u32[]{:S(2)}) copy-start(f32[4,72,128]{2,1,0:T(8,128)} %get-tuple-element.25) | copy-start | bytes 442372
  19.3 17.2 %copy-start.8 = (f32[4,72,128]{2,1,0:T(8,128)S(1)}, f32[4,72,128]{2,1,0:T(8,128)}, u32[]{:S(2)}) copy-start(f32[4,72,128]{2,1,0:T(8,128)} %get-tuple-element.26) | copy-start | bytes 442372
  19.3 18.5 %copy-start.7 = (f32[8,512]{1,0:T(8,128)S(1)}, f32[8,512]{1,0:T(8,128)}, u32[]{:S(2)}) copy-start(f32[8,512]{1,0:T(8,128)} %param.15) | copy-start | bytes 49156
  19.3 19.1 %copy-start.3 = (f32[8,64,512]{2,1,0:T(8,128)S(1)}, f32[8,64,512]{2,1,0:T(8,128)}, u32[]{:S(2)}) copy-start(f32[8,64,512]{2,1,0:T(8,128)} %observed.1) | copy-start | bytes 3145732
  35.1 3.3 %collective-permute-start.4 = (f32[4,4,32,128]{3,2,1,0:T(8,128)S(1)}, f32[4,4,32,128]{3,2,1,0:T(8,128)S(1)}, u32[]{:S(2)}, u32[]{:S(2)}) collective-permute-start(f32[4,4,32,128]{3,2,1,0:T(8,128)S(1)} %get-tuple-element.27), channel_id=1, source_target_pairs={{0,16},{16,0},{1,17},{17,1},{2,18},{18,2},{3,19},{19,3},{4,20},{20... | collective-permute-start | bytes 786440 | tf_op jit(solution)/shard_map/ppermute | solution.py:503
  35.2 5.3 %collective-permute-start.2 = (f32[4,72,128]{2,1,0:T(8,128)S(1)}, f32[4,72,128]{2,1,0:T(8,128)S(1)}, u32[]{:S(2)}, u32[]{:S(2)}) collective-permute-start(f32[4,72,128]{2,1,0:T(8,128)S(1)} %copy-done.9), channel_id=1, source_target_pairs={{0,1},{1,2},{2,3},{3,4},{4,5},{5,6},{6,7},{7,8},{8,9},{9,10},{10,1... | collective-permute-start | bytes 442376 | tf_op jit(solution)/shard_map/ppermute | solution.py:506
  36.5 8.1 %collective-permute-start.3 = (f32[4,72,128]{2,1,0:T(8,128)S(1)}, f32[4,72,128]{2,1,0:T(8,128)S(1)}, u32[]{:S(2)}, u32[]{:S(2)}) collective-permute-start(f32[4,72,128]{2,1,0:T(8,128)S(1)} %copy-done.8), channel_id=1, source_target_pairs={{1,0},{2,1},{3,2},{4,3},{5,4},{6,5},{7,6},{8,7},{9,8},{10,9},{11,1... | collective-permute-start | bytes 442376 | tf_op jit(solution)/shard_map/ppermute | solution.py:507
  37.8 71.8 %collective-permute-start.10 = (f32[64,2,32,128]{3,2,1,0:T(8,128)S(1)}, f32[64,2,32,128]{3,2,1,0:T(8,128)S(1)}, u32[]{:S(2)}, u32[]{:S(2)}) collective-permute-start(f32[64,2,32,128]{3,2,1,0:T(8,128)S(1)} %get-tuple-element.30), channel_id=1, source_target_pairs={{0,16},{16,0},{1,17},{17,1},{2,18},{18,2},{3,19},{19,3},{4,20},{20... | collective-permute-start | bytes 6291464 | tf_op jit(solution)/shard_map/ppermute | solution.py:510
  55.8 53.8 %collective-permute-start.11 = (f32[64,2,32,128]{3,2,1,0:T(8,128)S(1)}, f32[64,2,32,128]{3,2,1,0:T(8,128)S(1)}, u32[]{:S(2)}, u32[]{:S(2)}) collective-permute-start(f32[64,2,32,128]{3,2,1,0:T(8,128)S(1)} %get-tuple-element.34), channel_id=1, source_target_pairs={{0,16},{16,0},{1,17},{17,1},{2,18},{18,2},{3,19},{19,3},{4,20},{20... | collective-permute-start | bytes 6291464 | tf_op jit(solution)/shard_map/ppermute | solution.py:511
  55.9 5.9 %collective-permute-start.5 = (f32[4,64,128]{2,1,0:T(8,128)S(1)}, f32[4,64,128]{2,1,0:T(8,128)S(1)}, u32[]{:S(2)}, u32[]{:S(2)}) collective-permute-start(f32[4,64,128]{2,1,0:T(8,128)S(1)} %gram.1), channel_id=1, source_target_pairs={{0,1},{1,0},{2,3},{3,2},{4,5},{5,4},{6,7},{7,6},{8,9},{9,8},{10,11... | collective-permute-start | bytes 393224 | tf_op jit(solution)/shard_map/ppermute | solution.py:514
  61.8 6.4 %collective-permute-start.6 = (f32[4,64,128]{2,1,0:T(8,128)S(1)}, f32[4,64,128]{2,1,0:T(8,128)S(1)}, u32[]{:S(2)}, u32[]{:S(2)}) collective-permute-start(f32[4,64,128]{2,1,0:T(8,128)S(1)} %add.12), channel_id=1, source_target_pairs={{0,2},{1,3},{2,0},{3,1},{4,6},{5,7},{6,4},{7,5},{8,10},{9,11},{10,... | collective-permute-start | bytes 393224 | tf_op jit(solution)/shard_map/ppermute | solution.py:514
  68.2 10.6 %collective-permute-start.7 = (f32[4,64,128]{2,1,0:T(8,128)S(1)}, f32[4,64,128]{2,1,0:T(8,128)S(1)}, u32[]{:S(2)}, u32[]{:S(2)}) collective-permute-start(f32[4,64,128]{2,1,0:T(8,128)S(1)} %add.13), channel_id=1, source_target_pairs={{0,4},{1,5},{2,6},{3,7},{4,0},{5,1},{6,2},{7,3},{8,12},{9,13},{10,... | collective-permute-start | bytes 393224 | tf_op jit(solution)/shard_map/ppermute | solution.py:514
  78.9 5.9 %collective-permute-start.8 = (f32[4,64,128]{2,1,0:T(8,128)S(1)}, f32[4,64,128]{2,1,0:T(8,128)S(1)}, u32[]{:S(2)}, u32[]{:S(2)}) collective-permute-start(f32[4,64,128]{2,1,0:T(8,128)S(1)} %add.14), channel_id=1, source_target_pairs={{0,8},{1,9},{2,10},{3,11},{4,12},{5,13},{6,14},{7,15},{8,0},{9,1},... | collective-permute-start | bytes 393224 | tf_op jit(solution)/shard_map/ppermute | solution.py:514
  84.8 1.4 %collective-permute-start.9 = (f32[4,64,128]{2,1,0:T(8,128)S(1)}, f32[4,64,128]{2,1,0:T(8,128)S(1)}, u32[]{:S(2)}, u32[]{:S(2)}) collective-permute-start(f32[4,64,128]{2,1,0:T(8,128)S(1)} %add.15.mine), channel_id=1, source_target_pairs={{0,16},{16,0},{1,17},{17,1},{2,18},{18,2},{3,19},{19,3},{4,20},{20... | collective-permute-start | bytes 393224 | tf_op jit(solution)/shard_map/ppermute | solution.py:516

commit v3 on v2

--- a/solution.py
+++ b/solution.py
@@ -49,58 +49,62 @@
     return back.reshape(*lead, r8 * sub, ct * lanes)
 
 
-def pack_kernel(first, last, flow_first, flow_last, nu_first, nu_last, *outs):
-    members = first.shape[0]
-    fields = first.shape[1]
-    nct = first.shape[3]
-    up, down = outs[:fields], outs[fields:]
+def pack_kernel(state, flow, nu, *rest):
+    fields = state.shape[1]
+    members, _, r8, nct = state.shape[:4]
+    outs, (edge_flow, edge_nu, sems) = rest[: 2 * fields], rest[2 * fields :]
+    sides = ((r8 - 1, (SUB - 2, SUB - 1)), (0, (0, 1)))
+    copies = []
+    for side, (block, rows) in enumerate(sides):
+        copies.append(pltpu.make_async_copy(flow.at[:, block], edge_flow.at[side], sems.at[len(copies)]))
+        copies.append(pltpu.make_async_copy(nu.at[:, block], edge_nu.at[side], sems.at[len(copies)]))
     for field in range(fields):
-        for msg, src, flow, nu, rows, edge in (
-            (up[field], last, flow_last, nu_last, (SUB - 2, SUB - 1), SUB - 1),
-            (down[field], first, flow_first, nu_first, (0, 1), 0),
-        ):
-            flat = src.reshape(members * fields * nct * SUB, LANES)
+        for side, (block, rows) in enumerate(sides):
+            msg = outs[side * fields + field]
             for ct in range(nct):
                 for at, row in enumerate(rows):
-                    start = (field * nct + ct) * SUB + row
-                    msg[ct, pl.ds(at * members, members), :] = flat[
-                        pl.ds(start, members, stride=fields * nct * SUB), :
-                    ]
-                extra = jnp.concatenate(
+                    copies.append(
+                        pltpu.make_async_copy(
+                            state.at[:, field, block, ct, row, :],
+                            msg.at[ct, pl.ds(at * members, members), :],
+                            sems.at[len(copies)],
+                        )
+                    )
+    for copy in copies:
+        copy.start()
+    for copy in copies[:4]:
+        copy.wait()
+    for field in range(fields):
+        for side in range(2):
+            msg = outs[side * fields + field]
+            edge = (SUB - 1, 0)[side]
+            for ct in range(nct):
+                msg[ct, pl.ds(2 * members, PACK), :] = jnp.concatenate(
                     [
-                        flow[0, 0, ct, edge : edge + 1, :],
-                        flow[1, 0, ct, edge : edge + 1, :],
-                        nu[field, 0, ct, edge : edge + 1, :],
+                        edge_flow[side, 0, ct, edge : edge + 1, :],
+                        edge_flow[side, 1, ct, edge : edge + 1, :],
+                        edge_nu[side, field, ct, edge : edge + 1, :],
                         jnp.zeros((PACK - 3, LANES), F32),
                     ],
                     axis=0,
                 )
-                msg[ct, pl.ds(2 * members, PACK), :] = extra
+    for copy in copies[4:]:
+        copy.wait()
 
 
 def pack_edges(state6, flow5, nu5):
     members, fields, r8, nct = state6.shape[:4]
     msg = jax.ShapeDtypeStruct((nct, 2 * members + PACK, LANES), F32)
-    last = r8 - 1
-
-    def state_block(at):
-        return pl.BlockSpec((members, fields, 1, nct, SUB, LANES), lambda i: (0, 0, at, 0, 0, 0))
-
-    def row_block(at):
-        return pl.BlockSpec((2, 1, nct, SUB, LANES), lambda i: (0, at, 0, 0, 0))
-
+    edge = pltpu.VMEM((2, 2, nct, SUB, LANES), F32)
     return pl.pallas_call(
         pack_kernel,
-        grid=(1,),
         out_shape=[msg] * (2 * fields),
-        in_specs=[
-            state_block(0), state_block(last), row_block(0), row_block(last),
-            row_block(0), row_block(last),
-        ],
-        out_specs=[pl.BlockSpec(msg.shape, lambda i: (0, 0, 0))] * (2 * fields),
-        compiler_params=params(60),
+        in_specs=[pl.BlockSpec(memory_space=pltpu.HBM)] * 3,
+        out_specs=[pl.BlockSpec(memory_space=pltpu.VMEM)] * (2 * fields),
+        scratch_shapes=[edge, edge, pltpu.SemaphoreType.DMA((4 + 4 * fields * nct,))],
+        compiler_params=params(56),
         name="pack_edges",
-    )(state6, state6, flow5, flow5, nu5, nu5)
+    )(state6, flow5, nu5)
 
 
 def stencil_coefs(flow_x, flow_y, nu, col, width):
@@ -119,8 +123,7 @@
     lane = lax.broadcasted_iota(jnp.int32, (SUB, LANES), 1)
     first, last = lane == 0, lane == LANES - 1
     weights = [
-        [jnp.broadcast_to(coef[k, ct, pl.ds(row, 1), :], (SUB, LANES)) for k in range(5)]
-        for ct in range(nct)
+        [jnp.broadcast_to(coef(k, ct, row), (SUB, LANES)) for k in range(5)] for ct in range(nct)
     ]
     for group in range(members // SUB):
         rows = pl.ds(group * SUB, SUB)
@@ -140,77 +143,137 @@
             dst(ct, rows, value)
 
 
-def forecast_kernel(
-    gather, ids, cells, owner, order, state, flow, nu, before, after, *rest
+def forecast_rows(lo, hi, field, member, state, flow, nu, before, after, q0, q1, coef, put):
+    members, fields, r8, nct = state.shape[:4]
+    rows = r8 * SUB
+    half = nct // 2
+    width = nct * LANES
+    flat = state.reshape(members * fields * r8 * nct * SUB, LANES)
+    stride = fields * r8 * nct * SUB
+
+    def phys(ct):
+        return lax.rem(ct + member * half, nct)
+
+    first = max(lo - 1, 0) // SUB
+    count = min(hi, rows - 1) // SUB + 1 - first
+    base = first * SUB - SUB
+    for ct in range(nct):
+        at = phys(ct)
+        col = lax.broadcasted_iota(jnp.int32, (count * SUB, LANES), 1) + at * LANES
+        block = pl.ds(first, count)
+        flow_x = flow[0, block, at, :, :].reshape(count * SUB, LANES)
+        flow_y = flow[1, block, at, :, :].reshape(count * SUB, LANES)
+        diffuse = nu[field, block, at, :, :].reshape(count * SUB, LANES)
+        for k, value in enumerate(stencil_coefs(flow_x, flow_y, diffuse, col, width)):
+            coef[k, ct, pl.ds(SUB, count * SUB), :] = value
+        for msg, row, needed in ((before, -1, lo == 0), (after, rows, hi == rows)):
+            if needed:
+                edge = [msg[at, pl.ds(2 * members + k, 1), :] for k in range(3)]
+                for k, value in enumerate(stencil_coefs(*edge, col[0:1], width)):
+                    coef[k, ct, pl.ds(row - base, 1), :] = value
+        if lo == 0:
+            for k in range(2):
+                q0[k, ct] = before[at, pl.ds(k * members, members), :]
+        if hi == rows:
+            for k in range(2):
+                q0[rows - lo + 2 + k, ct] = after[at, pl.ds(k * members, members), :]
+
+    start = max(lo - 2, 0)
+    stop = min(hi + 2, rows)
+
+    def load(i):
+        r = start + i
+        for ct in range(nct):
+            at = (lax.div(r, SUB) * nct + phys(ct)) * SUB + lax.rem(r, SUB) + field * r8 * nct * SUB
+            q0[r - lo + 2, ct] = flat[pl.ds(at, members, stride=stride), :]
+
+    rows_loop(stop - start, 8, load)
+
+    def first_step(i):
+        def keep(ct, at, value):
+            q1[i, ct, at, :] = value
+
+        stencil_row(
+            q0, i, keep, lambda k, ct, r: coef[k, ct, pl.ds(r + (lo - 1 - base), 1), :], members
+        )
+
+    rows_loop(hi - lo + 2, 6, first_step)
+
+    def second_step(i):
+        def keep(ct, at, value):
+            put(lo + i, ct, at, value)
+
+        stencil_row(
+            q1, i, keep, lambda k, ct, r: coef[k, ct, pl.ds(r + (lo - base), 1), :], members
+        )
+
+    rows_loop(hi - lo, 4, second_step)
+
+
+def row_scratch(count, nct, members):
+    return [
+        pltpu.VMEM((count + 4, nct, members, LANES), F32),
+        pltpu.VMEM((count + 2, nct, members, LANES), F32),
+        pltpu.VMEM((5, nct, -(-count // SUB) * SUB + 4 * SUB, LANES), F32),
+    ]
+
+
+def cost(count, nct, members):
+    cells = count * nct * members * LANES
+    return pl.CostEstimate(flops=40 * cells, bytes_accessed=8 * cells, transcendentals=0)
+
+
+SMEM = pl.BlockSpec(memory_space=pltpu.SMEM)
+VMEM = pl.BlockSpec(memory_space=pltpu.VMEM)
+
+
+def inner_kernel(lo, hi, ids, state, flow, nu, full, send, *scratch):
+    half = full.shape[1] // 2
+
+    def put(r, ct, at, value):
+        full[r, ct, at, :] = value
+        if ct >= half:
+            send[r, ct - half, at, :] = value
+
+    forecast_rows(lo, hi, 0, ids[1], state, flow, nu, None, None, *scratch, put)
+
+
+def forecast_inner(ids, state6, flow5, nu5):
+    members, _, r8, nct = state6.shape[:4]
+    rows = r8 * SUB
+    return pl.pallas_call(
+        functools.partial(inner_kernel, 2, rows - 2),
+        out_shape=[
+            jax.ShapeDtypeStruct((rows, nct, members, LANES), F32),
+            jax.ShapeDtypeStruct((rows, nct // 2, members, LANES), F32),
+        ],
+        in_specs=[SMEM] + [VMEM] * 3,
+        out_specs=[VMEM] * 2,
+        scratch_shapes=row_scratch(rows - 4, nct, members),
+        compiler_params=params(16),
+        cost_estimate=cost(rows, nct, members),
+        name="forecast_inner",
+    )(ids, state6, flow5, nu5)
+
+
+def edge_kernel(
+    ids, cells, owner, order, state, flow, nu, before, after, full_in, send_in,
+    full, send, keep, away, *scratch
 ):
-    if gather:
-        own, send, keep, away, q0, q1, coef = rest
-    else:
-        own, send, q0, q1, coef = rest
     members, _, r8, nct = state.shape[:4]
     rows = r8 * SUB
     half = nct // 2
     width = nct * LANES
     slab, member = ids[0], ids[1]
-    flat = state.reshape(members * r8 * nct * SUB, LANES)
-
-    def phys(ct):
-        return lax.rem(ct + member * half, nct)
-
-    for ct in range(nct):
-        at = phys(ct)
-        col = lax.broadcasted_iota(jnp.int32, (rows, LANES), 1) + at * LANES
-        flow_x = flow[0, :, at, :, :].reshape(rows, LANES)
-        flow_y = flow[1, :, at, :, :].reshape(rows, LANES)
-        diffuse = nu[0, :, at, :, :].reshape(rows, LANES)
-        for k, value in enumerate(stencil_coefs(flow_x, flow_y, diffuse, col, width)):
-            coef[k, ct, pl.ds(SUB, rows), :] = value
-        for msg, row in ((before, SUB - 1), (after, SUB + rows)):
-            base = 2 * members
-            edge = [msg[at, pl.ds(base + k, 1), :] for k in range(3)]
-            for k, value in enumerate(stencil_coefs(*edge, col[0:1], width)):
-                coef[k, ct, pl.ds(row, 1), :] = value
-
-    for ct in range(nct):
-        at = phys(ct)
-        for k in range(2):
-            q0[k, ct] = before[at, pl.ds(k * members, members), :]
-            q0[rows + 2 + k, ct] = after[at, pl.ds(k * members, members), :]
-
-    def load(block, carry):
-        for sub in range(SUB):
-            for ct in range(nct):
-                start = (block * nct + phys(ct)) * SUB + sub
-                q0[block * SUB + sub + 2, ct] = flat[
-                    pl.ds(start, members, stride=r8 * nct * SUB), :
-                ]
-        return carry
-
-    lax.fori_loop(0, r8, load, 0)
-
-    def first_step(r):
-        def put(ct, at, value):
-            q1[r, ct, at, :] = value
-
-        stencil_row(q0, r, put, coef.at[:, :, pl.ds(SUB - 1, rows + 2)], members)
-
-    rows_loop(rows + 2, 6, first_step)
-
-    def second_step(r):
-        def put(ct, at, value):
-            if ct < half:
-                own[r, ct, at, :] = value
-            else:
-                send[r, ct - half, at, :] = value
-            if gather:
-                q0[r, ct, at, :] = value
-
-        stencil_row(q1, r, put, coef.at[:, :, pl.ds(SUB, rows)], members)
-
-    rows_loop(rows, 4, second_step)
-
-    if not gather:
-        return
+
+    def put(r, ct, at, value):
+        full[r, ct, at, :] = value
+        if ct >= half:
+            send[r, ct - half, at, :] = value
+
+    for lo, hi in ((0, 2), (rows - 2, rows)):
+        forecast_rows(lo, hi, 0, member, state, flow, nu, before, after, *scratch, put)
+
     nobs = cells.shape[1]
     bits = width.bit_length() - 1
     assert width == 1 << bits
@@ -228,7 +291,7 @@
                     r = lax.shift_right_logical(cell, bits)
                     c = cell & (width - 1)
                     at = (lax.shift_right_logical(c, 7) + member * half) & (nct - 1)
-                    moved = pltpu.roll(q0[r, at], (o - c) & (LANES - 1), 1)
+                    moved = pltpu.roll(full[r, at], (o - c) & (LANES - 1), 1)
                     acc = jnp.where(lane == o, moved, acc)
                 return acc
 
@@ -249,46 +312,53 @@
         lax.fori_loop(0, nobs // LANES, pick, 0)
 
 
-def forecast(field, gather, ids, cells, owner, order, state6, flow5, nu5, before, after):
-    members, fields, r8, nct = state6.shape[:4]
+def forecast_edges(ids, cells, owner, order, state6, flow5, nu5, before, after, full, send):
+    members, _, r8, nct = state6.shape[:4]
+    nb, nobs = cells.shape
+    picks = jax.ShapeDtypeStruct((nb // 2, nobs // LANES, members, LANES), F32)
+    return pl.pallas_call(
+        edge_kernel,
+        out_shape=[
+            jax.ShapeDtypeStruct(full.shape, F32), jax.ShapeDtypeStruct(send.shape, F32), picks, picks,
+        ],
+        in_specs=[SMEM] * 4 + [VMEM] * 7,
+        out_specs=[VMEM] * 4,
+        input_output_aliases={9: 0, 10: 1},
+        scratch_shapes=row_scratch(2, nct, members),
+        compiler_params=params(8),
+        cost_estimate=cost(SUB, nct, members),
+        name="forecast_edges",
+    )(ids, cells, owner, order, state6, flow5, nu5, before, after, full, send)
+
+
+def piece_kernel(lo, hi, ids, state, flow, nu, before, after, *rest):
+    own, send, *scratch = rest[-5:]
+    half = own.shape[1]
+
+    def put(r, ct, at, value):
+        if ct < half:
+            own[r, ct, at, :] = value
+        else:
+            send[r, ct - half, at, :] = value
+
+    forecast_rows(lo, hi, 1, ids[1], state, flow, nu, before, after, *scratch, put)
+
+
+def forecast_piece(lo, hi, ids, state6, flow5, nu5, before, after, done):
+    members, _, r8, nct = state6.shape[:4]
     rows = r8 * SUB
-    half = nct // 2
-    part = jax.ShapeDtypeStruct((rows, half, members, LANES), F32)
-    out_shape = [part, part]
-    if gather:
-        nb, nobs = cells.shape
-        picks = jax.ShapeDtypeStruct((nb // 2, nobs // LANES, members, LANES), F32)
-        out_shape += [picks, picks]
-    msg = pl.BlockSpec(before.shape, lambda i, *s: (0, 0, 0))
-    cells_n = rows * nct * members * LANES
+    part = jax.ShapeDtypeStruct((rows, nct // 2, members, LANES), F32)
     return pl.pallas_call(
-        functools.partial(forecast_kernel, gather),
-        out_shape=out_shape,
-        grid_spec=pltpu.PrefetchScalarGridSpec(
-            num_scalar_prefetch=4,
-            grid=(1,),
-            in_specs=[
-                pl.BlockSpec((members, 1, r8, nct, SUB, LANES), lambda i, *s: (0, field, 0, 0, 0, 0)),
-                pl.BlockSpec((2, r8, nct, SUB, LANES), lambda i, *s: (0, 0, 0, 0, 0)),
-                pl.BlockSpec((1, r8, nct, SUB, LANES), lambda i, *s: (field, 0, 0, 0, 0)),
-                msg,
-                msg,
-            ],
-            out_specs=[
-                pl.BlockSpec(o.shape, lambda i, *s: (0, 0, 0, 0)) for o in out_shape
-            ],
-            scratch_shapes=[
-                pltpu.VMEM((rows + 4, nct, members, LANES), F32),
-                pltpu.VMEM((rows + 2, nct, members, LANES), F32),
-                pltpu.VMEM((5, nct, rows + 2 * SUB, LANES), F32),
-            ],
-        ),
-        compiler_params=params(32),
-        cost_estimate=pl.CostEstimate(
-            flops=40 * cells_n, bytes_accessed=8 * cells_n, transcendentals=0
-        ),
-        name="forecast_gather" if gather else "forecast",
-    )(ids, cells, owner, order, state6, flow5, nu5, before, after)
+        functools.partial(piece_kernel, lo, hi),
+        out_shape=[part, part],
+        in_specs=[SMEM] + [VMEM] * (5 + len(done)),
+        out_specs=[VMEM] * 2,
+        input_output_aliases={6: 0, 7: 1} if done else {},
+        scratch_shapes=row_scratch(hi - lo, nct, members),
+        compiler_params=params(10),
+        cost_estimate=cost(hi - lo, nct, members),
+        name=f"forecast_rows_{lo}",
+    )(ids, state6, flow5, nu5, before, after, *done)
 
 
 def gram_kernel(ids, owner, order, keep, other, observed, variance, out):
@@ -356,15 +426,20 @@
     for p in range(groups):
         cols = [[column(a[g], p * SUB + k) for k in range(SUB)] for g in range(groups)]
         c, pa, pb = cols[p], a[p], b[p]
-        for k in range(SUB):
-            here = sub == k
-            scale = 1.0 / row(c[k], k)
-            for j in range(k + 1, SUB):
-                t = row(c[j], k) * scale
-                c[j] = jnp.where(here, t, c[j] - c[k] * t)
-            ra, rb = row(pa, k) * scale, row(pb, k) * scale
-            pa = jnp.where(here, ra, pa - c[k] * ra)
-            pb = jnp.where(here, rb, pb - c[k] * rb)
+        for k in range(0, SUB, 2):
+            ck, cl = c[k], c[k + 1]
+            kk, kl, lk, ll = row(ck, k), row(cl, k), row(ck, k + 1), row(cl, k + 1)
+            scale = 1.0 / (kk * ll - kl * lk)
+
+            def eliminate(x, k=k, ck=ck, cl=cl, kk=kk, kl=kl, lk=lk, ll=ll, scale=scale):
+                u, w = row(x, k), row(x, k + 1)
+                n0, n1 = ll * u - kl * w, kk * w - lk * u
+                rest = x - scale * (ck * n0 + cl * n1)
+                return jnp.where(sub == k, scale * n0, jnp.where(sub == k + 1, scale * n1, rest))
+
+            for j in range(k + 2, SUB):
+                c[j] = eliminate(c[j])
+            pa, pb = eliminate(pa), eliminate(pb)
         a[p], b[p] = pa, pb
         ra = [row(pa, k) for k in range(SUB)]
         rb = [row(pb, k) for k in range(SUB)]
@@ -466,7 +541,7 @@
 
 
 def apply(weights, own0, other0, own1, other1):
-    rows, half, members, _ = own0.shape
+    rows, half, members, _ = other0.shape
     size = 2 * members
     r8 = rows // SUB
     block = (SUB, half, members, LANES)
@@ -498,24 +573,38 @@
     up0, up1, down0, down1 = pack_edges(state6, flow5, nu5)
     before0 = lax.ppermute(up0, "space", up)
     after0 = lax.ppermute(down0, "space", down)
-    scalars = (ids, obs_cells, obs_owner, batch_order)
-    own0, send0, keep, away = forecast(0, True, *scalars, state6, flow5, nu5, before0, after0)
+    full0, send0 = forecast_inner(ids, state6, flow5, nu5)
+    full0, send0, keep, away = forecast_edges(
+        ids, obs_cells, obs_owner, batch_order, state6, flow5, nu5, before0, after0, full0, send0
+    )
     other = lax.ppermute(away, "member", swap)
-    gh = gram(ids, obs_owner, batch_order, keep, other, obs_values, obs_error)
-    up1, down1, _ = lax.optimization_barrier((up1, down1, keep))
+    up1, down1, keep = lax.optimization_barrier((up1, down1, keep))
     before1 = lax.ppermute(up1, "space", up)
     after1 = lax.ppermute(down1, "space", down)
-    before1, after1, gh = lax.optimization_barrier((before1, after1, gh))
-    own1, send1 = forecast(1, False, *scalars, state6, flow5, nu5, before1, after1)
+    gh = gram(ids, obs_owner, batch_order, keep, other, obs_values, obs_error)
+    send0, gh = lax.optimization_barrier((send0, gh))
     other0 = lax.ppermute(send0, "member", swap)
-    other1 = lax.ppermute(send1, "member", swap)
+
+    rows = state.shape[2]
+    pieces = [(r, r + rows // 4) for r in range(0, rows, rows // 4)]
+    pieces = pieces[1:] + pieces[:1]
+    field1 = ()
     bit = 1
     while bit < space:
-        gh = gh + lax.ppermute(gh, "space", [(i, i ^ bit) for i in range(space)])
+        received = lax.ppermute(gh, "space", [(i, i ^ bit) for i in range(space)])
+        if pieces:
+            before1, after1, gh = lax.optimization_barrier((before1, after1, gh))
+            field1 = forecast_piece(*pieces.pop(0), ids, state6, flow5, nu5, before1, after1, field1)
+            received, *field1 = lax.optimization_barrier((received, *field1))
+        gh = gh + received
         bit *= 2
+    for piece in pieces:
+        field1 = forecast_piece(*piece, ids, state6, flow5, nu5, before1, after1, field1)
+    own1, send1 = field1
     theirs = lax.ppermute(gh, "member", swap)
+    other1 = lax.ppermute(send1, "member", swap)
     weights = chain(ids, gh, theirs)
-    return untiled(apply(weights, own0, other0, own1, other1))
+    return untiled(apply(weights, full0, other0, own1, other1))
 
 
 def solution(mesh):

time: 119 us -> 104 us (0.87)
  waiting for transfers between devices: 28.9 us -> 9 us
  starting transfers between devices: 22.8 us -> 27.9 us
  Pallas kernels: 63.7 us -> 62.4 us
    ppermute x4, waiting for transfers between devices: 15.6 us -> 0.31 us  [body(): received = lax.ppermute(gh, 'space', [(i, i ^ bit) for i in range(space)])]
    ppermute x1, waiting for transfers between devices: 5 us -> 0.01 us  [body(): after0 = lax.ppermute(down0, 'space', down)]
    ppermute x1, starting transfers between devices: 1.3 us -> 4.55 us  [body(): before1 = lax.ppermute(up1, 'space', up)]
    pallas_call x1, Pallas kernels: 23.4 us -> 20.4 us  [chain(): pl.pallas_call(chain_kernel, out_shape=jax.ShapeDtypeStruct((2 * size, 2...]
    ppermute x1, waiting for transfers between devices: 1.33 us -> 3.78 us  [body(): theirs = lax.ppermute(gh, 'member', swap)]
    pallas_call x3 -> x7, Pallas kernels: 29.5 us -> 31.6 us  [the longest x4 14.3 us: forecast_piece(): pl.pallas_call(functools.partial(piece_kernel, lo, hi), out_shape=[part,...]
    ppermute x1, waiting for transfers between devices: 2.02 us -> 0.01 us  [body(): before0 = lax.ppermute(up0, 'space', up)]
    ppermute x4, starting transfers between devices: 13.3 us -> 15.2 us  [body(): received = lax.ppermute(gh, 'space', [(i, i ^ bit) for i in range(space)])]
  transfers between devices with their start and end apart: 12 -> 12, of which waited for: 9 -> 4; matrix products, arithmetic and copies ran while one was open for 0% -> 0% of each run, Pallas kernels for 30% -> 47%
where the time goes in v3:
time: 104 us; the launch traced here: 103 us
  Pallas kernels  62.4 us (60%)
  starting transfers between devices  27.9 us (27%)
  waiting for transfers between devices  9 us (9%)
  local copies, waits for them, and re-layouts  3.44 us (3%)
    pallas_call x1, Pallas kernels, chain(): pl.pallas_call(chain_kernel, out_shape=jax.ShapeDtypeStruct((2 * size, 2...  20.4 us
    ppermute x4, starting transfers between devices, body(): received = lax.ppermute(gh, 'space', [(i, i ^ bit) for i in range(space)])  15.2 us
    pallas_call x4, Pallas kernels, forecast_piece(): pl.pallas_call(functools.partial(piece_kernel, lo, hi), out_shape=[part,...  14.3 us
    pallas_call x1, Pallas kernels, forecast_inner(): pl.pallas_call(functools.partial(inner_kernel, 2, rows - 2), out_shape=[j...  12.6 us
    pallas_call x1, Pallas kernels, apply(): pl.pallas_call(apply_kernel, grid=(2, r8), out_shape=jax.ShapeDtypeStruct...  9.62 us
    ppermute x1, waiting for transfers between devices, body(): after1 = lax.ppermute(down1, 'space', down)  4.9 us
    ppermute x1, starting transfers between devices, body(): before0 = lax.ppermute(up0, 'space', up)  4.85 us
    ppermute x1, starting transfers between devices, body(): before1 = lax.ppermute(up1, 'space', up)  4.55 us
  transfers between devices with their start and end apart: 12, of which 4 were waited for; matrix products, arithmetic and copies ran while one was open for 0% of the time, Pallas kernels for 47%

profile of v3, /device:TPU:0, one launch (start us, length us, event | category | flops | bytes accessed | tf_op | source)
XLA Modules:
  0.0 103.2 jit_solution(18150860024109732497)
XLA Ops:
  0.0 2.2 %pack_edges.1 = (f32[4,72,128]{2,1,0:T(8,128)}, f32[4,72,128]{2,1,0:T(8,128)}, f32[4,72,128]{2,1,0:T(8,128)}, f32[4,72,128]{2,1,0:T(8,128)}) custom-call(f32[32,2,8,4,8,128]{5,4,3,2,1,0:T(8,128)} %bitcast.14, f32[2,8,4,8,128]{4,3,2,1,0:T(8,128)} %bitcast.21, f32[2,8,4,8,128]{4,3,2,1,0:T(8,128)} %bitcast.28), custom_call_target="tpu_custom_call" | custom-call | tf_op jit(solution)/shard_map/pack_edges/pallas_call | solution.py:99
  2.2 4.9 %collective-permute-start = (f32[4,72,128]{2,1,0:T(8,128)}, f32[4,72,128]{2,1,0:T(8,128)S(1)}, u32[]{:S(2)}, u32[]{:S(2)}) collective-permute-start(f32[4,72,128]{2,1,0:T(8,128)} %get-tuple-element.54), channel_id=1, source_target_pairs={{0,1},{1,2},{2,3},{3,4},{4,5},{5,6},{6,7},{7,8},{8,9},{9,10},{10,1... | collective-permute-start | bytes 442376 | tf_op jit(solution)/shard_map/ppermute | solution.py:574
  7.1 1.3 %collective-permute-start.1 = (f32[4,72,128]{2,1,0:T(8,128)}, f32[4,72,128]{2,1,0:T(8,128)S(1)}, u32[]{:S(2)}, u32[]{:S(2)}) collective-permute-start(f32[4,72,128]{2,1,0:T(8,128)} %get-tuple-element.55), channel_id=1, source_target_pairs={{1,0},{2,1},{3,2},{4,3},{5,4},{6,5},{7,6},{8,7},{9,8},{10,9},{11,1... | collective-permute-start | bytes 442376 | tf_op jit(solution)/shard_map/ppermute | solution.py:575
  8.5 3.4 %copy-done = f32[32,2,64,512]{3,2,1,0:T(8,128)S(1)} copy-done((f32[32,2,64,512]{3,2,1,0:T(8,128)S(1)}, f32[32,2,64,512]{3,2,1,0:T(8,128)}, u32[]{:S(2)}) %copy-start) | copy-done | bytes 8388632
  11.9 12.6 %forecast_inner.1 = (f32[64,4,32,128]{3,2,1,0:T(8,128)S(1)}, f32[64,2,32,128]{3,2,1,0:T(8,128)S(1)}) custom-call(s32[2]{0:T(128)S(1)} %pad_add_fusion.ids, f32[32,2,8,4,8,128]{5,4,3,2,1,0:T(8,128)S(1)} %bitcast.15, f32[2,8,4,8,128]{4,3,2,1,0:T(8,128)S(1)} %bitcast.22, f32[2,8,4,8,128]{4,3,2,1,0:T(8,128)S(1)} %bitcast.29), custom_call_target="tpu_custom_call" | custom-call | flops 41943040 | bytes 8388608 | tf_op jit(solution)/shard_map/forecast_inner/pallas_call | solution.py:244
  24.6 2.4 %forecast_edges.1 = (f32[64,4,32,128]{3,2,1,0:T(8,128)S(1)}, f32[64,2,32,128]{3,2,1,0:T(8,128)S(1)}, f32[4,4,32,128]{3,2,1,0:T(8,128)S(1)}, f32[4,4,32,128]{3,2,1,0:T(8,128)S(1)}) custom-call(s32[2]{0:T(128)S(1)} %pad_add_fusion.ids, s32[8,512]{1,0:T(8,128)S(1)} %copy-done.5, s32[8]{0:T(128)S(1)} %copy-done.6, ...), custom_call_target="tpu_custom_call", output_to_operand_aliasing={{0}: (9, {}), {1}: (10, {})} | custom-call | flops 5242880 | bytes 1048576 | tf_op jit(solution)/shard_map/forecast_edges/pallas_call | solution.py:319
  27.1 4.6 %collective-permute-start.2 = (f32[4,72,128]{2,1,0:T(8,128)S(1)}, f32[4,72,128]{2,1,0:T(8,128)S(1)}, u32[]{:S(2)}, u32[]{:S(2)}) collective-permute-start(f32[4,72,128]{2,1,0:T(8,128)S(1)} %copy-done.10), channel_id=1, source_target_pairs={{0,1},{1,2},{2,3},{3,4},{4,5},{5,6},{6,7},{7,8},{8,9},{9,10},{10,1... | collective-permute-start | bytes 442376 | tf_op jit(solution)/shard_map/ppermute | solution.py:582
  31.7 1.3 %collective-permute-start.3 = (f32[4,72,128]{2,1,0:T(8,128)S(1)}, f32[4,72,128]{2,1,0:T(8,128)S(1)}, u32[]{:S(2)}, u32[]{:S(2)}) collective-permute-start(f32[4,72,128]{2,1,0:T(8,128)S(1)} %copy-done.9), channel_id=1, source_target_pairs={{1,0},{2,1},{3,2},{4,3},{5,4},{6,5},{7,6},{8,7},{9,8},{10,9},{11,1... | collective-permute-start | bytes 442376 | tf_op jit(solution)/shard_map/ppermute | solution.py:583
  33.1 0.8 gram.1
  33.9 3.1 %collective-permute-start.5 = (f32[4,64,128]{2,1,0:T(8,128)S(1)}, f32[4,64,128]{2,1,0:T(8,128)S(1)}, u32[]{:S(2)}, u32[]{:S(2)}) collective-permute-start(f32[4,64,128]{2,1,0:T(8,128)S(1)} %gram.1), channel_id=1, source_target_pairs={{0,1},{1,0},{2,3},{3,2},{4,5},{5,4},{6,7},{7,6},{8,9},{9,8},{10,11... | collective-permute-start | bytes 393224 | tf_op jit(solution)/shard_map/ppermute | solution.py:594
  36.9 4.9 %collective-permute-done.3.after = f32[4,72,128]{2,1,0:T(8,128)S(1)} collective-permute-done((f32[4,72,128]{2,1,0:T(8,128)S(1)}, f32[4,72,128]{2,1,0:T(8,128)S(1)}, u32[]{:S(2)}, u32[]{:S(2)}) %collective-permute-start.3) | collective-permute-done | bytes 147488 | tf_op jit(solution)/shard_map/ppermute | solution.py:583
  41.8 3.6 %forecast_rows_16.1 = (f32[64,2,32,128]{3,2,1,0:T(8,128)S(1)}, f32[64,2,32,128]{3,2,1,0:T(8,128)S(1)}) custom-call(s32[2]{0:T(128)S(1)} %pad_add_fusion.ids, f32[32,2,8,4,8,128]{5,4,3,2,1,0:T(8,128)S(1)} %bitcast.17, f32[2,8,4,8,128]{4,3,2,1,0:T(8,128)S(1)} %bitcast.24, f32[2,8,4,8,128]{4,3,2,1,0:T(8,128)S(1)} %bitcast.31, ...), custom_call_target="tpu_custom_call" | custom-call | flops 10485760 | bytes 2097152 | tf_op jit(solution)/shard_map/forecast_rows_16/pallas_call | solution.py:351
  45.5 1.3 %collective-permute-start.6 = (f32[4,64,128]{2,1,0:T(8,128)S(1)}, f32[4,64,128]{2,1,0:T(8,128)S(1)}, u32[]{:S(2)}, u32[]{:S(2)}) collective-permute-start(f32[4,64,128]{2,1,0:T(8,128)S(1)} %add.12), channel_id=1, source_target_pairs={{0,2},{1,3},{2,0},{3,1},{4,6},{5,7},{6,4},{7,5},{8,10},{9,11},{10,... | collective-permute-start | bytes 393224 | tf_op jit(solution)/shard_map/ppermute | solution.py:594
  46.8 3.6 %forecast_rows_32.1 = (f32[64,2,32,128]{3,2,1,0:T(8,128)S(1)}, f32[64,2,32,128]{3,2,1,0:T(8,128)S(1)}) custom-call(s32[2]{0:T(128)S(1)} %pad_add_fusion.ids, f32[32,2,8,4,8,128]{5,4,3,2,1,0:T(8,128)S(1)} %bitcast.18, f32[2,8,4,8,128]{4,3,2,1,0:T(8,128)S(1)} %bitcast.25, ...), custom_call_target="tpu_custom_call", output_to_operand_aliasing={{0}: (6, {}), {1}: (7, {})} | custom-call | flops 10485760 | bytes 2097152 | tf_op jit(solution)/shard_map/forecast_rows_32/pallas_call | solution.py:351
  50.6 5.5 %collective-permute-start.7 = (f32[4,64,128]{2,1,0:T(8,128)S(1)}, f32[4,64,128]{2,1,0:T(8,128)S(1)}, u32[]{:S(2)}, u32[]{:S(2)}) collective-permute-start(f32[4,64,128]{2,1,0:T(8,128)S(1)} %add.13), channel_id=1, source_target_pairs={{0,4},{1,5},{2,6},{3,7},{4,0},{5,1},{6,2},{7,3},{8,12},{9,13},{10,... | collective-permute-start | bytes 393224 | tf_op jit(solution)/shard_map/ppermute | solution.py:594
  56.0 3.5 %forecast_rows_48.1 = (f32[64,2,32,128]{3,2,1,0:T(8,128)S(1)}, f32[64,2,32,128]{3,2,1,0:T(8,128)S(1)}) custom-call(s32[2]{0:T(128)S(1)} %pad_add_fusion.ids, f32[32,2,8,4,8,128]{5,4,3,2,1,0:T(8,128)S(1)} %bitcast.19, f32[2,8,4,8,128]{4,3,2,1,0:T(8,128)S(1)} %bitcast.26, ...), custom_call_target="tpu_custom_call", output_to_operand_aliasing={{0}: (6, {}), {1}: (7, {})} | custom-call | flops 10485760 | bytes 2097152 | tf_op jit(solution)/shard_map/forecast_rows_48/pallas_call | solution.py:351
  59.6 5.4 %collective-permute-start.8 = (f32[4,64,128]{2,1,0:T(8,128)S(1)}, f32[4,64,128]{2,1,0:T(8,128)S(1)}, u32[]{:S(2)}, u32[]{:S(2)}) collective-permute-start(f32[4,64,128]{2,1,0:T(8,128)S(1)} %add.14), channel_id=1, source_target_pairs={{0,8},{1,9},{2,10},{3,11},{4,12},{5,13},{6,14},{7,15},{8,0},{9,1},... | collective-permute-start | bytes 393224 | tf_op jit(solution)/shard_map/ppermute | solution.py:594
  65.0 3.5 %forecast_rows_0.1 = (f32[64,2,32,128]{3,2,1,0:T(8,128)S(1)}, f32[64,2,32,128]{3,2,1,0:T(8,128)S(1)}) custom-call(s32[2]{0:T(128)S(1)} %pad_add_fusion.ids, f32[32,2,8,4,8,128]{5,4,3,2,1,0:T(8,128)S(1)} %bitcast.20, f32[2,8,4,8,128]{4,3,2,1,0:T(8,128)S(1)} %bitcast.27, ...), custom_call_target="tpu_custom_call", output_to_operand_aliasing={{0}: (6, {}), {1}: (7, {})} | custom-call | flops 10485760 | bytes 2097152 | tf_op jit(solution)/shard_map/forecast_rows_0/pallas_call | solution.py:351
  68.5 0.2 collective-permute-done.8
  68.7 0.4 collective-permute-start.11
  69.1 0.2 collective-permute-start.9
  69.3 3.8 %collective-permute-done.9.other = f32[4,64,128]{2,1,0:T(8,128)S(1)} collective-permute-done((f32[4,64,128]{2,1,0:T(8,128)S(1)}, f32[4,64,128]{2,1,0:T(8,128)S(1)}, u32[]{:S(2)}, u32[]{:S(2)}) %collective-permute-start.9) | collective-permute-done | bytes 131104 | tf_op jit(solution)/shard_map/ppermute | solution.py:604
  73.1 20.4 %chain.1.w_ref = f32[128,128]{1,0:T(8,128)S(1)} custom-call(s32[2]{0:T(128)S(1)} %pad_add_fusion.ids, f32[4,64,128]{2,1,0:T(8,128)S(1)} %add.15.mine, f32[4,64,128]{2,1,0:T(8,128)S(1)} %collective-permute-done.9.other), custom_call_target="tpu_custom_call" | custom-call | tf_op jit(solution)/shard_map/chain/pallas_call | solution.py:502
  93.5 9.6 %apply.1 = f32[64,2,8,2,8,128]{5,4,3,2,1,0:T(8,128)} custom-call(f32[128,128]{1,0:T(8,128)S(1)} %chain.1.w_ref, f32[64,4,32,128]{3,2,1,0:T(8,128)S(1)} %get-tuple-element.95.own0, f32[64,2,32,128]{3,2,1,0:T(8,128)S(1)} %collective-permute-done.10.other0, f32[64,2,32,128]{3,2,1,0:T(8,128)S(1)} %get-tuple-element.97.own1, ...), custom_call_target="tpu_custom_call" | custom-call | tf_op jit(solution)/shard_map/apply/pallas_call | solution.py:550
  (38 shorter events, 0.4 us)
Async XLA Ops:
  0.0 8.5 %copy-start.2 = (f32[2,64,512]{2,1,0:T(8,128)S(1)}, f32[2,64,512]{2,1,0:T(8,128)}, u32[]{:S(2)}) copy-start(f32[2,64,512]{2,1,0:T(8,128)} %param.9) | copy-start | bytes 786436
  0.0 8.5 %copy-start.3 = (f32[2,64,512]{2,1,0:T(8,128)S(1)}, f32[2,64,512]{2,1,0:T(8,128)}, u32[]{:S(2)}) copy-start(f32[2,64,512]{2,1,0:T(8,128)} %param.10) | copy-start | bytes 786436
  2.2 22.3 %collective-permute-start = (f32[4,72,128]{2,1,0:T(8,128)}, f32[4,72,128]{2,1,0:T(8,128)S(1)}, u32[]{:S(2)}, u32[]{:S(2)}) collective-permute-start(f32[4,72,128]{2,1,0:T(8,128)} %get-tuple-element.54), channel_id=1, source_target_pairs={{0,1},{1,2},{2,3},{3,4},{4,5},{5,6},{6,7},{7,8},{8,9},{9,10},{10,1... | collective-permute-start | bytes 442376 | tf_op jit(solution)/shard_map/ppermute | solution.py:574
  7.1 17.4 %collective-permute-start.1 = (f32[4,72,128]{2,1,0:T(8,128)}, f32[4,72,128]{2,1,0:T(8,128)S(1)}, u32[]{:S(2)}, u32[]{:S(2)}) collective-permute-start(f32[4,72,128]{2,1,0:T(8,128)} %get-tuple-element.55), channel_id=1, source_target_pairs={{1,0},{2,1},{3,2},{4,3},{5,4},{6,5},{7,6},{8,7},{9,8},{10,9},{11,1... | collective-permute-start | bytes 442376 | tf_op jit(solution)/shard_map/ppermute | solution.py:575
  8.5 3.4 %copy-start = (f32[32,2,64,512]{3,2,1,0:T(8,128)S(1)}, f32[32,2,64,512]{3,2,1,0:T(8,128)}, u32[]{:S(2)}) copy-start(f32[32,2,64,512]{3,2,1,0:T(8,128)} %param.8) | copy-start | bytes 25165828
  11.9 12.7 %copy-start.1 = (f32[32,2,64,512]{3,2,1,0:T(8,128)S(1)}, f32[32,2,64,512]{3,2,1,0:T(8,128)}, u32[]{:S(2)}) copy-start(f32[32,2,64,512]{3,2,1,0:T(8,128)} %param.8) | copy-start | bytes 25165828
  11.9 12.7 %copy-start.5 = (s32[8,512]{1,0:T(8,128)S(1)}, s32[8,512]{1,0:T(8,128)}, u32[]{:S(2)}) copy-start(s32[8,512]{1,0:T(8,128)} %cells.1) | copy-start | bytes 49156
  11.9 12.7 %copy-start.6 = (s32[8]{0:T(128)S(1)}, s32[8]{0:T(128)}, u32[]{:S(2)}) copy-start(s32[8]{0:T(128)} %owner.3) | copy-start | bytes 100
  11.9 12.7 %copy-start.7 = (s32[8]{0:T(128)S(1)}, s32[8]{0:T(128)}, u32[]{:S(2)}) copy-start(s32[8]{0:T(128)} %order.3) | copy-start | bytes 100
  24.6 2.6 %copy-start.10 = (f32[4,72,128]{2,1,0:T(8,128)S(1)}, f32[4,72,128]{2,1,0:T(8,128)}, u32[]{:S(2)}) copy-start(f32[4,72,128]{2,1,0:T(8,128)} %get-tuple-element.59) | copy-start | bytes 442372
  24.6 7.1 %copy-start.9 = (f32[4,72,128]{2,1,0:T(8,128)S(1)}, f32[4,72,128]{2,1,0:T(8,128)}, u32[]{:S(2)}) copy-start(f32[4,72,128]{2,1,0:T(8,128)} %get-tuple-element.60) | copy-start | bytes 442372
  24.6 8.4 %copy-start.8 = (f32[8,512]{1,0:T(8,128)S(1)}, f32[8,512]{1,0:T(8,128)}, u32[]{:S(2)}) copy-start(f32[8,512]{1,0:T(8,128)} %param.15) | copy-start | bytes 49156
  24.6 8.5 %copy-start.4 = (f32[8,64,512]{2,1,0:T(8,128)S(1)}, f32[8,64,512]{2,1,0:T(8,128)}, u32[]{:S(2)}) copy-start(f32[8,64,512]{2,1,0:T(8,128)} %observed.1) | copy-start | bytes 3145732
  27.0 6.0 %collective-permute-start.4 = (f32[4,4,32,128]{3,2,1,0:T(8,128)S(1)}, f32[4,4,32,128]{3,2,1,0:T(8,128)S(1)}, u32[]{:S(2)}, u32[]{:S(2)}) collective-permute-start(f32[4,4,32,128]{3,2,1,0:T(8,128)S(1)} %get-tuple-element.63), channel_id=1, source_target_pairs={{0,16},{16,0},{1,17},{17,1},{2,18},{18,2},{3,19},{19,3},{4,20},{20... | collective-permute-start | bytes 786440 | tf_op jit(solution)/shard_map/ppermute | solution.py:580
  27.1 9.8 %collective-permute-start.2 = (f32[4,72,128]{2,1,0:T(8,128)S(1)}, f32[4,72,128]{2,1,0:T(8,128)S(1)}, u32[]{:S(2)}, u32[]{:S(2)}) collective-permute-start(f32[4,72,128]{2,1,0:T(8,128)S(1)} %copy-done.10), channel_id=1, source_target_pairs={{0,1},{1,2},{2,3},{3,4},{4,5},{5,6},{6,7},{7,8},{8,9},{9,10},{10,1... | collective-permute-start | bytes 442376 | tf_op jit(solution)/shard_map/ppermute | solution.py:582
  31.7 10.1 %collective-permute-start.3 = (f32[4,72,128]{2,1,0:T(8,128)S(1)}, f32[4,72,128]{2,1,0:T(8,128)S(1)}, u32[]{:S(2)}, u32[]{:S(2)}) collective-permute-start(f32[4,72,128]{2,1,0:T(8,128)S(1)} %copy-done.9), channel_id=1, source_target_pairs={{1,0},{2,1},{3,2},{4,3},{5,4},{6,5},{7,6},{8,7},{9,8},{10,9},{11,1... | collective-permute-start | bytes 442376 | tf_op jit(solution)/shard_map/ppermute | solution.py:583
  33.9 11.6 %collective-permute-start.5 = (f32[4,64,128]{2,1,0:T(8,128)S(1)}, f32[4,64,128]{2,1,0:T(8,128)S(1)}, u32[]{:S(2)}, u32[]{:S(2)}) collective-permute-start(f32[4,64,128]{2,1,0:T(8,128)S(1)} %gram.1), channel_id=1, source_target_pairs={{0,1},{1,0},{2,3},{3,2},{4,5},{5,4},{6,7},{7,6},{8,9},{9,8},{10,11... | collective-permute-start | bytes 393224 | tf_op jit(solution)/shard_map/ppermute | solution.py:594
  45.5 5.0 %collective-permute-start.6 = (f32[4,64,128]{2,1,0:T(8,128)S(1)}, f32[4,64,128]{2,1,0:T(8,128)S(1)}, u32[]{:S(2)}, u32[]{:S(2)}) collective-permute-start(f32[4,64,128]{2,1,0:T(8,128)S(1)} %add.12), channel_id=1, source_target_pairs={{0,2},{1,3},{2,0},{3,1},{4,6},{5,7},{6,4},{7,5},{8,10},{9,11},{10,... | collective-permute-start | bytes 393224 | tf_op jit(solution)/shard_map/ppermute | solution.py:594
  50.6 9.0 %collective-permute-start.7 = (f32[4,64,128]{2,1,0:T(8,128)S(1)}, f32[4,64,128]{2,1,0:T(8,128)S(1)}, u32[]{:S(2)}, u32[]{:S(2)}) collective-permute-start(f32[4,64,128]{2,1,0:T(8,128)S(1)} %add.13), channel_id=1, source_target_pairs={{0,4},{1,5},{2,6},{3,7},{4,0},{5,1},{6,2},{7,3},{8,12},{9,13},{10,... | collective-permute-start | bytes 393224 | tf_op jit(solution)/shard_map/ppermute | solution.py:594
  59.6 9.1 %collective-permute-start.8 = (f32[4,64,128]{2,1,0:T(8,128)S(1)}, f32[4,64,128]{2,1,0:T(8,128)S(1)}, u32[]{:S(2)}, u32[]{:S(2)}) collective-permute-start(f32[4,64,128]{2,1,0:T(8,128)S(1)} %add.14), channel_id=1, source_target_pairs={{0,8},{1,9},{2,10},{3,11},{4,12},{5,13},{6,14},{7,15},{8,0},{9,1},... | collective-permute-start | bytes 393224 | tf_op jit(solution)/shard_map/ppermute | solution.py:594
  65.0 28.5 %collective-permute-start.10 = (f32[64,2,32,128]{3,2,1,0:T(8,128)S(1)}, f32[64,2,32,128]{3,2,1,0:T(8,128)S(1)}, u32[]{:S(2)}, u32[]{:S(2)}) collective-permute-start(f32[64,2,32,128]{3,2,1,0:T(8,128)S(1)} %get-tuple-element.96), channel_id=1, source_target_pairs={{0,16},{16,0},{1,17},{17,1},{2,18},{18,2},{3,19},{19,3},{4,20},{20... | collective-permute-start | bytes 6291464 | tf_op jit(solution)/shard_map/ppermute | solution.py:586
  68.7 24.8 %collective-permute-start.11 = (f32[64,2,32,128]{3,2,1,0:T(8,128)S(1)}, f32[64,2,32,128]{3,2,1,0:T(8,128)S(1)}, u32[]{:S(2)}, u32[]{:S(2)}) collective-permute-start(f32[64,2,32,128]{3,2,1,0:T(8,128)S(1)} %get-tuple-element.98), channel_id=1, source_target_pairs={{0,16},{16,0},{1,17},{17,1},{2,18},{18,2},{3,19},{19,3},{4,20},{20... | collective-permute-start | bytes 6291464 | tf_op jit(solution)/shard_map/ppermute | solution.py:605
  69.1 4.0 %collective-permute-start.9 = (f32[4,64,128]{2,1,0:T(8,128)S(1)}, f32[4,64,128]{2,1,0:T(8,128)S(1)}, u32[]{:S(2)}, u32[]{:S(2)}) collective-permute-start(f32[4,64,128]{2,1,0:T(8,128)S(1)} %add.15.mine), channel_id=1, source_target_pairs={{0,16},{16,0},{1,17},{17,1},{2,18},{18,2},{3,19},{19,3},{4,20},{20... | collective-permute-start | bytes 393224 | tf_op jit(solution)/shard_map/ppermute | solution.py:604

commit v4 on v3

--- a/solution.py
+++ b/solution.py
@@ -49,58 +49,49 @@
     return back.reshape(*lead, r8 * sub, ct * lanes)
 
 
-def pack_kernel(state, flow, nu, *rest):
-    fields = state.shape[1]
-    members, _, r8, nct = state.shape[:4]
-    outs, (edge_flow, edge_nu, sems) = rest[: 2 * fields], rest[2 * fields :]
-    sides = ((r8 - 1, (SUB - 2, SUB - 1)), (0, (0, 1)))
+def pack_kernel(state, flow, nu, up, down, edge_flow, edge_nu, sems):
+    members, fields, r8, nct = state.shape[:4]
+    sides = ((up, r8 - 1, (SUB - 2, SUB - 1)), (down, 0, (0, 1)))
     copies = []
-    for side, (block, rows) in enumerate(sides):
-        copies.append(pltpu.make_async_copy(flow.at[:, block], edge_flow.at[side], sems.at[len(copies)]))
-        copies.append(pltpu.make_async_copy(nu.at[:, block], edge_nu.at[side], sems.at[len(copies)]))
-    for field in range(fields):
-        for side, (block, rows) in enumerate(sides):
-            msg = outs[side * fields + field]
+
+    def copy(src, dst):
+        copies.append(pltpu.make_async_copy(src, dst, sems.at[len(copies)]))
+
+    for side, (msg, block, rows) in enumerate(sides):
+        copy(flow.at[:, block], edge_flow.at[side])
+        copy(nu.at[:, block], edge_nu.at[side])
+    for msg, block, rows in sides:
+        for field in range(fields):
             for ct in range(nct):
                 for at, row in enumerate(rows):
-                    copies.append(
-                        pltpu.make_async_copy(
-                            state.at[:, field, block, ct, row, :],
-                            msg.at[ct, pl.ds(at * members, members), :],
-                            sems.at[len(copies)],
-                        )
+                    copy(
+                        state.at[:, field, block, ct, row, :],
+                        msg.at[ct, pl.ds((field * 2 + at) * members, members), :],
                     )
-    for copy in copies:
-        copy.start()
-    for copy in copies[:4]:
-        copy.wait()
-    for field in range(fields):
-        for side in range(2):
-            msg = outs[side * fields + field]
-            edge = (SUB - 1, 0)[side]
-            for ct in range(nct):
-                msg[ct, pl.ds(2 * members, PACK), :] = jnp.concatenate(
-                    [
-                        edge_flow[side, 0, ct, edge : edge + 1, :],
-                        edge_flow[side, 1, ct, edge : edge + 1, :],
-                        edge_nu[side, field, ct, edge : edge + 1, :],
-                        jnp.zeros((PACK - 3, LANES), F32),
-                    ],
-                    axis=0,
-                )
-    for copy in copies[4:]:
-        copy.wait()
+    for one in copies:
+        one.start()
+    for one in copies[:4]:
+        one.wait()
+    for side, (msg, block, rows) in enumerate(sides):
+        edge = (SUB - 1, 0)[side]
+        for ct in range(nct):
+            numbers = [edge_flow[side, k, ct, edge : edge + 1, :] for k in range(2)]
+            numbers += [edge_nu[side, k, ct, edge : edge + 1, :] for k in range(fields)]
+            numbers.append(jnp.zeros((PACK - 2 - fields, LANES), F32))
+            msg[ct, pl.ds(2 * fields * members, PACK), :] = jnp.concatenate(numbers, axis=0)
+    for one in copies[4:]:
+        one.wait()
 
 
 def pack_edges(state6, flow5, nu5):
     members, fields, r8, nct = state6.shape[:4]
-    msg = jax.ShapeDtypeStruct((nct, 2 * members + PACK, LANES), F32)
+    msg = jax.ShapeDtypeStruct((nct, 2 * fields * members + PACK, LANES), F32)
     edge = pltpu.VMEM((2, 2, nct, SUB, LANES), F32)
     return pl.pallas_call(
         pack_kernel,
-        out_shape=[msg] * (2 * fields),
-        in_specs=[pl.BlockSpec(memory_space=pltpu.HBM)] * 3,
-        out_specs=[pl.BlockSpec(memory_space=pltpu.VMEM)] * (2 * fields),
+        out_shape=[msg] * 2,
+        in_specs=[pl.BlockSpec(memory_space=pl.ANY)] * 3,
+        out_specs=[pl.BlockSpec(memory_space=pltpu.VMEM)] * 2,
         scratch_shapes=[edge, edge, pltpu.SemaphoreType.DMA((4 + 4 * fields * nct,))],
         compiler_params=params(56),
         name="pack_edges",
@@ -123,7 +114,7 @@
     lane = lax.broadcasted_iota(jnp.int32, (SUB, LANES), 1)
     first, last = lane == 0, lane == LANES - 1
     weights = [
-        [jnp.broadcast_to(coef(k, ct, row), (SUB, LANES)) for k in range(5)] for ct in range(nct)
+        [coef(k, ct, row) for k in range(5)] for ct in range(nct)
     ]
     for group in range(members // SUB):
         rows = pl.ds(group * SUB, SUB)
@@ -143,13 +134,21 @@
             dst(ct, rows, value)
 
 
-def forecast_rows(lo, hi, field, member, state, flow, nu, before, after, q0, q1, coef, put):
+def forecast_rows(
+    lo, hi, field, member, state, flow, nu, before, after, q0, q1, coef, put, wait=None
+):
     members, fields, r8, nct = state.shape[:4]
     rows = r8 * SUB
     half = nct // 2
     width = nct * LANES
     flat = state.reshape(members * fields * r8 * nct * SUB, LANES)
     stride = fields * r8 * nct * SUB
+    offset = min(field, fields - 1) * r8 * nct * SUB
+    room = coef.shape[2]
+    coef_flat = coef.reshape(5 * nct * room, LANES)
+
+    def weight(k, ct, at):
+        return coef_flat[pl.ds((k * nct + ct) * room + at, SUB, stride=0), :]
 
     def phys(ct):
         return lax.rem(ct + member * half, nct)
@@ -168,15 +167,15 @@
             coef[k, ct, pl.ds(SUB, count * SUB), :] = value
         for msg, row, needed in ((before, -1, lo == 0), (after, rows, hi == rows)):
             if needed:
-                edge = [msg[at, pl.ds(2 * members + k, 1), :] for k in range(3)]
+                edge = [msg[at, pl.ds(4 * members + k, 1), :] for k in (0, 1, 2 + field)]
                 for k, value in enumerate(stencil_coefs(*edge, col[0:1], width)):
                     coef[k, ct, pl.ds(row - base, 1), :] = value
         if lo == 0:
             for k in range(2):
-                q0[k, ct] = before[at, pl.ds(k * members, members), :]
+                q0[k, ct] = before[at, pl.ds((2 * field + k) * members, members), :]
         if hi == rows:
             for k in range(2):
-                q0[rows - lo + 2 + k, ct] = after[at, pl.ds(k * members, members), :]
+                q0[rows - lo + 2 + k, ct] = after[at, pl.ds((2 * field + k) * members, members), :]
 
     start = max(lo - 2, 0)
     stop = min(hi + 2, rows)
@@ -184,17 +183,23 @@
     def load(i):
         r = start + i
         for ct in range(nct):
-            at = (lax.div(r, SUB) * nct + phys(ct)) * SUB + lax.rem(r, SUB) + field * r8 * nct * SUB
+            at = (lax.div(r, SUB) * nct + phys(ct)) * SUB + lax.rem(r, SUB) + offset
             q0[r - lo + 2, ct] = flat[pl.ds(at, members, stride=stride), :]
 
-    rows_loop(stop - start, 8, load)
+    if wait is None:
+        rows_loop(stop - start, 8, load)
+    else:
+        for block in range(r8):
+            wait(block)
+            for r in range(max(start, block * SUB), min(stop, block * SUB + SUB)):
+                load(r - start)
 
     def first_step(i):
         def keep(ct, at, value):
             q1[i, ct, at, :] = value
 
         stencil_row(
-            q0, i, keep, lambda k, ct, r: coef[k, ct, pl.ds(r + (lo - 1 - base), 1), :], members
+            q0, i, keep, lambda k, ct, r: weight(k, ct, r + (lo - 1 - base)), members
         )
 
     rows_loop(hi - lo + 2, 6, first_step)
@@ -204,7 +209,7 @@
             put(lo + i, ct, at, value)
 
         stencil_row(
-            q1, i, keep, lambda k, ct, r: coef[k, ct, pl.ds(r + (lo - base), 1), :], members
+            q1, i, keep, lambda k, ct, r: weight(k, ct, r + (lo - base)), members
         )
 
     rows_loop(hi - lo, 4, second_step)
@@ -227,15 +232,24 @@
 VMEM = pl.BlockSpec(memory_space=pltpu.VMEM)
 
 
-def inner_kernel(lo, hi, ids, state, flow, nu, full, send, *scratch):
+def inner_kernel(lo, hi, ids, state, flow, nu, full, send, held, sems, *scratch):
     half = full.shape[1] // 2
+    copies = [
+        pltpu.make_async_copy(state.at[:, 0, block], held.at[:, 0, block], sems.at[block])
+        for block in range(state.shape[2])
+    ]
+    for one in copies:
+        one.start()
 
     def put(r, ct, at, value):
         full[r, ct, at, :] = value
         if ct >= half:
             send[r, ct - half, at, :] = value
 
-    forecast_rows(lo, hi, 0, ids[1], state, flow, nu, None, None, *scratch, put)
+    forecast_rows(
+        lo, hi, 0, ids[1], held, flow, nu, None, None, *scratch, put,
+        wait=lambda block: copies[block].wait(),
+    )
 
 
 def forecast_inner(ids, state6, flow5, nu5):
@@ -247,10 +261,14 @@
             jax.ShapeDtypeStruct((rows, nct, members, LANES), F32),
             jax.ShapeDtypeStruct((rows, nct // 2, members, LANES), F32),
         ],
-        in_specs=[SMEM] + [VMEM] * 3,
+        in_specs=[SMEM, pl.BlockSpec(memory_space=pl.ANY)] + [VMEM] * 2,
         out_specs=[VMEM] * 2,
-        scratch_shapes=row_scratch(rows - 4, nct, members),
-        compiler_params=params(16),
+        scratch_shapes=[
+            pltpu.VMEM((members, 1, r8, nct, SUB, LANES), F32),
+            pltpu.SemaphoreType.DMA((r8,)),
+            *row_scratch(rows - 4, nct, members),
+        ],
+        compiler_params=params(44),
         cost_estimate=cost(rows, nct, members),
         name="forecast_inner",
     )(ids, state6, flow5, nu5)
@@ -570,38 +588,34 @@
     swap = [(0, 1), (1, 0)]
 
     state6, flow5, nu5 = tiled(state), tiled(courant), tiled(diffusion)
-    up0, up1, down0, down1 = pack_edges(state6, flow5, nu5)
-    before0 = lax.ppermute(up0, "space", up)
-    after0 = lax.ppermute(down0, "space", down)
+    up_edge, down_edge = pack_edges(state6, flow5, nu5)
+    before = lax.ppermute(up_edge, "space", up)
+    after = lax.ppermute(down_edge, "space", down)
     full0, send0 = forecast_inner(ids, state6, flow5, nu5)
     full0, send0, keep, away = forecast_edges(
-        ids, obs_cells, obs_owner, batch_order, state6, flow5, nu5, before0, after0, full0, send0
+        ids, obs_cells, obs_owner, batch_order, state6, flow5, nu5, before, after, full0, send0
     )
     other = lax.ppermute(away, "member", swap)
-    up1, down1, keep = lax.optimization_barrier((up1, down1, keep))
-    before1 = lax.ppermute(up1, "space", up)
-    after1 = lax.ppermute(down1, "space", down)
     gh = gram(ids, obs_owner, batch_order, keep, other, obs_values, obs_error)
-    send0, gh = lax.optimization_barrier((send0, gh))
-    other0 = lax.ppermute(send0, "member", swap)
 
     rows = state.shape[2]
     pieces = [(r, r + rows // 4) for r in range(0, rows, rows // 4)]
-    pieces = pieces[1:] + pieces[:1]
     field1 = ()
     bit = 1
     while bit < space:
         received = lax.ppermute(gh, "space", [(i, i ^ bit) for i in range(space)])
         if pieces:
-            before1, after1, gh = lax.optimization_barrier((before1, after1, gh))
-            field1 = forecast_piece(*pieces.pop(0), ids, state6, flow5, nu5, before1, after1, field1)
+            before, after, gh = lax.optimization_barrier((before, after, gh))
+            field1 = forecast_piece(*pieces.pop(0), ids, state6, flow5, nu5, before, after, field1)
             received, *field1 = lax.optimization_barrier((received, *field1))
         gh = gh + received
         bit *= 2
     for piece in pieces:
-        field1 = forecast_piece(*piece, ids, state6, flow5, nu5, before1, after1, field1)
+        field1 = forecast_piece(*piece, ids, state6, flow5, nu5, before, after, field1)
     own1, send1 = field1
     theirs = lax.ppermute(gh, "member", swap)
+    send0, send1, gh = lax.optimization_barrier((send0, send1, gh))
+    other0 = lax.ppermute(send0, "member", swap)
     other1 = lax.ppermute(send1, "member", swap)
     weights = chain(ids, gh, theirs)
     return untiled(apply(weights, full0, other0, own1, other1))

time: 104 us -> 97.2 us (0.935)
  starting transfers between devices: 27.9 us -> 14.5 us
  waiting for transfers between devices: 9 us -> 14.7 us
  Pallas kernels: 62.4 us -> 67.2 us
  local copies, waits for them, and re-layouts: 3.44 us -> 0.05 us
    ppermute x4, starting transfers between devices: 15.2 us -> 7.67 us  [body(): received = lax.ppermute(gh, 'space', [(i, i ^ bit) for i in range(space)])]
    ppermute x4, waiting for transfers between devices: 0.31 us -> 6.48 us  [body(): received = lax.ppermute(gh, 'space', [(i, i ^ bit) for i in range(space)])]
    ppermute x4 -> x2, starting transfers between devices: 12 us -> 6.15 us  [the longest x1 4.86 us: body(): before = lax.ppermute(up_edge, 'space', up)]
    ppermute x4 -> x2, waiting for transfers between devices: 4.9 us -> 0.01 us  [the longest x1 0.01 us: body(): before = lax.ppermute(up_edge, 'space', up)]
    pallas_call x1, Pallas kernels: 2.43 us -> 6.24 us  [forecast_edges(): pl.pallas_call(edge_kernel, out_shape=[jax.ShapeDtypeStruct(full.shape, F...]
    unnamed x22 -> x16, local copies, waits for them, and re-layouts: 3.43 us -> 0.04 us
    ppermute x1, waiting for transfers between devices: 3.78 us -> 6.76 us  [body(): theirs = lax.ppermute(gh, 'member', swap)]
    ppermute x1, waiting for transfers between devices: 0.01 us -> 1.49 us  [body(): other = lax.ppermute(away, 'member', swap)]
  transfers between devices with their start and end apart: 12 -> 10, of which waited for: 4 -> 5; matrix products, arithmetic and copies ran while one was open for 0% -> 0% of each run, Pallas kernels for 47% -> 49%
where the time goes in v4:
time: 97.2 us; the launch traced here: 96.9 us
  Pallas kernels  67.2 us (69%)
  waiting for transfers between devices  14.7 us (15%)
  starting transfers between devices  14.5 us (15%)
    pallas_call x1, Pallas kernels, chain(): pl.pallas_call(chain_kernel, out_shape=jax.ShapeDtypeStruct((2 * size, 2...  20.4 us
    pallas_call x4, Pallas kernels, forecast_piece(): pl.pallas_call(functools.partial(piece_kernel, lo, hi), out_shape=[part,...  14.3 us
    pallas_call x1, Pallas kernels, forecast_inner(): pl.pallas_call(functools.partial(inner_kernel, 2, rows - 2), out_shape=[j...  12.9 us
    pallas_call x1, Pallas kernels, apply(): pl.pallas_call(apply_kernel, grid=(2, r8), out_shape=jax.ShapeDtypeStruct...  9.62 us
    ppermute x4, starting transfers between devices, body(): received = lax.ppermute(gh, 'space', [(i, i ^ bit) for i in range(space)])  7.67 us
    ppermute x1, waiting for transfers between devices, body(): theirs = lax.ppermute(gh, 'member', swap)  6.76 us
    ppermute x4, waiting for transfers between devices, body(): received = lax.ppermute(gh, 'space', [(i, i ^ bit) for i in range(space)])  6.48 us
    pallas_call x1, Pallas kernels, forecast_edges(): pl.pallas_call(edge_kernel, out_shape=[jax.ShapeDtypeStruct(full.shape, F...  6.24 us
  transfers between devices with their start and end apart: 10, of which 5 were waited for; matrix products, arithmetic and copies ran while one was open for 0% of the time, Pallas kernels for 49%

profile of v4, /device:TPU:0, one launch (start us, length us, event | category | flops | bytes accessed | tf_op | source)
XLA Modules:
  0.0 96.9 jit_solution(258317814655918381)
XLA Ops:
  0.0 2.2 %pack_edges.1 = (f32[4,136,128]{2,1,0:T(8,128)}, f32[4,136,128]{2,1,0:T(8,128)}) custom-call(f32[32,2,8,4,8,128]{5,4,3,2,1,0:T(8,128)} %bitcast.14, f32[2,8,4,8,128]{4,3,2,1,0:T(8,128)} %bitcast.21, f32[2,8,4,8,128]{4,3,2,1,0:T(8,128)} %bitcast.28), custom_call_target="tpu_custom_call" | custom-call | tf_op jit(solution)/shard_map/pack_edges/pallas_call | solution.py:90
  2.2 4.9 %collective-permute-start = (f32[4,136,128]{2,1,0:T(8,128)}, f32[4,136,128]{2,1,0:T(8,128)S(1)}, u32[]{:S(2)}, u32[]{:S(2)}) collective-permute-start(f32[4,136,128]{2,1,0:T(8,128)} %get-tuple-element.48), channel_id=1, source_target_pairs={{0,1},{1,2},{2,3},{3,4},{4,5},{5,6},{6,7},{7,8},{8,9},{9,10},{10,1... | collective-permute-start | bytes 835592 | tf_op jit(solution)/shard_map/ppermute | solution.py:592
  7.1 1.3 %collective-permute-start.1 = (f32[4,136,128]{2,1,0:T(8,128)}, f32[4,136,128]{2,1,0:T(8,128)S(1)}, u32[]{:S(2)}, u32[]{:S(2)}) collective-permute-start(f32[4,136,128]{2,1,0:T(8,128)} %get-tuple-element.49), channel_id=1, source_target_pairs={{1,0},{2,1},{3,2},{4,3},{5,4},{6,5},{7,6},{8,7},{9,8},{10,9},{11,1... | collective-permute-start | bytes 835592 | tf_op jit(solution)/shard_map/ppermute | solution.py:593
  8.4 0.1 pad_add_fusion.ids
  8.5 12.9 %forecast_inner.1 = (f32[64,4,32,128]{3,2,1,0:T(8,128)S(1)}, f32[64,2,32,128]{3,2,1,0:T(8,128)S(1)}) custom-call(s32[2]{0:T(128)S(1)} %pad_add_fusion.ids, f32[32,2,8,4,8,128]{5,4,3,2,1,0:T(8,128)} %bitcast.15, f32[2,8,4,8,128]{4,3,2,1,0:T(8,128)S(1)} %bitcast.22, f32[2,8,4,8,128]{4,3,2,1,0:T(8,128)S(1)} %bitcast.29), custom_call_target="tpu_custom_call" | custom-call | flops 41943040 | bytes 8388608 | tf_op jit(solution)/shard_map/forecast_inner/pallas_call | solution.py:258
  21.6 6.2 %forecast_edges.1 = (f32[64,4,32,128]{3,2,1,0:T(8,128)S(1)}, f32[64,2,32,128]{3,2,1,0:T(8,128)S(1)}, f32[4,4,32,128]{3,2,1,0:T(8,128)S(1)}, f32[4,4,32,128]{3,2,1,0:T(8,128)S(1)}) custom-call(s32[2]{0:T(128)S(1)} %pad_add_fusion.ids, s32[8,512]{1,0:T(8,128)S(1)} %copy-done.4, s32[8]{0:T(128)S(1)} %copy-done.5, ...), custom_call_target="tpu_custom_call", output_to_operand_aliasing={{0}: (9, {}), {1}: (10, {})} | custom-call | flops 5242880 | bytes 1048576 | tf_op jit(solution)/shard_map/forecast_edges/pallas_call | solution.py:337
  27.8 0.1 collective-permute-start.2
  27.9 1.5 %collective-permute-done.2.other = f32[4,4,32,128]{3,2,1,0:T(8,128)S(1)} collective-permute-done((f32[4,4,32,128]{3,2,1,0:T(8,128)S(1)}, f32[4,4,32,128]{3,2,1,0:T(8,128)S(1)}, u32[]{:S(2)}, u32[]{:S(2)}) %collective-permute-start.2) | collective-permute-done | bytes 262176 | tf_op jit(solution)/shard_map/ppermute | solution.py:598
  29.4 1.4 %gram.1 = f32[4,64,128]{2,1,0:T(8,128)S(1)} custom-call(s32[2]{0:T(128)S(1)} %pad_add_fusion.ids, s32[8]{0:T(128)S(1)} %copy-done.5, s32[8]{0:T(128)S(1)} %copy-done.6, f32[4,4,32,128]{3,2,1,0:T(8,128)S(1)} %get-tuple-element.53.keep, f32[4,4,32,128]{3,2,1,0:T(8,128)S(1)} %collective-permute-done.2.other, f32[8,64,512]{2,1,0:T(8,128)S(1)} %copy-done.3, ...), custom_call_target="tpu_custom_call" | custom-call | tf_op jit(solution)/shard_map/gram/pallas_call | solution.py:420
  30.9 3.5 %forecast_rows_0.1 = (f32[64,2,32,128]{3,2,1,0:T(8,128)S(1)}, f32[64,2,32,128]{3,2,1,0:T(8,128)S(1)}) custom-call(s32[2]{0:T(128)S(1)} %pad_add_fusion.ids, f32[32,2,8,4,8,128]{5,4,3,2,1,0:T(8,128)S(1)} %bitcast.17, f32[2,8,4,8,128]{4,3,2,1,0:T(8,128)S(1)} %bitcast.24, f32[2,8,4,8,128]{4,3,2,1,0:T(8,128)S(1)} %bitcast.31, ...), custom_call_target="tpu_custom_call" | custom-call | flops 10485760 | bytes 2097152 | tf_op jit(solution)/shard_map/forecast_rows_0/pallas_call | solution.py:369
  34.4 1.4 %collective-permute-done.3 = f32[4,64,128]{2,1,0:T(8,128)S(1)} collective-permute-done((f32[4,64,128]{2,1,0:T(8,128)S(1)}, f32[4,64,128]{2,1,0:T(8,128)S(1)}, u32[]{:S(2)}, u32[]{:S(2)}) %collective-permute-start.3) | collective-permute-done | bytes 131104 | tf_op jit(solution)/shard_map/ppermute | solution.py:606
  36.0 3.6 %forecast_rows_16.1 = (f32[64,2,32,128]{3,2,1,0:T(8,128)S(1)}, f32[64,2,32,128]{3,2,1,0:T(8,128)S(1)}) custom-call(s32[2]{0:T(128)S(1)} %pad_add_fusion.ids, f32[32,2,8,4,8,128]{5,4,3,2,1,0:T(8,128)S(1)} %bitcast.18, f32[2,8,4,8,128]{4,3,2,1,0:T(8,128)S(1)} %bitcast.25, ...), custom_call_target="tpu_custom_call", output_to_operand_aliasing={{0}: (6, {}), {1}: (7, {})} | custom-call | flops 10485760 | bytes 2097152 | tf_op jit(solution)/shard_map/forecast_rows_16/pallas_call | solution.py:369
  39.6 1.3 %collective-permute-done.4 = f32[4,64,128]{2,1,0:T(8,128)S(1)} collective-permute-done((f32[4,64,128]{2,1,0:T(8,128)S(1)}, f32[4,64,128]{2,1,0:T(8,128)S(1)}, u32[]{:S(2)}, u32[]{:S(2)}) %collective-permute-start.4) | collective-permute-done | bytes 131104 | tf_op jit(solution)/shard_map/ppermute | solution.py:606
  40.9 7.5 %collective-permute-start.5 = (f32[4,64,128]{2,1,0:T(8,128)S(1)}, f32[4,64,128]{2,1,0:T(8,128)S(1)}, u32[]{:S(2)}, u32[]{:S(2)}) collective-permute-start(f32[4,64,128]{2,1,0:T(8,128)S(1)} %add.13), channel_id=1, source_target_pairs={{0,4},{1,5},{2,6},{3,7},{4,0},{5,1},{6,2},{7,3},{8,12},{9,13},{10,... | collective-permute-start | bytes 393224 | tf_op jit(solution)/shard_map/ppermute | solution.py:606
  48.4 3.6 %forecast_rows_32.1 = (f32[64,2,32,128]{3,2,1,0:T(8,128)S(1)}, f32[64,2,32,128]{3,2,1,0:T(8,128)S(1)}) custom-call(s32[2]{0:T(128)S(1)} %pad_add_fusion.ids, f32[32,2,8,4,8,128]{5,4,3,2,1,0:T(8,128)S(1)} %bitcast.19, f32[2,8,4,8,128]{4,3,2,1,0:T(8,128)S(1)} %bitcast.26, ...), custom_call_target="tpu_custom_call", output_to_operand_aliasing={{0}: (6, {}), {1}: (7, {})} | custom-call | flops 10485760 | bytes 2097152 | tf_op jit(solution)/shard_map/forecast_rows_32/pallas_call | solution.py:369
  52.1 0.1 collective-permute-start.6
  52.2 3.5 %forecast_rows_48.1 = (f32[64,2,32,128]{3,2,1,0:T(8,128)S(1)}, f32[64,2,32,128]{3,2,1,0:T(8,128)S(1)}) custom-call(s32[2]{0:T(128)S(1)} %pad_add_fusion.ids, f32[32,2,8,4,8,128]{5,4,3,2,1,0:T(8,128)S(1)} %bitcast.20, f32[2,8,4,8,128]{4,3,2,1,0:T(8,128)S(1)} %bitcast.27, ...), custom_call_target="tpu_custom_call", output_to_operand_aliasing={{0}: (6, {}), {1}: (7, {})} | custom-call | flops 10485760 | bytes 2097152 | tf_op jit(solution)/shard_map/forecast_rows_48/pallas_call | solution.py:369
  55.7 3.8 %collective-permute-done.6 = f32[4,64,128]{2,1,0:T(8,128)S(1)} collective-permute-done((f32[4,64,128]{2,1,0:T(8,128)S(1)}, f32[4,64,128]{2,1,0:T(8,128)S(1)}, u32[]{:S(2)}, u32[]{:S(2)}) %collective-permute-start.6) | collective-permute-done | bytes 131104 | tf_op jit(solution)/shard_map/ppermute | solution.py:606
  59.4 0.1 collective-permute-start.8
  59.5 0.5 collective-permute-start.9
  60.0 0.1 collective-permute-start.7
  60.1 6.8 %collective-permute-done.7.other = f32[4,64,128]{2,1,0:T(8,128)S(1)} collective-permute-done((f32[4,64,128]{2,1,0:T(8,128)S(1)}, f32[4,64,128]{2,1,0:T(8,128)S(1)}, u32[]{:S(2)}, u32[]{:S(2)}) %collective-permute-start.7) | collective-permute-done | bytes 131104 | tf_op jit(solution)/shard_map/ppermute | solution.py:616
  66.8 20.4 %chain.1.w_ref = f32[128,128]{1,0:T(8,128)S(1)} custom-call(s32[2]{0:T(128)S(1)} %pad_add_fusion.ids, f32[4,64,128]{2,1,0:T(8,128)S(1)} %add.15.mine, f32[4,64,128]{2,1,0:T(8,128)S(1)} %collective-permute-done.7.other), custom_call_target="tpu_custom_call" | custom-call | tf_op jit(solution)/shard_map/chain/pallas_call | solution.py:520
  87.3 9.6 %apply.1 = f32[64,2,8,2,8,128]{5,4,3,2,1,0:T(8,128)} custom-call(f32[128,128]{1,0:T(8,128)S(1)} %chain.1.w_ref, f32[64,4,32,128]{3,2,1,0:T(8,128)S(1)} %get-tuple-element.87.own0, f32[64,2,32,128]{3,2,1,0:T(8,128)S(1)} %collective-permute-done.8.other0, f32[64,2,32,128]{3,2,1,0:T(8,128)S(1)} %get-tuple-element.89.own1, ...), custom_call_target="tpu_custom_call" | custom-call | tf_op jit(solution)/shard_map/apply/pallas_call | solution.py:568
  (28 shorter events, 0.3 us)
Async XLA Ops:
  0.0 8.5 %copy-start.1 = (f32[2,64,512]{2,1,0:T(8,128)S(1)}, f32[2,64,512]{2,1,0:T(8,128)}, u32[]{:S(2)}) copy-start(f32[2,64,512]{2,1,0:T(8,128)} %param.9) | copy-start | bytes 786436
  0.0 8.5 %copy-start.2 = (f32[2,64,512]{2,1,0:T(8,128)S(1)}, f32[2,64,512]{2,1,0:T(8,128)}, u32[]{:S(2)}) copy-start(f32[2,64,512]{2,1,0:T(8,128)} %param.10) | copy-start | bytes 786436
  2.2 19.2 %collective-permute-start = (f32[4,136,128]{2,1,0:T(8,128)}, f32[4,136,128]{2,1,0:T(8,128)S(1)}, u32[]{:S(2)}, u32[]{:S(2)}) collective-permute-start(f32[4,136,128]{2,1,0:T(8,128)} %get-tuple-element.48), channel_id=1, source_target_pairs={{0,1},{1,2},{2,3},{3,4},{4,5},{5,6},{6,7},{7,8},{8,9},{9,10},{10,1... | collective-permute-start | bytes 835592 | tf_op jit(solution)/shard_map/ppermute | solution.py:592
  7.1 14.4 %collective-permute-start.1 = (f32[4,136,128]{2,1,0:T(8,128)}, f32[4,136,128]{2,1,0:T(8,128)S(1)}, u32[]{:S(2)}, u32[]{:S(2)}) collective-permute-start(f32[4,136,128]{2,1,0:T(8,128)} %get-tuple-element.49), channel_id=1, source_target_pairs={{1,0},{2,1},{3,2},{4,3},{5,4},{6,5},{7,6},{8,7},{9,8},{10,9},{11,1... | collective-permute-start | bytes 835592 | tf_op jit(solution)/shard_map/ppermute | solution.py:593
  8.5 13.0 %copy-start = (f32[32,2,64,512]{3,2,1,0:T(8,128)S(1)}, f32[32,2,64,512]{3,2,1,0:T(8,128)}, u32[]{:S(2)}) copy-start(f32[32,2,64,512]{3,2,1,0:T(8,128)} %param.8) | copy-start | bytes 25165828
  8.5 13.0 %copy-start.4 = (s32[8,512]{1,0:T(8,128)S(1)}, s32[8,512]{1,0:T(8,128)}, u32[]{:S(2)}) copy-start(s32[8,512]{1,0:T(8,128)} %cells.1) | copy-start | bytes 49156
  8.5 13.0 %copy-start.5 = (s32[8]{0:T(128)S(1)}, s32[8]{0:T(128)}, u32[]{:S(2)}) copy-start(s32[8]{0:T(128)} %owner.3) | copy-start | bytes 100
  8.5 13.0 %copy-start.6 = (s32[8]{0:T(128)S(1)}, s32[8]{0:T(128)}, u32[]{:S(2)}) copy-start(s32[8]{0:T(128)} %order.3) | copy-start | bytes 100
  21.5 6.4 %copy-start.7 = (f32[8,512]{1,0:T(8,128)S(1)}, f32[8,512]{1,0:T(8,128)}, u32[]{:S(2)}) copy-start(f32[8,512]{1,0:T(8,128)} %param.15) | copy-start | bytes 49156
  21.5 7.9 %copy-start.3 = (f32[8,64,512]{2,1,0:T(8,128)S(1)}, f32[8,64,512]{2,1,0:T(8,128)}, u32[]{:S(2)}) copy-start(f32[8,64,512]{2,1,0:T(8,128)} %observed.1) | copy-start | bytes 3145732
  27.8 1.6 %collective-permute-start.2 = (f32[4,4,32,128]{3,2,1,0:T(8,128)S(1)}, f32[4,4,32,128]{3,2,1,0:T(8,128)S(1)}, u32[]{:S(2)}, u32[]{:S(2)}) collective-permute-start(f32[4,4,32,128]{3,2,1,0:T(8,128)S(1)} %get-tuple-element.54), channel_id=1, source_target_pairs={{0,16},{16,0},{1,17},{17,1},{2,18},{18,2},{3,19},{19,3},{4,20},{20... | collective-permute-start | bytes 786440 | tf_op jit(solution)/shard_map/ppermute | solution.py:598
  30.8 5.0 %collective-permute-start.3 = (f32[4,64,128]{2,1,0:T(8,128)S(1)}, f32[4,64,128]{2,1,0:T(8,128)S(1)}, u32[]{:S(2)}, u32[]{:S(2)}) collective-permute-start(f32[4,64,128]{2,1,0:T(8,128)S(1)} %gram.1), channel_id=1, source_target_pairs={{0,1},{1,0},{2,3},{3,2},{4,5},{5,4},{6,7},{7,6},{8,9},{9,8},{10,11... | collective-permute-start | bytes 393224 | tf_op jit(solution)/shard_map/ppermute | solution.py:606
  35.9 5.0 %collective-permute-start.4 = (f32[4,64,128]{2,1,0:T(8,128)S(1)}, f32[4,64,128]{2,1,0:T(8,128)S(1)}, u32[]{:S(2)}, u32[]{:S(2)}) collective-permute-start(f32[4,64,128]{2,1,0:T(8,128)S(1)} %add.12), channel_id=1, source_target_pairs={{0,2},{1,3},{2,0},{3,1},{4,6},{5,7},{6,4},{7,5},{8,10},{9,11},{10,... | collective-permute-start | bytes 393224 | tf_op jit(solution)/shard_map/ppermute | solution.py:606
  40.9 11.1 %collective-permute-start.5 = (f32[4,64,128]{2,1,0:T(8,128)S(1)}, f32[4,64,128]{2,1,0:T(8,128)S(1)}, u32[]{:S(2)}, u32[]{:S(2)}) collective-permute-start(f32[4,64,128]{2,1,0:T(8,128)S(1)} %add.13), channel_id=1, source_target_pairs={{0,4},{1,5},{2,6},{3,7},{4,0},{5,1},{6,2},{7,3},{8,12},{9,13},{10,... | collective-permute-start | bytes 393224 | tf_op jit(solution)/shard_map/ppermute | solution.py:606
  52.1 7.3 %collective-permute-start.6 = (f32[4,64,128]{2,1,0:T(8,128)S(1)}, f32[4,64,128]{2,1,0:T(8,128)S(1)}, u32[]{:S(2)}, u32[]{:S(2)}) collective-permute-start(f32[4,64,128]{2,1,0:T(8,128)S(1)} %add.14), channel_id=1, source_target_pairs={{0,8},{1,9},{2,10},{3,11},{4,12},{5,13},{6,14},{7,15},{8,0},{9,1},... | collective-permute-start | bytes 393224 | tf_op jit(solution)/shard_map/ppermute | solution.py:606
  59.4 27.9 %collective-permute-start.8 = (f32[64,2,32,128]{3,2,1,0:T(8,128)S(1)}, f32[64,2,32,128]{3,2,1,0:T(8,128)S(1)}, u32[]{:S(2)}, u32[]{:S(2)}) collective-permute-start(f32[64,2,32,128]{3,2,1,0:T(8,128)S(1)} %get-tuple-element.88), channel_id=1, source_target_pairs={{0,16},{16,0},{1,17},{17,1},{2,18},{18,2},{3,19},{19,3},{4,20},{20... | collective-permute-start | bytes 6291464 | tf_op jit(solution)/shard_map/ppermute | solution.py:618
  59.5 27.8 %collective-permute-start.9 = (f32[64,2,32,128]{3,2,1,0:T(8,128)S(1)}, f32[64,2,32,128]{3,2,1,0:T(8,128)S(1)}, u32[]{:S(2)}, u32[]{:S(2)}) collective-permute-start(f32[64,2,32,128]{3,2,1,0:T(8,128)S(1)} %get-tuple-element.90), channel_id=1, source_target_pairs={{0,16},{16,0},{1,17},{17,1},{2,18},{18,2},{3,19},{19,3},{4,20},{20... | collective-permute-start | bytes 6291464 | tf_op jit(solution)/shard_map/ppermute | solution.py:619
  60.0 6.8 %collective-permute-start.7 = (f32[4,64,128]{2,1,0:T(8,128)S(1)}, f32[4,64,128]{2,1,0:T(8,128)S(1)}, u32[]{:S(2)}, u32[]{:S(2)}) collective-permute-start(f32[4,64,128]{2,1,0:T(8,128)S(1)} %add.15.mine), channel_id=1, source_target_pairs={{0,16},{16,0},{1,17},{17,1},{2,18},{18,2},{3,19},{19,3},{4,20},{20... | collective-permute-start | bytes 393224 | tf_op jit(solution)/shard_map/ppermute | solution.py:616

commit v5 on v4

--- a/solution.py
+++ b/solution.py
@@ -379,20 +379,22 @@
     )(ids, state6, flow5, nu5, before, after, *done)
 
 
-def gram_kernel(ids, owner, order, keep, other, observed, variance, out):
+def gram_kernel(ids, owner, order, keep, other, observed, variance, *outs):
     slab, member = ids[0], ids[1]
     count, tiles, members = keep.shape[:3]
     for k in range(count):
         batch = order[2 * k + member]
         mine = owner[batch] == slab
+        part = count // len(outs)
+        out = outs[k // part].at[k % part]
 
         @pl.when(jnp.logical_not(mine))
         def _():
-            out[k] = jnp.zeros(out.shape[1:], F32)
+            out[...] = jnp.zeros(out.shape, F32)
 
         @pl.when(mine)
         def _():
-            total = jnp.zeros(out.shape[1:], F32)
+            pair = jnp.zeros(out.shape, F32)
             for t in range(tiles):
                 a, b = keep[k, t], other[k, t]
                 prior = jnp.concatenate(
@@ -402,14 +404,14 @@
                 anomaly = prior - mean
                 scaled = anomaly / variance[batch, :, pl.ds(t * LANES, LANES)]
                 misfit = observed[batch, :, pl.ds(t * LANES, LANES)] - mean
-                total += lax.dot_general(
+                pair += lax.dot_general(
                     scaled,
                     jnp.concatenate([anomaly, misfit], axis=0),
                     (((1,), (1,)), ((), ())),
                     precision=HIGH,
                     preferred_element_type=F32,
                 )
-            out[k] = total
+            out[...] = pair
 
 
 def gram(ids, owner, order, keep, other, observed, variance):
@@ -419,12 +421,18 @@
     vmem = pl.BlockSpec(memory_space=pltpu.VMEM)
     return pl.pallas_call(
         gram_kernel,
-        out_shape=jax.ShapeDtypeStruct((count, total, 2 * total), F32),
+        out_shape=[jax.ShapeDtypeStruct((count // 2, total, 2 * total), F32)] * 2,
         in_specs=[smem] * 3 + [vmem] * 4,
-        out_specs=vmem,
+        out_specs=[vmem] * 2,
         compiler_params=params(12),
         name="gram",
     )(ids, owner, order, keep, other, observed, variance[:, None, :])
+
+
+def total(terms):
+    while len(terms) > 1:
+        terms = [x + y for x, y in zip(terms[::2], terms[1::2])]
+    return terms[0]
 
 
 def solve(inner, rhs):
@@ -444,36 +452,53 @@
     for p in range(groups):
         cols = [[column(a[g], p * SUB + k) for k in range(SUB)] for g in range(groups)]
         c, pa, pb = cols[p], a[p], b[p]
+        after = p + 1 if p + 1 < groups else None
+        e = cols[after] if after else []
         for k in range(0, SUB, 2):
             ck, cl = c[k], c[k + 1]
             kk, kl, lk, ll = row(ck, k), row(cl, k), row(ck, k + 1), row(cl, k + 1)
             scale = 1.0 / (kk * ll - kl * lk)
 
-            def eliminate(x, k=k, ck=ck, cl=cl, kk=kk, kl=kl, lk=lk, ll=ll, scale=scale):
+            def pivot_rows(x, k=k, kk=kk, kl=kl, lk=lk, ll=ll):
                 u, w = row(x, k), row(x, k + 1)
-                n0, n1 = ll * u - kl * w, kk * w - lk * u
+                return ll * u - kl * w, kk * w - lk * u
+
+            def inside(x, n0, n1, k=k, ck=ck, cl=cl, scale=scale):
                 rest = x - scale * (ck * n0 + cl * n1)
                 return jnp.where(sub == k, scale * n0, jnp.where(sub == k + 1, scale * n1, rest))
 
+            def outside(x, n0, n1, k=k, scale=scale):
+                return x - scale * (e[k] * n0 + e[k + 1] * n1)
+
             for j in range(k + 2, SUB):
-                c[j] = eliminate(c[j])
-            pa, pb = eliminate(pa), eliminate(pb)
+                n = pivot_rows(c[j])
+                c[j] = inside(c[j], *n)
+                if after:
+                    e[j] = outside(e[j], *n)
+            n = pivot_rows(pa)
+            pa = inside(pa, *n)
+            if after:
+                a[after] = outside(a[after], *n)
+            n = pivot_rows(pb)
+            pb = inside(pb, *n)
+            if after:
+                b[after] = outside(b[after], *n)
         a[p], b[p] = pa, pb
         ra = [row(pa, k) for k in range(SUB)]
         rb = [row(pb, k) for k in range(SUB)]
         for g in range(groups):
-            if g == p:
+            if g in (p, after):
                 continue
-            for k in range(SUB):
-                if p + 1 < groups:
-                    a[g] = a[g] - cols[g][k] * ra[k]
-                b[g] = b[g] - cols[g][k] * rb[k]
+            if p + 1 < groups:
+                a[g] = a[g] - total([cols[g][k] * ra[k] for k in range(SUB)])
+            b[g] = b[g] - total([cols[g][k] * rb[k] for k in range(SUB)])
     return jnp.concatenate(b, axis=0)
 
 
-def chain_kernel(ids, mine, other, out):
+def chain_kernel(last, ids, mine, other, *rest):
     member = ids[1]
     count, size, _ = mine.shape
+    out = rest[-1]
     eye = (
         lax.broadcasted_iota(jnp.int32, (size, 2 * size), 0)
         == lax.broadcasted_iota(jnp.int32, (size, 2 * size), 1)
@@ -497,8 +522,14 @@
         rhs = both[:, 2 * size :] - both[:, : 2 * size]
         return v + dot(z, solve(inner, rhs))
 
-    start = jnp.concatenate([unit - 1.0 / size, unit], axis=1)
+    if len(rest) > 1:
+        start = rest[0][...]
+    else:
+        start = jnp.concatenate([unit - 1.0 / size, unit], axis=1)
     v = lax.fori_loop(0, 2 * count, step, start)
+    if not last:
+        out[...] = v
+        return
     w = v[:, size:].T
     half = size // 2
     first, second = w[:, :half], w[:, half:]
@@ -513,18 +544,16 @@
     )
 
 
-def chain(ids, mine, other):
-    count, size, _ = mine.shape
-    smem = pl.BlockSpec(memory_space=pltpu.SMEM)
-    vmem = pl.BlockSpec(memory_space=pltpu.VMEM)
+def chain(last, ids, mine, other, *start):
+    size = mine.shape[1]
     return pl.pallas_call(
-        chain_kernel,
-        out_shape=jax.ShapeDtypeStruct((2 * size, 2 * size), F32),
-        in_specs=[smem, vmem, vmem],
-        out_specs=vmem,
+        functools.partial(chain_kernel, last),
+        out_shape=jax.ShapeDtypeStruct(((1 + last) * size, 2 * size), F32),
+        in_specs=[SMEM] + [VMEM] * (2 + len(start)),
+        out_specs=VMEM,
         compiler_params=params(12),
-        name="chain",
-    )(ids, mine, other)
+        name="chain_last" if last else "chain_first",
+    )(ids, mine, other, *start)
 
 
 def apply_kernel(w_ref, own0, other0, own1, other1, out):
@@ -596,28 +625,39 @@
         ids, obs_cells, obs_owner, batch_order, state6, flow5, nu5, before, after, full0, send0
     )
     other = lax.ppermute(away, "member", swap)
-    gh = gram(ids, obs_owner, batch_order, keep, other, obs_values, obs_error)
+    early, late = gram(ids, obs_owner, batch_order, keep, other, obs_values, obs_error)
 
     rows = state.shape[2]
     pieces = [(r, r + rows // 4) for r in range(0, rows, rows // 4)]
     field1 = ()
-    bit = 1
-    while bit < space:
-        received = lax.ppermute(gh, "space", [(i, i ^ bit) for i in range(space)])
+    bits = [1 << i for i in range(space.bit_length() - 1)]
+
+    def partner(bit):
+        return [(i, i ^ bit) for i in range(space)]
+
+    for turn, bit in enumerate(bits):
+        received = [lax.ppermute(early, "space", partner(bit))]
+        if turn > 0:
+            received.append(lax.ppermute(late, "space", partner(bits[turn - 1])))
         if pieces:
-            before, after, gh = lax.optimization_barrier((before, after, gh))
+            before, after, early, late = lax.optimization_barrier((before, after, early, late))
             field1 = forecast_piece(*pieces.pop(0), ids, state6, flow5, nu5, before, after, field1)
-            received, *field1 = lax.optimization_barrier((received, *field1))
-        gh = gh + received
-        bit *= 2
+            received, field1 = lax.optimization_barrier((received, field1))
+        early = early + received[0]
+        if turn > 0:
+            late = late + received[1]
     for piece in pieces:
         field1 = forecast_piece(*piece, ids, state6, flow5, nu5, before, after, field1)
     own1, send1 = field1
-    theirs = lax.ppermute(gh, "member", swap)
-    send0, send1, gh = lax.optimization_barrier((send0, send1, gh))
+    early_theirs = lax.ppermute(early, "member", swap)
+    late = late + lax.ppermute(late, "space", partner(bits[-1]))
+    early, early_theirs, late = lax.optimization_barrier((early, early_theirs, late))
+    late_theirs = lax.ppermute(late, "member", swap)
+    send0, send1, early = lax.optimization_barrier((send0, send1, early))
     other0 = lax.ppermute(send0, "member", swap)
     other1 = lax.ppermute(send1, "member", swap)
-    weights = chain(ids, gh, theirs)
+    v = chain(False, ids, early, early_theirs)
+    weights = chain(True, ids, late, late_theirs, v)
     return untiled(apply(weights, full0, other0, own1, other1))
 
 

time: 97.2 us -> 94 us (0.967)
  waiting for transfers between devices: 14.7 us -> 5.67 us
  starting transfers between devices: 14.5 us -> 21.2 us
  Pallas kernels: 67.2 us -> 65.6 us
    ppermute x5 -> x10, waiting for transfers between devices: 13.2 us -> 4.17 us  [the longest x1 4.14 us: body(): late = late + lax.ppermute(late, 'space', partner(bits[-1]))]
    ppermute x5 -> x10, starting transfers between devices: 7.75 us -> 14.4 us  [the longest x4 9.27 us: body(): received = [lax.ppermute(early, 'space', partner(bit))]]
    pallas_call x2 -> x3, Pallas kernels: 21.9 us -> 20.3 us  [the longest x2 19.5 us: chain(): pl.pallas_call(functools.partial(chain_kernel, last), out_shape=jax.Shape...]
  transfers between devices with their start and end apart: 10 -> 15, of which waited for: 5 -> 2; matrix products, arithmetic and copies ran while one was open for 0% -> 0% of each run, Pallas kernels for 49% -> 50%
where the time goes in v5:
time: 94 us; the launch traced here: 93 us
  Pallas kernels  65.6 us (70%)
  starting transfers between devices  21.2 us (23%)
  waiting for transfers between devices  5.67 us (6%)
    pallas_call x2, Pallas kernels, chain(): pl.pallas_call(functools.partial(chain_kernel, last), out_shape=jax.Shape...  19.5 us
    pallas_call x4, Pallas kernels, forecast_piece(): pl.pallas_call(functools.partial(piece_kernel, lo, hi), out_shape=[part,...  14.3 us
    pallas_call x1, Pallas kernels, forecast_inner(): pl.pallas_call(functools.partial(inner_kernel, 2, rows - 2), out_shape=[j...  12.9 us
    pallas_call x1, Pallas kernels, apply(): pl.pallas_call(apply_kernel, grid=(2, r8), out_shape=jax.ShapeDtypeStruct...  9.62 us
    ppermute x4, starting transfers between devices, body(): received = [lax.ppermute(early, 'space', partner(bit))]  9.27 us
    pallas_call x1, Pallas kernels, forecast_edges(): pl.pallas_call(edge_kernel, out_shape=[jax.ShapeDtypeStruct(full.shape, F...  6.24 us
    ppermute x1, starting transfers between devices, body(): before = lax.ppermute(up_edge, 'space', up)  4.86 us
    ppermute x1, waiting for transfers between devices, body(): late = late + lax.ppermute(late, 'space', partner(bits[-1]))  4.14 us
  transfers between devices with their start and end apart: 15, of which 2 were waited for; matrix products, arithmetic and copies ran while one was open for 0% of the time, Pallas kernels for 50%

profile of v5, /device:TPU:0, one launch (start us, length us, event | category | flops | bytes accessed | tf_op | source)
XLA Modules:
  0.0 93.0 jit_solution(8377694436007183310)
XLA Ops:
  0.0 2.2 %pack_edges.1 = (f32[4,136,128]{2,1,0:T(8,128)}, f32[4,136,128]{2,1,0:T(8,128)}) custom-call(f32[32,2,8,4,8,128]{5,4,3,2,1,0:T(8,128)} %bitcast.14, f32[2,8,4,8,128]{4,3,2,1,0:T(8,128)} %bitcast.21, f32[2,8,4,8,128]{4,3,2,1,0:T(8,128)} %bitcast.28), custom_call_target="tpu_custom_call" | custom-call | tf_op jit(solution)/shard_map/pack_edges/pallas_call | solution.py:90
  2.2 4.9 %collective-permute-start = (f32[4,136,128]{2,1,0:T(8,128)}, f32[4,136,128]{2,1,0:T(8,128)S(1)}, u32[]{:S(2)}, u32[]{:S(2)}) collective-permute-start(f32[4,136,128]{2,1,0:T(8,128)} %get-tuple-element.60), channel_id=1, source_target_pairs={{0,1},{1,2},{2,3},{3,4},{4,5},{5,6},{6,7},{7,8},{8,9},{9,10},{10,1... | collective-permute-start | bytes 835592 | tf_op jit(solution)/shard_map/ppermute | solution.py:621
  7.1 1.3 %collective-permute-start.1 = (f32[4,136,128]{2,1,0:T(8,128)}, f32[4,136,128]{2,1,0:T(8,128)S(1)}, u32[]{:S(2)}, u32[]{:S(2)}) collective-permute-start(f32[4,136,128]{2,1,0:T(8,128)} %get-tuple-element.61), channel_id=1, source_target_pairs={{1,0},{2,1},{3,2},{4,3},{5,4},{6,5},{7,6},{8,7},{9,8},{10,9},{11,1... | collective-permute-start | bytes 835592 | tf_op jit(solution)/shard_map/ppermute | solution.py:622
  8.5 12.9 %forecast_inner.1 = (f32[64,4,32,128]{3,2,1,0:T(8,128)S(1)}, f32[64,2,32,128]{3,2,1,0:T(8,128)S(1)}) custom-call(s32[2]{0:T(128)S(1)} %pad_add_fusion.ids, f32[32,2,8,4,8,128]{5,4,3,2,1,0:T(8,128)} %bitcast.15, f32[2,8,4,8,128]{4,3,2,1,0:T(8,128)S(1)} %bitcast.22, f32[2,8,4,8,128]{4,3,2,1,0:T(8,128)S(1)} %bitcast.29), custom_call_target="tpu_custom_call" | custom-call | flops 41943040 | bytes 8388608 | tf_op jit(solution)/shard_map/forecast_inner/pallas_call | solution.py:258
  21.5 6.2 %forecast_edges.1 = (f32[64,4,32,128]{3,2,1,0:T(8,128)S(1)}, f32[64,2,32,128]{3,2,1,0:T(8,128)S(1)}, f32[4,4,32,128]{3,2,1,0:T(8,128)S(1)}, f32[4,4,32,128]{3,2,1,0:T(8,128)S(1)}) custom-call(s32[2]{0:T(128)S(1)} %pad_add_fusion.ids, s32[8,512]{1,0:T(8,128)S(1)} %copy-done.4, s32[8]{0:T(128)S(1)} %copy-done.5, ...), custom_call_target="tpu_custom_call", output_to_operand_aliasing={{0}: (9, {}), {1}: (10, {})} | custom-call | flops 5242880 | bytes 1048576 | tf_op jit(solution)/shard_map/forecast_edges/pallas_call | solution.py:337
  27.9 1.5 %collective-permute-done.2.other = f32[4,4,32,128]{3,2,1,0:T(8,128)S(1)} collective-permute-done((f32[4,4,32,128]{3,2,1,0:T(8,128)S(1)}, f32[4,4,32,128]{3,2,1,0:T(8,128)S(1)}, u32[]{:S(2)}, u32[]{:S(2)}) %collective-permute-start.2) | collective-permute-done | bytes 262176 | tf_op jit(solution)/shard_map/ppermute | solution.py:627
  29.4 0.8 gram.1
  30.3 2.0 %collective-permute-start.5 = (f32[2,64,128]{2,1,0:T(8,128)S(1)}, f32[2,64,128]{2,1,0:T(8,128)S(1)}, u32[]{:S(2)}, u32[]{:S(2)}) collective-permute-start(f32[2,64,128]{2,1,0:T(8,128)S(1)} %get-tuple-element.83), channel_id=1, source_target_pairs={{0,1},{1,0},{2,3},{3,2},{4,5},{5,4},{6,7},{7,6},{8,9},{9,8},{10,11... | collective-permute-start | bytes 196616 | tf_op jit(solution)/shard_map/ppermute | solution.py:641
  32.3 3.5 %forecast_rows_0.1 = (f32[64,2,32,128]{3,2,1,0:T(8,128)S(1)}, f32[64,2,32,128]{3,2,1,0:T(8,128)S(1)}) custom-call(s32[2]{0:T(128)S(1)} %pad_add_fusion.ids, f32[32,2,8,4,8,128]{5,4,3,2,1,0:T(8,128)S(1)} %bitcast.17, f32[2,8,4,8,128]{4,3,2,1,0:T(8,128)S(1)} %bitcast.24, f32[2,8,4,8,128]{4,3,2,1,0:T(8,128)S(1)} %bitcast.31, ...), custom_call_target="tpu_custom_call" | custom-call | flops 10485760 | bytes 2097152 | tf_op jit(solution)/shard_map/forecast_rows_0/pallas_call | solution.py:369
  35.9 2.9 %collective-permute-start.4 = (f32[2,64,128]{2,1,0:T(8,128)S(1)}, f32[2,64,128]{2,1,0:T(8,128)S(1)}, u32[]{:S(2)}, u32[]{:S(2)}) collective-permute-start(f32[2,64,128]{2,1,0:T(8,128)S(1)} %add.24), channel_id=1, source_target_pairs={{0,2},{1,3},{2,0},{3,1},{4,6},{5,7},{6,4},{7,5},{8,10},{9,11},{10,... | collective-permute-start | bytes 196616 | tf_op jit(solution)/shard_map/ppermute | solution.py:639
  38.7 3.6 %forecast_rows_16.1 = (f32[64,2,32,128]{3,2,1,0:T(8,128)S(1)}, f32[64,2,32,128]{3,2,1,0:T(8,128)S(1)}) custom-call(s32[2]{0:T(128)S(1)} %pad_add_fusion.ids, f32[32,2,8,4,8,128]{5,4,3,2,1,0:T(8,128)S(1)} %bitcast.18, f32[2,8,4,8,128]{4,3,2,1,0:T(8,128)S(1)} %bitcast.25, ...), custom_call_target="tpu_custom_call", output_to_operand_aliasing={{0}: (6, {}), {1}: (7, {})} | custom-call | flops 10485760 | bytes 2097152 | tf_op jit(solution)/shard_map/forecast_rows_16/pallas_call | solution.py:369
  42.4 0.7 collective-permute-start.7
  43.1 3.2 %collective-permute-start.6 = (f32[2,64,128]{2,1,0:T(8,128)S(1)}, f32[2,64,128]{2,1,0:T(8,128)S(1)}, u32[]{:S(2)}, u32[]{:S(2)}) collective-permute-start(f32[2,64,128]{2,1,0:T(8,128)S(1)} %add.25), channel_id=1, source_target_pairs={{0,4},{1,5},{2,6},{3,7},{4,0},{5,1},{6,2},{7,3},{8,12},{9,13},{10,... | collective-permute-start | bytes 196616 | tf_op jit(solution)/shard_map/ppermute | solution.py:639
  46.3 3.6 %forecast_rows_32.1 = (f32[64,2,32,128]{3,2,1,0:T(8,128)S(1)}, f32[64,2,32,128]{3,2,1,0:T(8,128)S(1)}) custom-call(s32[2]{0:T(128)S(1)} %pad_add_fusion.ids, f32[32,2,8,4,8,128]{5,4,3,2,1,0:T(8,128)S(1)} %bitcast.19, f32[2,8,4,8,128]{4,3,2,1,0:T(8,128)S(1)} %bitcast.26, ...), custom_call_target="tpu_custom_call", output_to_operand_aliasing={{0}: (6, {}), {1}: (7, {})} | custom-call | flops 10485760 | bytes 2097152 | tf_op jit(solution)/shard_map/forecast_rows_32/pallas_call | solution.py:369
  50.0 0.7 collective-permute-start.9
  50.6 3.1 %collective-permute-start.8 = (f32[2,64,128]{2,1,0:T(8,128)S(1)}, f32[2,64,128]{2,1,0:T(8,128)S(1)}, u32[]{:S(2)}, u32[]{:S(2)}) collective-permute-start(f32[2,64,128]{2,1,0:T(8,128)S(1)} %add.27), channel_id=1, source_target_pairs={{0,8},{1,9},{2,10},{3,11},{4,12},{5,13},{6,14},{7,15},{8,0},{9,1},... | collective-permute-start | bytes 196616 | tf_op jit(solution)/shard_map/ppermute | solution.py:639
  53.8 3.5 %forecast_rows_48.1 = (f32[64,2,32,128]{3,2,1,0:T(8,128)S(1)}, f32[64,2,32,128]{3,2,1,0:T(8,128)S(1)}) custom-call(s32[2]{0:T(128)S(1)} %pad_add_fusion.ids, f32[32,2,8,4,8,128]{5,4,3,2,1,0:T(8,128)S(1)} %bitcast.20, f32[2,8,4,8,128]{4,3,2,1,0:T(8,128)S(1)} %bitcast.27, ...), custom_call_target="tpu_custom_call", output_to_operand_aliasing={{0}: (6, {}), {1}: (7, {})} | custom-call | flops 10485760 | bytes 2097152 | tf_op jit(solution)/shard_map/forecast_rows_48/pallas_call | solution.py:369
  57.3 1.7 %collective-permute-start.11 = (f32[2,64,128]{2,1,0:T(8,128)S(1)}, f32[2,64,128]{2,1,0:T(8,128)S(1)}, u32[]{:S(2)}, u32[]{:S(2)}) collective-permute-start(f32[2,64,128]{2,1,0:T(8,128)S(1)} %add.30), channel_id=1, source_target_pairs={{0,8},{1,9},{2,10},{3,11},{4,12},{5,13},{6,14},{7,15},{8,0},{9,1},... | collective-permute-start | bytes 196616 | tf_op jit(solution)/shard_map/ppermute | solution.py:653
  59.1 4.1 %collective-permute-done.11 = f32[2,64,128]{2,1,0:T(8,128)S(1)} collective-permute-done((f32[2,64,128]{2,1,0:T(8,128)S(1)}, f32[2,64,128]{2,1,0:T(8,128)S(1)}, u32[]{:S(2)}, u32[]{:S(2)}) %collective-permute-start.11) | collective-permute-done | bytes 65568 | tf_op jit(solution)/shard_map/ppermute | solution.py:653
  63.3 0.5 collective-permute-start.14
  63.8 0.1 collective-permute-start.12
  63.9 9.6 %chain_first.1.rest_0_ = f32[64,128]{1,0:T(8,128)S(1)} custom-call(s32[2]{0:T(128)S(1)} %pad_add_fusion.ids, f32[2,64,128]{2,1,0:T(8,128)S(1)} %add.29.mine, f32[2,64,128]{2,1,0:T(8,128)S(1)} %collective-permute-done.10.other), custom_call_target="tpu_custom_call" | custom-call | tf_op jit(solution)/shard_map/chain_first/pallas_call | solution.py:549
  73.6 9.9 %chain_last.1.w_ref = f32[128,128]{1,0:T(8,128)S(1)} custom-call(s32[2]{0:T(128)S(1)} %pad_add_fusion.ids, f32[2,64,128]{2,1,0:T(8,128)S(1)} %add.31.mine, f32[2,64,128]{2,1,0:T(8,128)S(1)} %collective-permute-done.12.other, f32[64,128]{1,0:T(8,128)S(1)} %chain_first.1.rest_0_), custom_call_target="tpu_custom_call" | custom-call | tf_op jit(solution)/shard_map/chain_last/pallas_call | solution.py:549
  83.4 9.6 %apply.1 = f32[64,2,8,2,8,128]{5,4,3,2,1,0:T(8,128)} custom-call(f32[128,128]{1,0:T(8,128)S(1)} %chain_last.1.w_ref, f32[64,4,32,128]{3,2,1,0:T(8,128)S(1)} %get-tuple-element.111.own0, f32[64,2,32,128]{3,2,1,0:T(8,128)S(1)} %collective-permute-done.13.other0, f32[64,2,32,128]{3,2,1,0:T(8,128)S(1)} %get-tuple-element.113.own1, ...), custom_call_target="tpu_custom_call" | custom-call | tf_op jit(solution)/shard_map/apply/pallas_call | solution.py:597
  (43 shorter events, 0.5 us)
Async XLA Ops:
  0.0 8.5 %copy-start.1 = (f32[2,64,512]{2,1,0:T(8,128)S(1)}, f32[2,64,512]{2,1,0:T(8,128)}, u32[]{:S(2)}) copy-start(f32[2,64,512]{2,1,0:T(8,128)} %param.9) | copy-start | bytes 786436
  0.0 8.5 %copy-start.2 = (f32[2,64,512]{2,1,0:T(8,128)S(1)}, f32[2,64,512]{2,1,0:T(8,128)}, u32[]{:S(2)}) copy-start(f32[2,64,512]{2,1,0:T(8,128)} %param.10) | copy-start | bytes 786436
  2.2 19.2 %collective-permute-start = (f32[4,136,128]{2,1,0:T(8,128)}, f32[4,136,128]{2,1,0:T(8,128)S(1)}, u32[]{:S(2)}, u32[]{:S(2)}) collective-permute-start(f32[4,136,128]{2,1,0:T(8,128)} %get-tuple-element.60), channel_id=1, source_target_pairs={{0,1},{1,2},{2,3},{3,4},{4,5},{5,6},{6,7},{7,8},{8,9},{9,10},{10,1... | collective-permute-start | bytes 835592 | tf_op jit(solution)/shard_map/ppermute | solution.py:621
  7.1 14.4 %collective-permute-start.1 = (f32[4,136,128]{2,1,0:T(8,128)}, f32[4,136,128]{2,1,0:T(8,128)S(1)}, u32[]{:S(2)}, u32[]{:S(2)}) collective-permute-start(f32[4,136,128]{2,1,0:T(8,128)} %get-tuple-element.61), channel_id=1, source_target_pairs={{1,0},{2,1},{3,2},{4,3},{5,4},{6,5},{7,6},{8,7},{9,8},{10,9},{11,1... | collective-permute-start | bytes 835592 | tf_op jit(solution)/shard_map/ppermute | solution.py:622
  8.5 13.0 %copy-start = (f32[32,2,64,512]{3,2,1,0:T(8,128)S(1)}, f32[32,2,64,512]{3,2,1,0:T(8,128)}, u32[]{:S(2)}) copy-start(f32[32,2,64,512]{3,2,1,0:T(8,128)} %param.8) | copy-start | bytes 25165828
  8.5 13.0 %copy-start.4 = (s32[8,512]{1,0:T(8,128)S(1)}, s32[8,512]{1,0:T(8,128)}, u32[]{:S(2)}) copy-start(s32[8,512]{1,0:T(8,128)} %cells.1) | copy-start | bytes 49156
  8.5 13.0 %copy-start.5 = (s32[8]{0:T(128)S(1)}, s32[8]{0:T(128)}, u32[]{:S(2)}) copy-start(s32[8]{0:T(128)} %owner.3) | copy-start | bytes 100
  8.5 13.0 %copy-start.6 = (s32[8]{0:T(128)S(1)}, s32[8]{0:T(128)}, u32[]{:S(2)}) copy-start(s32[8]{0:T(128)} %order.3) | copy-start | bytes 100
  21.5 6.4 %copy-start.7 = (f32[8,512]{1,0:T(8,128)S(1)}, f32[8,512]{1,0:T(8,128)}, u32[]{:S(2)}) copy-start(f32[8,512]{1,0:T(8,128)} %param.15) | copy-start | bytes 49156
  21.5 7.9 %copy-start.3 = (f32[8,64,512]{2,1,0:T(8,128)S(1)}, f32[8,64,512]{2,1,0:T(8,128)}, u32[]{:S(2)}) copy-start(f32[8,64,512]{2,1,0:T(8,128)} %observed.1) | copy-start | bytes 3145732
  27.8 1.6 %collective-permute-start.2 = (f32[4,4,32,128]{3,2,1,0:T(8,128)S(1)}, f32[4,4,32,128]{3,2,1,0:T(8,128)S(1)}, u32[]{:S(2)}, u32[]{:S(2)}) collective-permute-start(f32[4,4,32,128]{3,2,1,0:T(8,128)S(1)} %get-tuple-element.65), channel_id=1, source_target_pairs={{0,16},{16,0},{1,17},{17,1},{2,18},{18,2},{3,19},{19,3},{4,20},{20... | collective-permute-start | bytes 786440 | tf_op jit(solution)/shard_map/ppermute | solution.py:627
  30.2 5.6 %collective-permute-start.3 = (f32[2,64,128]{2,1,0:T(8,128)S(1)}, f32[2,64,128]{2,1,0:T(8,128)S(1)}, u32[]{:S(2)}, u32[]{:S(2)}) collective-permute-start(f32[2,64,128]{2,1,0:T(8,128)S(1)} %get-tuple-element.70), channel_id=1, source_target_pairs={{0,1},{1,0},{2,3},{3,2},{4,5},{5,4},{6,7},{7,6},{8,9},{9,8},{10,11... | collective-permute-start | bytes 196616 | tf_op jit(solution)/shard_map/ppermute | solution.py:639
  30.3 12.1 %collective-permute-start.5 = (f32[2,64,128]{2,1,0:T(8,128)S(1)}, f32[2,64,128]{2,1,0:T(8,128)S(1)}, u32[]{:S(2)}, u32[]{:S(2)}) collective-permute-start(f32[2,64,128]{2,1,0:T(8,128)S(1)} %get-tuple-element.83), channel_id=1, source_target_pairs={{0,1},{1,0},{2,3},{3,2},{4,5},{5,4},{6,7},{7,6},{8,9},{9,8},{10,11... | collective-permute-start | bytes 196616 | tf_op jit(solution)/shard_map/ppermute | solution.py:641
  35.9 6.5 %collective-permute-start.4 = (f32[2,64,128]{2,1,0:T(8,128)S(1)}, f32[2,64,128]{2,1,0:T(8,128)S(1)}, u32[]{:S(2)}, u32[]{:S(2)}) collective-permute-start(f32[2,64,128]{2,1,0:T(8,128)S(1)} %add.24), channel_id=1, source_target_pairs={{0,2},{1,3},{2,0},{3,1},{4,6},{5,7},{6,4},{7,5},{8,10},{9,11},{10,... | collective-permute-start | bytes 196616 | tf_op jit(solution)/shard_map/ppermute | solution.py:639
  42.4 7.5 %collective-permute-start.7 = (f32[2,64,128]{2,1,0:T(8,128)S(1)}, f32[2,64,128]{2,1,0:T(8,128)S(1)}, u32[]{:S(2)}, u32[]{:S(2)}) collective-permute-start(f32[2,64,128]{2,1,0:T(8,128)S(1)} %add.26), channel_id=1, source_target_pairs={{0,2},{1,3},{2,0},{3,1},{4,6},{5,7},{6,4},{7,5},{8,10},{9,11},{10,... | collective-permute-start | bytes 196616 | tf_op jit(solution)/shard_map/ppermute | solution.py:641
  43.1 6.9 %collective-permute-start.6 = (f32[2,64,128]{2,1,0:T(8,128)S(1)}, f32[2,64,128]{2,1,0:T(8,128)S(1)}, u32[]{:S(2)}, u32[]{:S(2)}) collective-permute-start(f32[2,64,128]{2,1,0:T(8,128)S(1)} %add.25), channel_id=1, source_target_pairs={{0,4},{1,5},{2,6},{3,7},{4,0},{5,1},{6,2},{7,3},{8,12},{9,13},{10,... | collective-permute-start | bytes 196616 | tf_op jit(solution)/shard_map/ppermute | solution.py:639
  50.0 7.3 %collective-permute-start.9 = (f32[2,64,128]{2,1,0:T(8,128)S(1)}, f32[2,64,128]{2,1,0:T(8,128)S(1)}, u32[]{:S(2)}, u32[]{:S(2)}) collective-permute-start(f32[2,64,128]{2,1,0:T(8,128)S(1)} %add.28), channel_id=1, source_target_pairs={{0,4},{1,5},{2,6},{3,7},{4,0},{5,1},{6,2},{7,3},{8,12},{9,13},{10,... | collective-permute-start | bytes 196616 | tf_op jit(solution)/shard_map/ppermute | solution.py:641
  50.6 6.6 %collective-permute-start.8 = (f32[2,64,128]{2,1,0:T(8,128)S(1)}, f32[2,64,128]{2,1,0:T(8,128)S(1)}, u32[]{:S(2)}, u32[]{:S(2)}) collective-permute-start(f32[2,64,128]{2,1,0:T(8,128)S(1)} %add.27), channel_id=1, source_target_pairs={{0,8},{1,9},{2,10},{3,11},{4,12},{5,13},{6,14},{7,15},{8,0},{9,1},... | collective-permute-start | bytes 196616 | tf_op jit(solution)/shard_map/ppermute | solution.py:639
  57.3 5.9 %collective-permute-start.11 = (f32[2,64,128]{2,1,0:T(8,128)S(1)}, f32[2,64,128]{2,1,0:T(8,128)S(1)}, u32[]{:S(2)}, u32[]{:S(2)}) collective-permute-start(f32[2,64,128]{2,1,0:T(8,128)S(1)} %add.30), channel_id=1, source_target_pairs={{0,8},{1,9},{2,10},{3,11},{4,12},{5,13},{6,14},{7,15},{8,0},{9,1},... | collective-permute-start | bytes 196616 | tf_op jit(solution)/shard_map/ppermute | solution.py:653
  59.0 4.2 %collective-permute-start.10 = (f32[2,64,128]{2,1,0:T(8,128)S(1)}, f32[2,64,128]{2,1,0:T(8,128)S(1)}, u32[]{:S(2)}, u32[]{:S(2)}) collective-permute-start(f32[2,64,128]{2,1,0:T(8,128)S(1)} %add.29.mine), channel_id=1, source_target_pairs={{0,16},{16,0},{1,17},{17,1},{2,18},{18,2},{3,19},{19,3},{4,20},{20... | collective-permute-start | bytes 196616 | tf_op jit(solution)/shard_map/ppermute | solution.py:652
  63.3 20.2 %collective-permute-start.13 = (f32[64,2,32,128]{3,2,1,0:T(8,128)S(1)}, f32[64,2,32,128]{3,2,1,0:T(8,128)S(1)}, u32[]{:S(2)}, u32[]{:S(2)}) collective-permute-start(f32[64,2,32,128]{3,2,1,0:T(8,128)S(1)} %get-tuple-element.112), channel_id=1, source_target_pairs={{0,16},{16,0},{1,17},{17,1},{2,18},{18,2},{3,19},{19,3},{4,20},{20... | collective-permute-start | bytes 6291464 | tf_op jit(solution)/shard_map/ppermute | solution.py:657
  63.3 20.1 %collective-permute-start.14 = (f32[64,2,32,128]{3,2,1,0:T(8,128)S(1)}, f32[64,2,32,128]{3,2,1,0:T(8,128)S(1)}, u32[]{:S(2)}, u32[]{:S(2)}) collective-permute-start(f32[64,2,32,128]{3,2,1,0:T(8,128)S(1)} %get-tuple-element.114), channel_id=1, source_target_pairs={{0,16},{16,0},{1,17},{17,1},{2,18},{18,2},{3,19},{19,3},{4,20},{20... | collective-permute-start | bytes 6291464 | tf_op jit(solution)/shard_map/ppermute | solution.py:658
  63.8 9.7 %collective-permute-start.12 = (f32[2,64,128]{2,1,0:T(8,128)S(1)}, f32[2,64,128]{2,1,0:T(8,128)S(1)}, u32[]{:S(2)}, u32[]{:S(2)}) collective-permute-start(f32[2,64,128]{2,1,0:T(8,128)S(1)} %add.31.mine), channel_id=1, source_target_pairs={{0,16},{16,0},{1,17},{17,1},{2,18},{18,2},{3,19},{19,3},{4,20},{20... | collective-permute-start | bytes 196616 | tf_op jit(solution)/shard_map/ppermute | solution.py:655

commit v6 on v5

--- a/solution.py
+++ b/solution.py
@@ -98,6 +98,9 @@
     )(state6, flow5, nu5)
 
 
+PAD = SUB
+
+
 def stencil_coefs(flow_x, flow_y, nu, col, width):
     east = nu - jnp.minimum(flow_x, 0.0)
     west = nu + jnp.maximum(flow_x, 0.0)
@@ -109,122 +112,104 @@
     return centre, west, east, south, north
 
 
-def stencil_row(src, row, dst, coef, members):
-    nct = src.shape[1]
+def fill_coefs(coef, field, member, flow, nu, blocks, before=None, after=None):
+    _, r8, nct = flow.shape[:3]
+    width = nct * LANES
+    for ct in range(nct):
+        at = lax.rem(ct + member * (nct // 2), nct)
+        for first, count in blocks:
+            shape = (count * SUB, LANES)
+            col = lax.broadcasted_iota(jnp.int32, shape, 1) + at * LANES
+            part = pl.ds(first, count)
+            numbers = (flow[0, part, at], flow[1, part, at], nu[field, part, at])
+            numbers = [x.reshape(shape) for x in numbers]
+            for k, value in enumerate(stencil_coefs(*numbers, col, width)):
+                coef[k, ct, pl.ds(PAD + first * SUB, count * SUB), :] = value
+        for msg, row in ((before, PAD - 1), (after, PAD + r8 * SUB)):
+            if msg is not None:
+                col = lax.broadcasted_iota(jnp.int32, (1, LANES), 1) + at * LANES
+                base = msg.shape[1] - PACK
+                numbers = [msg[at, pl.ds(base + k, 1), :] for k in (0, 1, 2 + field)]
+                for k, value in enumerate(stencil_coefs(*numbers, col, width)):
+                    coef[k, ct, pl.ds(row, 1), :] = value
+
+
+def stencil(mid, west, east, weights):
+    nct = len(mid)
     lane = lax.broadcasted_iota(jnp.int32, (SUB, LANES), 1)
-    first, last = lane == 0, lane == LANES - 1
-    weights = [
-        [coef(k, ct, row) for k in range(5)] for ct in range(nct)
-    ]
-    for group in range(members // SUB):
-        rows = pl.ds(group * SUB, SUB)
-        mid = [src[row + 1, ct, rows, :] for ct in range(nct)]
-        right = [pltpu.roll(x, 1, 1) for x in mid]
-        left = [pltpu.roll(x, LANES - 1, 1) for x in mid]
-        for ct in range(nct):
-            south = jnp.where(first, right[(ct - 1) % nct], right[ct])
-            north = jnp.where(last, left[(ct + 1) % nct], left[ct])
-            centre, west, east, w_s, w_n = weights[ct]
-            value = (
-                centre * mid[ct]
-                + west * src[row, ct, rows, :]
-                + east * src[row + 2, ct, rows, :]
-                + (w_s * south + w_n * north)
-            )
-            dst(ct, rows, value)
-
-
-def forecast_rows(
-    lo, hi, field, member, state, flow, nu, before, after, q0, q1, coef, put, wait=None
-):
-    members, fields, r8, nct = state.shape[:4]
-    rows = r8 * SUB
-    half = nct // 2
-    width = nct * LANES
-    flat = state.reshape(members * fields * r8 * nct * SUB, LANES)
-    stride = fields * r8 * nct * SUB
-    offset = min(field, fields - 1) * r8 * nct * SUB
-    room = coef.shape[2]
-    coef_flat = coef.reshape(5 * nct * room, LANES)
-
-    def weight(k, ct, at):
-        return coef_flat[pl.ds((k * nct + ct) * room + at, SUB, stride=0), :]
-
-    def phys(ct):
-        return lax.rem(ct + member * half, nct)
-
-    first = max(lo - 1, 0) // SUB
-    count = min(hi, rows - 1) // SUB + 1 - first
-    base = first * SUB - SUB
+    right = [pltpu.roll(x, 1, 1) for x in mid]
+    left = [pltpu.roll(x, LANES - 1, 1) for x in mid]
+    out = []
     for ct in range(nct):
-        at = phys(ct)
-        col = lax.broadcasted_iota(jnp.int32, (count * SUB, LANES), 1) + at * LANES
-        block = pl.ds(first, count)
-        flow_x = flow[0, block, at, :, :].reshape(count * SUB, LANES)
-        flow_y = flow[1, block, at, :, :].reshape(count * SUB, LANES)
-        diffuse = nu[field, block, at, :, :].reshape(count * SUB, LANES)
-        for k, value in enumerate(stencil_coefs(flow_x, flow_y, diffuse, col, width)):
-            coef[k, ct, pl.ds(SUB, count * SUB), :] = value
-        for msg, row, needed in ((before, -1, lo == 0), (after, rows, hi == rows)):
-            if needed:
-                edge = [msg[at, pl.ds(4 * members + k, 1), :] for k in (0, 1, 2 + field)]
-                for k, value in enumerate(stencil_coefs(*edge, col[0:1], width)):
-                    coef[k, ct, pl.ds(row - base, 1), :] = value
-        if lo == 0:
-            for k in range(2):
-                q0[k, ct] = before[at, pl.ds((2 * field + k) * members, members), :]
-        if hi == rows:
-            for k in range(2):
-                q0[rows - lo + 2 + k, ct] = after[at, pl.ds((2 * field + k) * members, members), :]
-
-    start = max(lo - 2, 0)
-    stop = min(hi + 2, rows)
-
-    def load(i):
-        r = start + i
-        for ct in range(nct):
-            at = (lax.div(r, SUB) * nct + phys(ct)) * SUB + lax.rem(r, SUB) + offset
-            q0[r - lo + 2, ct] = flat[pl.ds(at, members, stride=stride), :]
-
-    if wait is None:
-        rows_loop(stop - start, 8, load)
-    else:
-        for block in range(r8):
-            wait(block)
-            for r in range(max(start, block * SUB), min(stop, block * SUB + SUB)):
-                load(r - start)
-
-    def first_step(i):
-        def keep(ct, at, value):
-            q1[i, ct, at, :] = value
-
-        stencil_row(
-            q0, i, keep, lambda k, ct, r: weight(k, ct, r + (lo - 1 - base)), members
+        south = jnp.where(lane == 0, right[(ct - 1) % nct], right[ct])
+        north = jnp.where(lane == LANES - 1, left[(ct + 1) % nct], left[ct])
+        centre, w_w, w_e, w_s, w_n = weights[ct]
+        out.append(
+            (centre * mid[ct] + w_w * west[ct]) + (w_e * east[ct] + (w_s * south + w_n * north))
         )
-
-    rows_loop(hi - lo + 2, 6, first_step)
-
-    def second_step(i):
-        def keep(ct, at, value):
-            put(lo + i, ct, at, value)
-
-        stencil_row(
-            q1, i, keep, lambda k, ct, r: weight(k, ct, r + (lo - base)), members
-        )
-
-    rows_loop(hi - lo, 4, second_step)
-
-
-def row_scratch(count, nct, members):
-    return [
-        pltpu.VMEM((count + 4, nct, members, LANES), F32),
-        pltpu.VMEM((count + 2, nct, members, LANES), F32),
-        pltpu.VMEM((5, nct, -(-count // SUB) * SUB + 4 * SUB, LANES), F32),
-    ]
-
-
-def cost(count, nct, members):
-    cells = count * nct * members * LANES
+    return out
+
+
+class Rows:
+    def __init__(self, held, coef):
+        self.nct, _, blocks = held.shape[-5:-2]
+        self.room = blocks * SUB
+        self.flat = held.reshape(held.size // LANES, LANES)
+        self.coef = coef.reshape(coef.size // LANES, LANES)
+
+    def at(self, group, ct, row):
+        start = (group * self.nct + ct) * SUB * self.room + PAD + row
+        return pl.ds(start, SUB, stride=self.room)
+
+    def load(self, group, row):
+        return [self.flat[self.at(group, ct, row), :] for ct in range(self.nct)]
+
+    def weights(self, row):
+        return [
+            [
+                self.coef[pl.ds((k * self.nct + ct) * self.room + PAD + row, SUB, stride=0), :]
+                for k in range(5)
+            ]
+            for ct in range(self.nct)
+        ]
+
+
+def group_steps(group, held, between, coef, put, edges):
+    groups, nct, _, blocks = held.shape[:4]
+    room = blocks * SUB
+    source = held.reshape(groups, nct, SUB, room, LANES)
+    middle = between.reshape(nct, SUB, room, LANES)
+
+    def block_step(block, load, store):
+        at = PAD + block * SUB
+        weights = [[coef[k, ct, pl.ds(at, SUB), :] for k in range(5)] for ct in range(nct)]
+        for m in range(SUB):
+            mid, west, east = [
+                [load(ct, m, pl.ds(at + off, SUB)) for ct in range(nct)] for off in (0, -1, 1)
+            ]
+            for ct, value in enumerate(stencil(mid, west, east, weights)):
+                store(block, ct, m, value)
+
+    def keep(block, ct, m, value):
+        middle[ct, m, pl.ds(PAD + block * SUB, SUB), :] = value
+
+    for block in range(blocks - 2):
+        block_step(block, lambda ct, m, rows: source[group, ct, m, rows, :], keep)
+    if edges:
+        field, inner = Rows(held, coef), Rows(between, coef)
+        for row in (-1, (blocks - 2) * SUB):
+            around = [field.load(group, row + off) for off in (0, -1, 1)]
+            for ct, value in enumerate(stencil(*around, field.weights(row))):
+                inner.flat[inner.at(0, ct, row), :] = value
+    for block in range(blocks - 2):
+        block_step(block, lambda ct, m, rows: middle[ct, m, rows, :], put)
+
+
+def held_shape(members, nct, r8):
+    return (members // SUB, nct, SUB, r8 + 2, SUB, LANES)
+
+
+def cost(cells):
     return pl.CostEstimate(flops=40 * cells, bytes_accessed=8 * cells, transcendentals=0)
 
 
@@ -232,65 +217,104 @@
 VMEM = pl.BlockSpec(memory_space=pltpu.VMEM)
 
 
-def inner_kernel(lo, hi, ids, state, flow, nu, full, send, held, sems, *scratch):
-    half = full.shape[1] // 2
-    copies = [
-        pltpu.make_async_copy(state.at[:, 0, block], held.at[:, 0, block], sems.at[block])
-        for block in range(state.shape[2])
-    ]
+def inner_kernel(ids, state, flow, nu, full, held0, held1, between, coef, sems):
+    groups, nct, _, blocks = held0.shape[:4]
+    members = groups * SUB
+    r8 = blocks - 2
+    half = nct // 2
+    member = ids[1]
+    copies = []
+    for field, held in ((0, held0), (1, held1)):
+        for group in range(groups):
+            for ct in range(nct):
+                at = lax.rem(ct + member * half, nct)
+                copies.append(
+                    pltpu.make_async_copy(
+                        state.at[pl.ds(group * SUB, SUB), field, :, at],
+                        held.at[group, ct, :, pl.ds(1, r8)],
+                        sems.at[len(copies)],
+                    )
+                )
     for one in copies:
         one.start()
-
-    def put(r, ct, at, value):
-        full[r, ct, at, :] = value
-        if ct >= half:
-            send[r, ct - half, at, :] = value
-
-    forecast_rows(
-        lo, hi, 0, ids[1], held, flow, nu, None, None, *scratch, put,
-        wait=lambda block: copies[block].wait(),
-    )
+    fill_coefs(coef, 0, member, flow, nu, [(0, r8)])
+    flat = full.reshape(full.size // LANES, LANES)
+
+    for group in range(groups):
+        for one in copies[group * nct : (group + 1) * nct]:
+            one.wait()
+
+    def run(group, carry):
+        def put(block, ct, m, value):
+            start = ((ct // half) * r8 * SUB + block * SUB) * half + ct % half
+            flat[pl.ds(start * members + group * SUB + m, SUB, stride=half * members), :] = value
+
+        group_steps(group, held0, between, coef, put, False)
+        return carry
+
+    lax.fori_loop(0, groups, run, 0)
+    for one in copies[groups * nct :]:
+        one.wait()
 
 
 def forecast_inner(ids, state6, flow5, nu5):
     members, _, r8, nct = state6.shape[:4]
-    rows = r8 * SUB
+    held = held_shape(members, nct, r8)
     return pl.pallas_call(
-        functools.partial(inner_kernel, 2, rows - 2),
+        inner_kernel,
         out_shape=[
-            jax.ShapeDtypeStruct((rows, nct, members, LANES), F32),
-            jax.ShapeDtypeStruct((rows, nct // 2, members, LANES), F32),
+            jax.ShapeDtypeStruct((2, r8 * SUB, nct // 2, members, LANES), F32),
+            jax.ShapeDtypeStruct(held, F32),
+            jax.ShapeDtypeStruct(held, F32),
         ],
         in_specs=[SMEM, pl.BlockSpec(memory_space=pl.ANY)] + [VMEM] * 2,
-        out_specs=[VMEM] * 2,
+        out_specs=[VMEM] * 3,
         scratch_shapes=[
-            pltpu.VMEM((members, 1, r8, nct, SUB, LANES), F32),
-            pltpu.SemaphoreType.DMA((r8,)),
-            *row_scratch(rows - 4, nct, members),
+            pltpu.VMEM(held[1:], F32),
+            pltpu.VMEM((5, nct, (r8 + 2) * SUB, LANES), F32),
+            pltpu.SemaphoreType.DMA((2 * held[0] * nct,)),
         ],
-        compiler_params=params(44),
-        cost_estimate=cost(rows, nct, members),
+        compiler_params=params(34),
+        cost_estimate=cost(members * r8 * SUB * nct * LANES),
         name="forecast_inner",
     )(ids, state6, flow5, nu5)
 
 
 def edge_kernel(
-    ids, cells, owner, order, state, flow, nu, before, after, full_in, send_in,
-    full, send, keep, away, *scratch
+    ids, cells, owner, order, flow, nu, before, after, full_in, held0_in, held1_in,
+    full, held0, held1, keep, away, coef
 ):
-    members, _, r8, nct = state.shape[:4]
+    groups, nct, _, blocks = held0.shape[:4]
+    members = groups * SUB
+    r8 = blocks - 2
     rows = r8 * SUB
     half = nct // 2
     width = nct * LANES
     slab, member = ids[0], ids[1]
 
-    def put(r, ct, at, value):
-        full[r, ct, at, :] = value
-        if ct >= half:
-            send[r, ct - half, at, :] = value
-
-    for lo, hi in ((0, 2), (rows - 2, rows)):
-        forecast_rows(lo, hi, 0, member, state, flow, nu, before, after, *scratch, put)
+    for field, held in ((0, held0), (1, held1)):
+        view = Rows(held, coef)
+        for ct in range(nct):
+            at = lax.rem(ct + member * half, nct)
+            for group in range(groups):
+                for k in range(2):
+                    part = pl.ds((2 * field + k) * members + group * SUB, SUB)
+                    view.flat[view.at(group, ct, k - 2), :] = before[at, part, :]
+                    view.flat[view.at(group, ct, rows + k), :] = after[at, part, :]
+
+    fill_coefs(coef, 0, member, flow, nu, [(0, 1), (r8 - 1, 1)], before, after)
+    view = Rows(held0, coef)
+    for first in (0, rows - 2):
+        for group in range(groups):
+            old = {r: view.load(group, r) for r in range(first - 2, first + 4)}
+            one = {
+                r: stencil(old[r], old[r - 1], old[r + 1], view.weights(r))
+                for r in range(first - 1, first + 3)
+            }
+            for r in range(first, first + 2):
+                new = stencil(one[r], one[r - 1], one[r + 1], view.weights(r))
+                for ct, value in enumerate(new):
+                    full[ct // half, r, ct % half, pl.ds(group * SUB, SUB), :] = value
 
     nobs = cells.shape[1]
     bits = width.bit_length() - 1
@@ -309,7 +333,7 @@
                     r = lax.shift_right_logical(cell, bits)
                     c = cell & (width - 1)
                     at = (lax.shift_right_logical(c, 7) + member * half) & (nct - 1)
-                    moved = pltpu.roll(full[r, at], (o - c) & (LANES - 1), 1)
+                    moved = pltpu.roll(full[at // half, r, at % half], (o - c) & (LANES - 1), 1)
                     acc = jnp.where(lane == o, moved, acc)
                 return acc
 
@@ -330,63 +354,67 @@
         lax.fori_loop(0, nobs // LANES, pick, 0)
 
 
-def forecast_edges(ids, cells, owner, order, state6, flow5, nu5, before, after, full, send):
-    members, _, r8, nct = state6.shape[:4]
+def forecast_edges(ids, cells, owner, order, flow5, nu5, before, after, full, held0, held1):
+    members = full.shape[3]
+    nct, _, blocks = held0.shape[1:4]
     nb, nobs = cells.shape
     picks = jax.ShapeDtypeStruct((nb // 2, nobs // LANES, members, LANES), F32)
+    same = [jax.ShapeDtypeStruct(x.shape, F32) for x in (full, held0, held1)]
     return pl.pallas_call(
         edge_kernel,
-        out_shape=[
-            jax.ShapeDtypeStruct(full.shape, F32), jax.ShapeDtypeStruct(send.shape, F32), picks, picks,
-        ],
+        out_shape=[*same, picks, picks],
         in_specs=[SMEM] * 4 + [VMEM] * 7,
-        out_specs=[VMEM] * 4,
-        input_output_aliases={9: 0, 10: 1},
-        scratch_shapes=row_scratch(2, nct, members),
-        compiler_params=params(8),
-        cost_estimate=cost(SUB, nct, members),
+        out_specs=[VMEM] * 5,
+        input_output_aliases={8: 0, 9: 1, 10: 2},
+        scratch_shapes=[pltpu.VMEM((5, nct, blocks * SUB, LANES), F32)],
+        compiler_params=params(6),
+        cost_estimate=cost(members * SUB * nct * LANES),
         name="forecast_edges",
-    )(ids, cells, owner, order, state6, flow5, nu5, before, after, full, send)
-
-
-def piece_kernel(lo, hi, ids, state, flow, nu, before, after, *rest):
-    own, send, *scratch = rest[-5:]
-    half = own.shape[1]
-
-    def put(r, ct, at, value):
-        if ct < half:
-            own[r, ct, at, :] = value
-        else:
-            send[r, ct - half, at, :] = value
-
-    forecast_rows(lo, hi, 1, ids[1], state, flow, nu, before, after, *scratch, put)
-
-
-def forecast_piece(lo, hi, ids, state6, flow5, nu5, before, after, done):
-    members, _, r8, nct = state6.shape[:4]
-    rows = r8 * SUB
-    part = jax.ShapeDtypeStruct((rows, nct // 2, members, LANES), F32)
+    )(ids, cells, owner, order, flow5, nu5, before, after, full, held0, held1)
+
+
+def piece_kernel(group, ids, flow, nu, before, after, held, *rest):
+    own, send, between, coef = rest[-4:]
+    rows, half, members = own.shape[:3]
+    flats = [x.reshape(x.size // LANES, LANES) for x in (own, send)]
+    fill_coefs(coef, 1, ids[1], flow, nu, [(0, rows // SUB)], before, after)
+
+    def put(block, ct, m, value):
+        start = block * SUB * half + ct % half
+        flats[ct // half][
+            pl.ds(start * members + group * SUB + m, SUB, stride=half * members), :
+        ] = value
+
+    group_steps(group, held, between, coef, put, True)
+
+
+def forecast_piece(group, ids, flow5, nu5, before, after, held, done):
+    groups, nct, _, blocks = held.shape[:4]
+    rows = (blocks - 2) * SUB
+    part = jax.ShapeDtypeStruct((rows, nct // 2, groups * SUB, LANES), F32)
     return pl.pallas_call(
-        functools.partial(piece_kernel, lo, hi),
+        functools.partial(piece_kernel, group),
         out_shape=[part, part],
         in_specs=[SMEM] + [VMEM] * (5 + len(done)),
         out_specs=[VMEM] * 2,
         input_output_aliases={6: 0, 7: 1} if done else {},
-        scratch_shapes=row_scratch(hi - lo, nct, members),
-        compiler_params=params(10),
-        cost_estimate=cost(hi - lo, nct, members),
-        name=f"forecast_rows_{lo}",
-    )(ids, state6, flow5, nu5, before, after, *done)
-
-
-def gram_kernel(ids, owner, order, keep, other, observed, variance, *outs):
+        scratch_shapes=[
+            pltpu.VMEM(held.shape[1:], F32),
+            pltpu.VMEM((5, nct, blocks * SUB, LANES), F32),
+        ],
+        compiler_params=params(6),
+        cost_estimate=cost(SUB * rows * nct * LANES),
+        name=f"forecast_members_{group}",
+    )(ids, flow5, nu5, before, after, held, *done)
+
+
+def gram_kernel(ids, owner, order, keep, other, observed, variance, gh):
     slab, member = ids[0], ids[1]
     count, tiles, members = keep.shape[:3]
     for k in range(count):
         batch = order[2 * k + member]
         mine = owner[batch] == slab
-        part = count // len(outs)
-        out = outs[k // part].at[k % part]
+        out = gh.at[k]
 
         @pl.when(jnp.logical_not(mine))
         def _():
@@ -421,9 +449,9 @@
     vmem = pl.BlockSpec(memory_space=pltpu.VMEM)
     return pl.pallas_call(
         gram_kernel,
-        out_shape=[jax.ShapeDtypeStruct((count // 2, total, 2 * total), F32)] * 2,
+        out_shape=jax.ShapeDtypeStruct((count, total, 2 * total), F32),
         in_specs=[smem] * 3 + [vmem] * 4,
-        out_specs=[vmem] * 2,
+        out_specs=vmem,
         compiler_params=params(12),
         name="gram",
     )(ids, owner, order, keep, other, observed, variance[:, None, :])
@@ -559,7 +587,7 @@
 def apply_kernel(w_ref, own0, other0, own1, other1, out):
     field = pl.program_id(0)
     size = w_ref.shape[0] // 2
-    rows, half = own0.shape[:2]
+    rows, half = own1.shape[:2]
     weights = w_ref[...].astype(BF16)
     flat = out.reshape(size * half * rows, LANES)
 
@@ -588,18 +616,23 @@
 
 
 def apply(weights, own0, other0, own1, other1):
-    rows, half, members, _ = other0.shape
+    rows, half, members, _ = other1.shape
     size = 2 * members
     r8 = rows // SUB
     block = (SUB, half, members, LANES)
-    zero = pl.BlockSpec(block, lambda f, r: (jnp.where(f == 0, r, r8 - 1), 0, 0, 0))
+
+    def zero(part):
+        return pl.BlockSpec(
+            (None, *block), lambda f, r: (part, jnp.where(f == 0, r, r8 - 1), 0, 0, 0)
+        )
+
     one = pl.BlockSpec(block, lambda f, r: (jnp.where(f == 1, r, 0), 0, 0, 0))
     return pl.pallas_call(
         apply_kernel,
         grid=(2, r8),
         out_shape=jax.ShapeDtypeStruct((size, 2, r8, half, SUB, LANES), F32),
         in_specs=[
-            pl.BlockSpec(weights.shape, lambda f, r: (0, 0)), zero, zero, one, one,
+            pl.BlockSpec(weights.shape, lambda f, r: (0, 0)), zero(0), zero(1), one, one,
         ],
         out_specs=pl.BlockSpec((size, 1, 1, half, SUB, LANES), lambda f, r: (0, f, r, 0, 0, 0)),
         compiler_params=params(12),
@@ -620,44 +653,32 @@
     up_edge, down_edge = pack_edges(state6, flow5, nu5)
     before = lax.ppermute(up_edge, "space", up)
     after = lax.ppermute(down_edge, "space", down)
-    full0, send0 = forecast_inner(ids, state6, flow5, nu5)
-    full0, send0, keep, away = forecast_edges(
-        ids, obs_cells, obs_owner, batch_order, state6, flow5, nu5, before, after, full0, send0
+    full0, held0, held1 = forecast_inner(ids, state6, flow5, nu5)
+    full0, _, held1, keep, away = forecast_edges(
+        ids, obs_cells, obs_owner, batch_order, flow5, nu5, before, after, full0, held0, held1
     )
     other = lax.ppermute(away, "member", swap)
-    early, late = gram(ids, obs_owner, batch_order, keep, other, obs_values, obs_error)
-
-    rows = state.shape[2]
-    pieces = [(r, r + rows // 4) for r in range(0, rows, rows // 4)]
+    gh = gram(ids, obs_owner, batch_order, keep, other, obs_values, obs_error)
+
+    groups = list(range(held1.shape[0]))
     field1 = ()
-    bits = [1 << i for i in range(space.bit_length() - 1)]
-
-    def partner(bit):
-        return [(i, i ^ bit) for i in range(space)]
-
-    for turn, bit in enumerate(bits):
-        received = [lax.ppermute(early, "space", partner(bit))]
-        if turn > 0:
-            received.append(lax.ppermute(late, "space", partner(bits[turn - 1])))
-        if pieces:
-            before, after, early, late = lax.optimization_barrier((before, after, early, late))
-            field1 = forecast_piece(*pieces.pop(0), ids, state6, flow5, nu5, before, after, field1)
+    bit = 1
+    while bit < space:
+        received = lax.ppermute(gh, "space", [(i, i ^ bit) for i in range(space)])
+        if groups:
+            held1, gh = lax.optimization_barrier((held1, gh))
+            field1 = forecast_piece(groups.pop(0), ids, flow5, nu5, before, after, held1, field1)
             received, field1 = lax.optimization_barrier((received, field1))
-        early = early + received[0]
-        if turn > 0:
-            late = late + received[1]
-    for piece in pieces:
-        field1 = forecast_piece(*piece, ids, state6, flow5, nu5, before, after, field1)
+        gh = gh + received
+        bit *= 2
+    for group in groups:
+        field1 = forecast_piece(group, ids, flow5, nu5, before, after, held1, field1)
     own1, send1 = field1
-    early_theirs = lax.ppermute(early, "member", swap)
-    late = late + lax.ppermute(late, "space", partner(bits[-1]))
-    early, early_theirs, late = lax.optimization_barrier((early, early_theirs, late))
-    late_theirs = lax.ppermute(late, "member", swap)
-    send0, send1, early = lax.optimization_barrier((send0, send1, early))
-    other0 = lax.ppermute(send0, "member", swap)
+    theirs = lax.ppermute(gh, "member", swap)
+    full0, send1, gh, theirs = lax.optimization_barrier((full0, send1, gh, theirs))
+    other0 = lax.ppermute(full0, "member", swap)
     other1 = lax.ppermute(send1, "member", swap)
-    v = chain(False, ids, early, early_theirs)
-    weights = chain(True, ids, late, late_theirs, v)
+    weights = chain(True, ids, gh, theirs)
     return untiled(apply(weights, full0, other0, own1, other1))
 
 

time: 94 us -> 88.4 us (0.940)
  Pallas kernels: 65.6 us -> 53.4 us
  waiting for transfers between devices: 5.67 us -> 11.6 us
    pallas_call x7, Pallas kernels: 34.3 us -> 22.7 us  [the longest x1 10.5 us: forecast_inner(): pl.pallas_call(inner_kernel, out_shape=[jax.ShapeDtypeStruct((2, r8 * SUB...]
    ppermute x11 -> x6, waiting for transfers between devices: 4.17 us -> 8.06 us  [the longest x4 6.72 us: body(): received = lax.ppermute(gh, 'space', [(i, i ^ bit) for i in range(space)])]
    ppermute x1, waiting for transfers between devices: 0.01 us -> 1.84 us  [body(): after = lax.ppermute(down_edge, 'space', down)]
    ppermute x11 -> x6, starting transfers between devices: 14.5 us -> 15.2 us  [the longest x4 15 us: body(): received = lax.ppermute(gh, 'space', [(i, i ^ bit) for i in range(space)])]
    pallas_call x2 -> x1, Pallas kernels: 19.5 us -> 18.9 us  [chain(): pl.pallas_call(functools.partial(chain_kernel, last), out_shape=jax.Shape...]
  transfers between devices with their start and end apart: 15 -> 10, of which waited for: 2 -> 8; matrix products, arithmetic and copies ran while one was open for 0% -> 0% of each run, Pallas kernels for 50% -> 44%
where the time goes in v6:
time: 88.4 us; the launch traced here: 87.2 us
  Pallas kernels  53.4 us (60%)
  starting transfers between devices  21.8 us (25%)
  waiting for transfers between devices  11.6 us (13%)
    pallas_call x1, Pallas kernels, chain(): pl.pallas_call(functools.partial(chain_kernel, last), out_shape=jax.Shape...  18.9 us
    ppermute x4, starting transfers between devices, body(): received = lax.ppermute(gh, 'space', [(i, i ^ bit) for i in range(space)])  15 us
    pallas_call x1, Pallas kernels, forecast_inner(): pl.pallas_call(inner_kernel, out_shape=[jax.ShapeDtypeStruct((2, r8 * SUB...  10.5 us
    pallas_call x1, Pallas kernels, apply(): pl.pallas_call(apply_kernel, grid=(2, r8), out_shape=jax.ShapeDtypeStruct...  9.55 us
    pallas_call x4, Pallas kernels, forecast_piece(): pl.pallas_call(functools.partial(piece_kernel, group), out_shape=[part, p...  8.85 us
    ppermute x4, waiting for transfers between devices, body(): received = lax.ppermute(gh, 'space', [(i, i ^ bit) for i in range(space)])  6.72 us
    ppermute x1, starting transfers between devices, body(): before = lax.ppermute(up_edge, 'space', up)  4.86 us
    pallas_call x1, Pallas kernels, forecast_edges(): pl.pallas_call(edge_kernel, out_shape=[*same, picks, picks], in_specs=[SM...  2.56 us
  transfers between devices with their start and end apart: 10, of which 8 were waited for; matrix products, arithmetic and copies ran while one was open for 0% of the time, Pallas kernels for 44%

profile of v6, /device:TPU:0, one launch (start us, length us, event | category | flops | bytes accessed | tf_op | source)
XLA Modules:
  0.0 87.2 jit_solution(4289664166003817988)
XLA Ops:
  0.0 2.2 %pack_edges.1 = (f32[4,136,128]{2,1,0:T(8,128)}, f32[4,136,128]{2,1,0:T(8,128)}) custom-call(f32[32,2,8,4,8,128]{5,4,3,2,1,0:T(8,128)} %bitcast.28, f32[2,8,4,8,128]{4,3,2,1,0:T(8,128)} %bitcast.14, f32[2,8,4,8,128]{4,3,2,1,0:T(8,128)} %bitcast.21), custom_call_target="tpu_custom_call" | custom-call | tf_op jit(solution)/shard_map/pack_edges/pallas_call | solution.py:90
  2.2 4.9 %collective-permute-start = (f32[4,136,128]{2,1,0:T(8,128)}, f32[4,136,128]{2,1,0:T(8,128)S(1)}, u32[]{:S(2)}, u32[]{:S(2)}) collective-permute-start(f32[4,136,128]{2,1,0:T(8,128)} %get-tuple-element.46), channel_id=1, source_target_pairs={{0,1},{1,2},{2,3},{3,4},{4,5},{5,6},{6,7},{7,8},{8,9},{9,10},{10,1... | collective-permute-start | bytes 835592 | tf_op jit(solution)/shard_map/ppermute | solution.py:654
  7.1 1.3 %collective-permute-start.1 = (f32[4,136,128]{2,1,0:T(8,128)}, f32[4,136,128]{2,1,0:T(8,128)S(1)}, u32[]{:S(2)}, u32[]{:S(2)}) collective-permute-start(f32[4,136,128]{2,1,0:T(8,128)} %get-tuple-element.47), channel_id=1, source_target_pairs={{1,0},{2,1},{3,2},{4,3},{5,4},{6,5},{7,6},{8,7},{9,8},{10,9},{11,1... | collective-permute-start | bytes 835592 | tf_op jit(solution)/shard_map/ppermute | solution.py:655
  8.5 10.5 %forecast_inner.1 = (f32[2,64,2,32,128]{4,3,2,1,0:T(8,128)S(1)}, f32[4,4,8,10,8,128]{5,4,3,2,1,0:T(8,128)S(1)}, f32[4,4,8,10,8,128]{5,4,3,2,1,0:T(8,128)S(1)}) custom-call(s32[2]{0:T(128)S(1)} %pad_add_fusion.ids, f32[32,2,8,4,8,128]{5,4,3,2,1,0:T(8,128)} %bitcast.29, f32[2,8,4,8,128]{4,3,2,1,0:T(8,128)S(1)} %bitcast.15, f32[2,8,4,8,128]{4,3,2,1,0:T(8,128)S(1)} %bitcast.22), custom_call_target="tpu_custom_call" | custom-call | flops 41943040 | bytes 8388608 | tf_op jit(solution)/shard_map/forecast_inner/pallas_call | solution.py:263
  19.3 1.8 %collective-permute-done.1.after = f32[4,136,128]{2,1,0:T(8,128)S(1)} collective-permute-done((f32[4,136,128]{2,1,0:T(8,128)}, f32[4,136,128]{2,1,0:T(8,128)S(1)}, u32[]{:S(2)}, u32[]{:S(2)}) %collective-permute-start.1) | collective-permute-done | bytes 278560 | tf_op jit(solution)/shard_map/ppermute | solution.py:655
  21.1 2.6 %forecast_edges.1 = (f32[2,64,2,32,128]{4,3,2,1,0:T(8,128)S(1)}, f32[4,4,8,10,8,128]{5,4,3,2,1,0:T(8,128)S(1)}, f32[4,4,8,10,8,128]{5,4,3,2,1,0:T(8,128)S(1)}, f...) custom-call(s32[2]{0:T(128)S(1)} %pad_add_fusion.ids, ...), custom_call_target="tpu_custom_call", output_to_operand_aliasing={{0}: (8, {}), {1}: (9, {}), {2}: (10, {})} | custom-call | flops 5242880 | bytes 1048576 | tf_op jit(solution)/shard_map/forecast_edges/pallas_call | solution.py:363
  23.8 1.5 %collective-permute-done.2.other = f32[4,4,32,128]{3,2,1,0:T(8,128)S(1)} collective-permute-done((f32[4,4,32,128]{3,2,1,0:T(8,128)S(1)}, f32[4,4,32,128]{3,2,1,0:T(8,128)S(1)}, u32[]{:S(2)}, u32[]{:S(2)}) %collective-permute-start.2) | collective-permute-done | bytes 262176 | tf_op jit(solution)/shard_map/ppermute | solution.py:660
  25.3 0.8 gram.1
  26.1 7.2 %collective-permute-start.3 = (f32[4,64,128]{2,1,0:T(8,128)S(1)}, f32[4,64,128]{2,1,0:T(8,128)S(1)}, u32[]{:S(2)}, u32[]{:S(2)}) collective-permute-start(f32[4,64,128]{2,1,0:T(8,128)S(1)} %gram.1), channel_id=1, source_target_pairs={{0,1},{1,0},{2,3},{3,2},{4,5},{5,4},{6,7},{7,6},{8,9},{9,8},{10,11... | collective-permute-start | bytes 393224 | tf_op jit(solution)/shard_map/ppermute | solution.py:667
  33.4 2.2 %forecast_members_0.1 = (f32[64,2,32,128]{3,2,1,0:T(8,128)S(1)}, f32[64,2,32,128]{3,2,1,0:T(8,128)S(1)}) custom-call(s32[2]{0:T(128)S(1)} %pad_add_fusion.ids, f32[2,8,4,8,128]{4,3,2,1,0:T(8,128)S(1)} %bitcast.17, f32[2,8,4,8,128]{4,3,2,1,0:T(8,128)S(1)} %bitcast.24, f32[4,136,128]{2,1,0:T(8,128)S(1)} %collective-permute-done.before, ...), custom_call_target="tpu_custom_call" | custom-call | flops 10485760 | bytes 2097152 | tf_op jit(solution)/shard_map/forecast_members_0/pallas_call | solution.py:395
  35.6 2.1 %collective-permute-done.3 = f32[4,64,128]{2,1,0:T(8,128)S(1)} collective-permute-done((f32[4,64,128]{2,1,0:T(8,128)S(1)}, f32[4,64,128]{2,1,0:T(8,128)S(1)}, u32[]{:S(2)}, u32[]{:S(2)}) %collective-permute-start.3) | collective-permute-done | bytes 131104 | tf_op jit(solution)/shard_map/ppermute | solution.py:667
  37.7 1.4 %collective-permute-start.4 = (f32[4,64,128]{2,1,0:T(8,128)S(1)}, f32[4,64,128]{2,1,0:T(8,128)S(1)}, u32[]{:S(2)}, u32[]{:S(2)}) collective-permute-start(f32[4,64,128]{2,1,0:T(8,128)S(1)} %add.12), channel_id=1, source_target_pairs={{0,2},{1,3},{2,0},{3,1},{4,6},{5,7},{6,4},{7,5},{8,10},{9,11},{10,... | collective-permute-start | bytes 393224 | tf_op jit(solution)/shard_map/ppermute | solution.py:667
  39.0 2.2 %forecast_members_1.1 = (f32[64,2,32,128]{3,2,1,0:T(8,128)S(1)}, f32[64,2,32,128]{3,2,1,0:T(8,128)S(1)}) custom-call(s32[2]{0:T(128)S(1)} %pad_add_fusion.ids, f32[2,8,4,8,128]{4,3,2,1,0:T(8,128)S(1)} %bitcast.18, f32[2,8,4,8,128]{4,3,2,1,0:T(8,128)S(1)} %bitcast.25, ...), custom_call_target="tpu_custom_call", output_to_operand_aliasing={{0}: (6, {}), {1}: (7, {})} | custom-call | flops 10485760 | bytes 2097152 | tf_op jit(solution)/shard_map/forecast_members_1/pallas_call | solution.py:395
  41.3 2.0 %collective-permute-done.4 = f32[4,64,128]{2,1,0:T(8,128)S(1)} collective-permute-done((f32[4,64,128]{2,1,0:T(8,128)S(1)}, f32[4,64,128]{2,1,0:T(8,128)S(1)}, u32[]{:S(2)}, u32[]{:S(2)}) %collective-permute-start.4) | collective-permute-done | bytes 131104 | tf_op jit(solution)/shard_map/ppermute | solution.py:667
  43.3 1.8 %collective-permute-start.5 = (f32[4,64,128]{2,1,0:T(8,128)S(1)}, f32[4,64,128]{2,1,0:T(8,128)S(1)}, u32[]{:S(2)}, u32[]{:S(2)}) collective-permute-start(f32[4,64,128]{2,1,0:T(8,128)S(1)} %add.13), channel_id=1, source_target_pairs={{0,4},{1,5},{2,6},{3,7},{4,0},{5,1},{6,2},{7,3},{8,12},{9,13},{10,... | collective-permute-start | bytes 393224 | tf_op jit(solution)/shard_map/ppermute | solution.py:667
  45.0 2.2 %forecast_members_2.1 = (f32[64,2,32,128]{3,2,1,0:T(8,128)S(1)}, f32[64,2,32,128]{3,2,1,0:T(8,128)S(1)}) custom-call(s32[2]{0:T(128)S(1)} %pad_add_fusion.ids, f32[2,8,4,8,128]{4,3,2,1,0:T(8,128)S(1)} %bitcast.19, f32[2,8,4,8,128]{4,3,2,1,0:T(8,128)S(1)} %bitcast.26, ...), custom_call_target="tpu_custom_call", output_to_operand_aliasing={{0}: (6, {}), {1}: (7, {})} | custom-call | flops 10485760 | bytes 2097152 | tf_op jit(solution)/shard_map/forecast_members_2/pallas_call | solution.py:395
  47.3 1.0 %collective-permute-done.5 = f32[4,64,128]{2,1,0:T(8,128)S(1)} collective-permute-done((f32[4,64,128]{2,1,0:T(8,128)S(1)}, f32[4,64,128]{2,1,0:T(8,128)S(1)}, u32[]{:S(2)}, u32[]{:S(2)}) %collective-permute-start.5) | collective-permute-done | bytes 131104 | tf_op jit(solution)/shard_map/ppermute | solution.py:667
  48.3 4.6 %collective-permute-start.6 = (f32[4,64,128]{2,1,0:T(8,128)S(1)}, f32[4,64,128]{2,1,0:T(8,128)S(1)}, u32[]{:S(2)}, u32[]{:S(2)}) collective-permute-start(f32[4,64,128]{2,1,0:T(8,128)S(1)} %add.14), channel_id=1, source_target_pairs={{0,8},{1,9},{2,10},{3,11},{4,12},{5,13},{6,14},{7,15},{8,0},{9,1},... | collective-permute-start | bytes 393224 | tf_op jit(solution)/shard_map/ppermute | solution.py:667
  53.0 2.2 %forecast_members_3.1 = (f32[64,2,32,128]{3,2,1,0:T(8,128)S(1)}, f32[64,2,32,128]{3,2,1,0:T(8,128)S(1)}) custom-call(s32[2]{0:T(128)S(1)} %pad_add_fusion.ids, f32[2,8,4,8,128]{4,3,2,1,0:T(8,128)S(1)} %bitcast.20, f32[2,8,4,8,128]{4,3,2,1,0:T(8,128)S(1)} %bitcast.27, ...), custom_call_target="tpu_custom_call", output_to_operand_aliasing={{0}: (6, {}), {1}: (7, {})} | custom-call | flops 10485760 | bytes 2097152 | tf_op jit(solution)/shard_map/forecast_members_3/pallas_call | solution.py:395
  55.2 1.6 %collective-permute-done.6 = f32[4,64,128]{2,1,0:T(8,128)S(1)} collective-permute-done((f32[4,64,128]{2,1,0:T(8,128)S(1)}, f32[4,64,128]{2,1,0:T(8,128)S(1)}, u32[]{:S(2)}, u32[]{:S(2)}) %collective-permute-start.6) | collective-permute-done | bytes 131104 | tf_op jit(solution)/shard_map/ppermute | solution.py:667
  56.9 1.3 %collective-permute-done.7.other = f32[4,64,128]{2,1,0:T(8,128)S(1)} collective-permute-done((f32[4,64,128]{2,1,0:T(8,128)S(1)}, f32[4,64,128]{2,1,0:T(8,128)S(1)}, u32[]{:S(2)}, u32[]{:S(2)}) %collective-permute-start.7) | collective-permute-done | bytes 131104 | tf_op jit(solution)/shard_map/ppermute | solution.py:677
  58.4 0.4 collective-permute-start.9
  58.7 18.9 %chain_last.1.w_ref = f32[128,128]{1,0:T(8,128)S(1)} custom-call(s32[2]{0:T(128)S(1)} %pad_add_fusion.ids, f32[4,64,128]{2,1,0:T(8,128)S(1)} %add.15.mine, f32[4,64,128]{2,1,0:T(8,128)S(1)} %collective-permute-done.7.other), custom_call_target="tpu_custom_call" | custom-call | tf_op jit(solution)/shard_map/chain_last/pallas_call | solution.py:577
  77.7 9.6 %apply.1 = f32[64,2,8,2,8,128]{5,4,3,2,1,0:T(8,128)} custom-call(f32[128,128]{1,0:T(8,128)S(1)} %chain_last.1.w_ref, f32[2,64,2,32,128]{4,3,2,1,0:T(8,128)S(1)} %get-tuple-element.84.own0, f32[2,64,2,32,128]{4,3,2,1,0:T(8,128)S(1)} %collective-permute-done.8.other0, f32[64,2,32,128]{3,2,1,0:T(8,128)S(1)} %get-tuple-element.85.own1, ...), custom_call_target="tpu_custom_call" | custom-call | tf_op jit(solution)/shard_map/apply/pallas_call | solution.py:630
  (26 shorter events, 0.7 us)
Async XLA Ops:
  0.0 8.5 %copy-start = (f32[2,64,512]{2,1,0:T(8,128)S(1)}, f32[2,64,512]{2,1,0:T(8,128)}, u32[]{:S(2)}) copy-start(f32[2,64,512]{2,1,0:T(8,128)} %param.9) | copy-start | bytes 786436
  0.0 8.5 %copy-start.1 = (f32[2,64,512]{2,1,0:T(8,128)S(1)}, f32[2,64,512]{2,1,0:T(8,128)}, u32[]{:S(2)}) copy-start(f32[2,64,512]{2,1,0:T(8,128)} %param.10) | copy-start | bytes 786436
  2.2 17.0 %collective-permute-start = (f32[4,136,128]{2,1,0:T(8,128)}, f32[4,136,128]{2,1,0:T(8,128)S(1)}, u32[]{:S(2)}, u32[]{:S(2)}) collective-permute-start(f32[4,136,128]{2,1,0:T(8,128)} %get-tuple-element.46), channel_id=1, source_target_pairs={{0,1},{1,2},{2,3},{3,4},{4,5},{5,6},{6,7},{7,8},{8,9},{9,10},{10,1... | collective-permute-start | bytes 835592 | tf_op jit(solution)/shard_map/ppermute | solution.py:654
  7.1 14.0 %collective-permute-start.1 = (f32[4,136,128]{2,1,0:T(8,128)}, f32[4,136,128]{2,1,0:T(8,128)S(1)}, u32[]{:S(2)}, u32[]{:S(2)}) collective-permute-start(f32[4,136,128]{2,1,0:T(8,128)} %get-tuple-element.47), channel_id=1, source_target_pairs={{1,0},{2,1},{3,2},{4,3},{5,4},{6,5},{7,6},{8,7},{9,8},{10,9},{11,1... | collective-permute-start | bytes 835592 | tf_op jit(solution)/shard_map/ppermute | solution.py:655
  8.5 12.6 %copy-start.3 = (s32[8,512]{1,0:T(8,128)S(1)}, s32[8,512]{1,0:T(8,128)}, u32[]{:S(2)}) copy-start(s32[8,512]{1,0:T(8,128)} %cells.1) | copy-start | bytes 49156
  8.5 12.6 %copy-start.4 = (s32[8]{0:T(128)S(1)}, s32[8]{0:T(128)}, u32[]{:S(2)}) copy-start(s32[8]{0:T(128)} %owner.3) | copy-start | bytes 100
  8.5 12.6 %copy-start.5 = (s32[8]{0:T(128)S(1)}, s32[8]{0:T(128)}, u32[]{:S(2)}) copy-start(s32[8]{0:T(128)} %order.3) | copy-start | bytes 100
  21.1 2.7 %copy-start.6 = (f32[8,512]{1,0:T(8,128)S(1)}, f32[8,512]{1,0:T(8,128)}, u32[]{:S(2)}) copy-start(f32[8,512]{1,0:T(8,128)} %param.15) | copy-start | bytes 49156
  21.1 4.2 %copy-start.2 = (f32[8,64,512]{2,1,0:T(8,128)S(1)}, f32[8,64,512]{2,1,0:T(8,128)}, u32[]{:S(2)}) copy-start(f32[8,64,512]{2,1,0:T(8,128)} %observed.1) | copy-start | bytes 3145732
  23.7 1.6 %collective-permute-start.2 = (f32[4,4,32,128]{3,2,1,0:T(8,128)S(1)}, f32[4,4,32,128]{3,2,1,0:T(8,128)S(1)}, u32[]{:S(2)}, u32[]{:S(2)}) collective-permute-start(f32[4,4,32,128]{3,2,1,0:T(8,128)S(1)} %get-tuple-element.54), channel_id=1, source_target_pairs={{0,16},{16,0},{1,17},{17,1},{2,18},{18,2},{3,19},{19,3},{4,20},{20... | collective-permute-start | bytes 786440 | tf_op jit(solution)/shard_map/ppermute | solution.py:660
  26.1 11.5 %collective-permute-start.3 = (f32[4,64,128]{2,1,0:T(8,128)S(1)}, f32[4,64,128]{2,1,0:T(8,128)S(1)}, u32[]{:S(2)}, u32[]{:S(2)}) collective-permute-start(f32[4,64,128]{2,1,0:T(8,128)S(1)} %gram.1), channel_id=1, source_target_pairs={{0,1},{1,0},{2,3},{3,2},{4,5},{5,4},{6,7},{7,6},{8,9},{9,8},{10,11... | collective-permute-start | bytes 393224 | tf_op jit(solution)/shard_map/ppermute | solution.py:667
  37.7 5.6 %collective-permute-start.4 = (f32[4,64,128]{2,1,0:T(8,128)S(1)}, f32[4,64,128]{2,1,0:T(8,128)S(1)}, u32[]{:S(2)}, u32[]{:S(2)}) collective-permute-start(f32[4,64,128]{2,1,0:T(8,128)S(1)} %add.12), channel_id=1, source_target_pairs={{0,2},{1,3},{2,0},{3,1},{4,6},{5,7},{6,4},{7,5},{8,10},{9,11},{10,... | collective-permute-start | bytes 393224 | tf_op jit(solution)/shard_map/ppermute | solution.py:667
  43.3 5.0 %collective-permute-start.5 = (f32[4,64,128]{2,1,0:T(8,128)S(1)}, f32[4,64,128]{2,1,0:T(8,128)S(1)}, u32[]{:S(2)}, u32[]{:S(2)}) collective-permute-start(f32[4,64,128]{2,1,0:T(8,128)S(1)} %add.13), channel_id=1, source_target_pairs={{0,4},{1,5},{2,6},{3,7},{4,0},{5,1},{6,2},{7,3},{8,12},{9,13},{10,... | collective-permute-start | bytes 393224 | tf_op jit(solution)/shard_map/ppermute | solution.py:667
  48.3 8.5 %collective-permute-start.6 = (f32[4,64,128]{2,1,0:T(8,128)S(1)}, f32[4,64,128]{2,1,0:T(8,128)S(1)}, u32[]{:S(2)}, u32[]{:S(2)}) collective-permute-start(f32[4,64,128]{2,1,0:T(8,128)S(1)} %add.14), channel_id=1, source_target_pairs={{0,8},{1,9},{2,10},{3,11},{4,12},{5,13},{6,14},{7,15},{8,0},{9,1},... | collective-permute-start | bytes 393224 | tf_op jit(solution)/shard_map/ppermute | solution.py:667
  56.8 1.4 %collective-permute-start.7 = (f32[4,64,128]{2,1,0:T(8,128)S(1)}, f32[4,64,128]{2,1,0:T(8,128)S(1)}, u32[]{:S(2)}, u32[]{:S(2)}) collective-permute-start(f32[4,64,128]{2,1,0:T(8,128)S(1)} %add.15.mine), channel_id=1, source_target_pairs={{0,16},{16,0},{1,17},{17,1},{2,18},{18,2},{3,19},{19,3},{4,20},{20... | collective-permute-start | bytes 393224 | tf_op jit(solution)/shard_map/ppermute | solution.py:677
  58.2 19.5 %collective-permute-start.8 = (f32[2,64,2,32,128]{4,3,2,1,0:T(8,128)S(1)}, f32[2,64,2,32,128]{4,3,2,1,0:T(8,128)S(1)}, u32[]{:S(2)}, u32[]{:S(2)}) collective-permute-start(f32[2,64,2,32,128]{4,3,2,1,0:T(8,128)S(1)} %get-tuple-element.84.own0), channel_id=1, source_target_pairs={{0,16},{16,0},{1,17},{17,1},{2,18},{18,2},{3,19},{19,3},{4,20},{20... | collective-permute-start | bytes 12582920 | tf_op jit(solution)/shard_map/ppermute | solution.py:679
  58.4 19.3 %collective-permute-start.9 = (f32[64,2,32,128]{3,2,1,0:T(8,128)S(1)}, f32[64,2,32,128]{3,2,1,0:T(8,128)S(1)}, u32[]{:S(2)}, u32[]{:S(2)}) collective-permute-start(f32[64,2,32,128]{3,2,1,0:T(8,128)S(1)} %get-tuple-element.86), channel_id=1, source_target_pairs={{0,16},{16,0},{1,17},{17,1},{2,18},{18,2},{3,19},{19,3},{4,20},{20... | collective-permute-start | bytes 6291464 | tf_op jit(solution)/shard_map/ppermute | solution.py:680
